TPU v7x, 512 devices: a whole 4x4x16 slice. The times are simulated.
512 devices in a mesh: seq: 128 (over x, z_hi, y, core), heads: 4 (over z_lo).
Axes of the slice: x: 4, y: 4, z: 16 (z_hi: 4, z_lo: 4; z = z_hi * 4 + z_lo), core: 2. Of those that a mesh axis runs over, the one named last changes fastest.
Arguments:
- x_tiles: bfloat16 [24576, 1536], P('seq'), may hold values from -6 to 6
- x_text: bfloat16 [256, 1536], P('seq'), may hold values from -6 to 6
- w_query: bfloat16 [1536, 1536], P('seq', 'heads'), may hold values from -0.15625 to 0.15625
- w_key: bfloat16 [1536, 1536], P('seq', 'heads'), may hold values from -0.15625 to 0.15625
- w_value: bfloat16 [1536, 1536], P('seq', 'heads'), may hold values from -0.15625 to 0.15625
- w_output: bfloat16 [1536, 1536], P('seq', 'heads'), may hold values from -0.15625 to 0.15625
- q_gain: float32 [1536], P('heads'), may hold values from 0.5 to 8
- k_gain: float32 [1536], P('heads'), may hold values from 0.5 to 8
- text_mask: int32 [256], replicated, may hold values 0 or 1
- windows: int32 [128, 2], replicated, may hold values from 0 to 30, as said below
- grad_out: bfloat16 [24576, 1536], P('seq'), may hold values from -6 to 6
Outputs:
- out_tiles: bfloat16 [24576, 1536], P('seq', 'heads')
- grad_tiles: bfloat16 [24576, 1536], P('seq', 'heads')
Inputs may be any that keep to these rules, and one draw needn't show every extreme that they name: windows[t, 0] is tile t's grid row or the one before, and windows[t, 1] its grid column or the one before, so that the window holds tile t and lies in the grid of 4 rows and 32 columns; windows[t, 1] is the same for all tiles of one grid column.
All inputs are finite; a program needn't handle non-finite values.
Results may differ from a plain program's by a relative error of at most 0.019.
Values may be sent and summed in bfloat16 or wider, within the bound.
No kernel may reach another device: no remote copies, remote signals or barrier semaphores. Data moves between devices by JAX's collectives and lax.ppermute only.
A program may use at most 64 MiB of HBM per device.

v0:
```python
import jax
import jax.numpy as jnp
from jax import lax
from jax.sharding import PartitionSpec as P

HD = 128


def from_behind(shard, axis, by):
    size = lax.axis_size(axis)
    pairs = [(i, i + by) for i in range(size) if 0 <= i + by < size]
    return lax.ppermute(shard, axis, pairs)


def head_norm(values, gain):
    rows = values.shape[0]
    split = values.reshape(rows, -1, HD)
    mean_sq = jnp.mean(split * split, axis=-1, keepdims=True)
    scaled = split * lax.rsqrt(mean_sq + 1e-06)
    return scaled.reshape(rows, -1) * gain[None, :]


def softmax_probs(queries, keys, bias):
    scores = jnp.einsum("qhd,khd->hqk", queries, keys, preferred_element_type=jnp.float32)
    scores = scores * HD ** (-0.5) + bias[None, None, :]
    top = jnp.max(scores, axis=-1, keepdims=True)
    expd = jnp.exp(scores - top)
    return expd / jnp.sum(expd, axis=-1, keepdims=True)


def per_device(
    x_tiles, x_text, w_query, w_key, w_value, w_output, q_gain, k_gain, text_mask, windows, grad_out
):
    rows = x_tiles.shape[0]
    feats = w_query.shape[1]
    nheads = feats // HD
    grid_cols = lax.axis_size("seq") // 4
    dims = (((1,), (1,)), ((), ()))
    full_q, full_k, full_v, full_o = (
        lax.all_gather(w_query, "seq", axis=0, tiled=True),
        lax.all_gather(w_key, "seq", axis=0, tiled=True),
        lax.all_gather(w_value, "seq", axis=0, tiled=True),
        lax.all_gather(w_output, "seq", axis=0, tiled=True),
    )
    q = jnp.dot(x_tiles, full_q, preferred_element_type=jnp.float32)
    k = jnp.dot(x_tiles, full_k, preferred_element_type=jnp.float32)
    v = jnp.dot(x_tiles, full_v, preferred_element_type=jnp.float32)
    text_k = jnp.dot(x_text, full_k, preferred_element_type=jnp.float32)
    text_v = jnp.dot(x_text, full_v, preferred_element_type=jnp.float32)
    qn = head_norm(q, q_gain).astype(jnp.bfloat16)
    kn = head_norm(k, k_gain).astype(jnp.bfloat16)
    vb = v.astype(jnp.bfloat16)
    text_kn = head_norm(text_k, k_gain).astype(jnp.bfloat16)
    text_vb = text_v.astype(jnp.bfloat16)
    all_text_k, all_text_v = (
        lax.all_gather(text_kn, "seq", axis=0, tiled=True),
        lax.all_gather(text_vb, "seq", axis=0, tiled=True),
    )
    place = lax.axis_index("seq")
    my_row = place // grid_cols
    my_col = place % grid_cols
    start = lax.dynamic_slice(windows, (place, jnp.int32(0)), (1, 2))
    first_row = start[0, 0]
    first_col = start[0, 1]
    own = jnp.stack([kn, vb])
    offsets = []
    for step_row in (0, 1):
        for step_col in (0, 1):
            offsets.append((first_row + step_row - my_row, first_col + step_col - my_col))
    table = []
    for near_row in (-1, 0, 1):
        for near_col in (-1, 0, 1):
            if near_row == 0 and near_col == 0:
                table.append(own)
            else:
                table.append(from_behind(own, "seq", -(near_row * grid_cols + near_col)))
    table = jnp.stack(table)
    picks = []
    for off_row, off_col in offsets:
        position = (off_row + 1) * 3 + off_col + 1
        picks.append(lax.dynamic_index_in_dim(table, position, 0, keepdims=False))
    window_kv = jnp.stack(picks)
    keys = jnp.concatenate([window_kv[:, 0].reshape(4 * rows, feats), all_text_k], axis=0).reshape(
        -1, nheads, HD
    )
    vals = jnp.concatenate([window_kv[:, 1].reshape(4 * rows, feats), all_text_v], axis=0).reshape(
        -1, nheads, HD
    )
    bias = jnp.concatenate(
        [
            jnp.zeros((4 * rows,), jnp.float32),
            jnp.where(text_mask == 1, 0.0, -1e30).astype(jnp.float32),
        ]
    )
    queries = qn.reshape(rows, nheads, HD)
    probs = softmax_probs(queries, keys, bias)
    probs_b = probs.astype(jnp.bfloat16)
    attended = jnp.einsum("hqk,khd->qhd", probs_b, vals, preferred_element_type=jnp.float32)
    attended = attended.astype(jnp.bfloat16).reshape(rows, feats)
    out_part = lax.dot_general(attended, full_o, dims, preferred_element_type=jnp.float32)
    out_tiles = lax.psum_scatter(
        out_part.astype(jnp.bfloat16), "heads", scatter_dimension=1, tiled=True
    )
    d_att = jnp.dot(grad_out, full_o, preferred_element_type=jnp.float32).astype(jnp.bfloat16)
    d_heads = d_att.reshape(rows, nheads, HD)
    probs = softmax_probs(queries, keys, bias)
    probs_b = probs.astype(jnp.bfloat16)
    dp = jnp.einsum("qhd,khd->hqk", d_heads, vals, preferred_element_type=jnp.float32)
    delta = jnp.sum(probs * dp, axis=-1, keepdims=True)
    d_scores = (probs * (dp - delta)).astype(jnp.bfloat16)
    scale = HD ** (-0.5)
    d_q = jnp.einsum("hqk,khd->qhd", d_scores, keys, preferred_element_type=jnp.float32) * scale
    key_terms = (
        jnp.einsum(
            "hqk,qhd->khd", d_scores[:, :, : 4 * rows], queries, preferred_element_type=jnp.float32
        )
        * scale
    )
    val_terms = jnp.einsum(
        "hqk,qhd->khd", probs_b[:, :, : 4 * rows], d_heads, preferred_element_type=jnp.float32
    )
    terms = jnp.stack(
        [key_terms.reshape(4, rows, feats), val_terms.reshape(4, rows, feats)], axis=1
    ).astype(jnp.bfloat16)
    total = jnp.zeros((2, rows, feats), jnp.float32)
    for index in range(4):
        off_row, off_col = offsets[index]
        total = total + jnp.where(
            (off_row == 0) & (off_col == 0), terms[index].astype(jnp.float32), 0.0
        )
    for near_row in (-1, 0, 1):
        for near_col in (-1, 0, 1):
            if near_row == 0 and near_col == 0:
                continue
            outgoing = jnp.zeros((2, rows, feats), jnp.bfloat16)
            for index in range(4):
                off_row, off_col = offsets[index]
                outgoing = jnp.where(
                    (off_row == near_row) & (off_col == near_col), terms[index], outgoing
                )
            incoming = from_behind(outgoing, "seq", near_row * grid_cols + near_col)
            total = total + incoming.astype(jnp.float32)
    pull_q = jax.vjp(lambda a: head_norm(a, q_gain), q)[1]
    pull_k = jax.vjp(lambda a: head_norm(a, k_gain), k)[1]
    d_q_raw = pull_q(d_q.reshape(rows, feats))[0].astype(jnp.bfloat16)
    d_k_raw = pull_k(total[0])[0].astype(jnp.bfloat16)
    d_v = total[1].astype(jnp.bfloat16)
    grad_part = lax.dot_general(d_q_raw, full_q, dims, preferred_element_type=jnp.float32)
    grad_part = grad_part + lax.dot_general(
        d_k_raw, full_k, dims, preferred_element_type=jnp.float32
    )
    grad_part = grad_part + lax.dot_general(d_v, full_v, dims, preferred_element_type=jnp.float32)
    grad_tiles = lax.psum_scatter(
        grad_part.astype(jnp.bfloat16), "heads", scatter_dimension=1, tiled=True
    )
    return (out_tiles, grad_tiles)


def solution(mesh):
    in_specs = (
        P("seq", None),
        P("seq", None),
        P("seq", "heads"),
        P("seq", "heads"),
        P("seq", "heads"),
        P("seq", "heads"),
        P("heads"),
        P("heads"),
        P(),
        P(),
        P("seq", None),
    )
    out_specs = (P("seq", "heads"), P("seq", "heads"))
    return jax.shard_map(
        per_device, mesh=mesh, in_specs=in_specs, out_specs=out_specs, check_vma=False
    )
```

profile of v0, /device:TPU:25, one launch (start us, length us, event | category | flops | bytes accessed | tf_op | source)
XLA Modules:
  0.0 876.0 jit_solution(16259114979072248656)
XLA Ops:
  14.7 1.2 multiply_bitcast_fusion
  16.6 102.0 %all-gather.11.cloned.1.call-done = bf16[128,12,384]{2,1,0:T(8,128)(2,1)} async-done(((bf16[1,12,384]{2,1,0:T(8,128)(2,1)}), bf16[128,12,384]{2,1,0:T(8,128)(2,1)}) %all-gather.11.cloned.1.call-update) | async-done | bytes 1179664 | tf_op jit(solution)/shard_map/all_gather | solution.py:41
  118.5 2.3 reshape.206
  123.1 98.1 %all-gather.13.cloned.1.call-done = bf16[128,12,384]{2,1,0:T(8,128)(2,1)} async-done(((bf16[1,12,384]{2,1,0:T(8,128)(2,1)}), bf16[128,12,384]{2,1,0:T(8,128)(2,1)}) %all-gather.13.cloned.1.call-update) | async-done | bytes 1179664 | tf_op jit(solution)/shard_map/all_gather | solution.py:42
  221.1 2.3 reshape.208
  224.6 5.6 collective-permute-start
  230.2 3.1 collective-permute-start.1
  233.3 2.0 collective-permute-start.2
  235.3 10.2 %collective-permute-start.3 = (bf16[2,192,384]{2,1,0:T(8,128)(2,1)}, bf16[2,192,384]{2,1,0:T(8,128)(2,1)}, u32[]{:S(2)}, u32[]{:S(2)}) collective-permute-start(bf16[2,192,384]{2,1,0:T(8,128)(2,1)} %pad_maximum_fusion.2), channel_id=1, source_target_pairs={{0,4},{4,8},{8,12},{12,16},{16,20},{20,24},{24,28},{28,32},{32,36}... | collective-permute-start | bytes 884744 | tf_op jit(solution)/shard_map/ppermute | solution.py:12
  245.5 1.9 collective-permute-start.4
  248.0 204.4 %all-gather.4 = bf16[128,2,384]{2,1,0:T(2,128)(2,1)S(1)} all-gather(bf16[1,2,384]{2,1,0:T(2,128)(2,1)S(1)} %fusion.66), channel_id=1, replica_groups=mesh['seq'=128,'heads'=4] {'seq'}, dimensions={0}, use_global_device_ids=true | all-gather | bytes 198144 | tf_op jit(solution)/shard_map/all_gather | solution.py:56
  453.2 3.2 reshape.212
  456.4 1.7 fusion.80
  459.0 1.9 multiply_reduce_fusion.2
  462.7 1.6 fusion.12
  464.6 1.4 fusion.36
  466.0 3.2 reshape.216
  469.2 2.6 fusion.10
  471.8 221.3 %all-gather.2 = bf16[128,2,384]{2,1,0:T(2,128)(2,1)S(1)} all-gather(bf16[1,2,384]{2,1,0:T(2,128)(2,1)S(1)} %copy-done.31), channel_id=1, replica_groups=mesh['seq'=128,'heads'=4] {'seq'}, dimensions={0}, use_global_device_ids=true | all-gather | bytes 198144 | tf_op jit(solution)/shard_map/all_gather | solution.py:57
  693.9 1.3 collective-permute-start.5
  695.2 1.0 bitcast_dynamic-update-slice_fusion.8
  696.2 1.3 collective-permute-start.6
  697.5 1.0 bitcast_dynamic-update-slice_fusion.7
  698.5 1.5 collective-permute-start.7
  700.0 1.0 bitcast_dynamic-update-slice_fusion.6
  701.0 1.0 bitcast_dynamic-update-slice_fusion.5
  702.1 1.0 bitcast_dynamic-update-slice_fusion.3
  703.9 3.5 collective-permute-done.6
  707.5 14.8 %collective-permute-done.7 = bf16[2,192,384]{2,1,0:T(8,128)(2,1)S(1)} collective-permute-done((bf16[2,192,384]{2,1,0:T(8,128)(2,1)}, bf16[2,192,384]{2,1,0:T(8,128)(2,1)S(1)}, u32[]{:S(2)}, u32[]{:S(2)}) %collective-permute-start.7) | collective-permute-done | bytes 294944 | tf_op jit(solution)/shard_map/ppermute | solution.py:12
  723.6 2.6 concatenate.22
  726.2 2.0 copy_dynamic-update-slice_fusion
  729.2 2.1 copy_dynamic-update-slice_fusion.1
  732.8 3.4 fusion.76
  736.2 2.6 multiply_reduce_fusion
  740.2 2.3 fusion.11
  742.5 1.2 fusion.4
  743.6 2.9 reshape.219
  746.6 2.1 copy.104
  748.7 1.6 reshape.220
  750.2 2.1 copy.105
  752.4 2.2 select_bitcast_fusion.7
  754.6 1.1 select_bitcast_fusion.6
  755.8 2.0 collective-permute-start.12
  757.8 6.0 collective-permute-start.13
  763.8 1.3 collective-permute-start.9
  765.1 1.1 select_bitcast_fusion.5
  766.2 1.3 collective-permute-start.10
  767.5 2.1 collective-permute-start.11
  769.6 2.3 fusion.31
  771.9 1.4 convolution_convert_fusion
  773.9 2.2 copy.112
  776.4 11.0 %collective-permute-start.14 = (bf16[2,192,384]{2,1,0:T(8,128)(2,1)}, bf16[2,192,384]{2,1,0:T(8,128)(2,1)S(1)}, u32[]{:S(2)}, u32[]{:S(2)}) collective-permute-start(bf16[2,192,384]{2,1,0:T(8,128)(2,1)} %get-tuple-element.18), channel_id=1, source_target_pairs={{0,128},{4,132},{8,136},{12,140},{16,144},{20,148},{24,152},{28,15... | collective-permute-start | bytes 884744 | tf_op jit(solution)/shard_map/ppermute | solution.py:12
  787.3 12.0 %collective-permute-start.15 = (bf16[2,192,384]{2,1,0:T(8,128)(2,1)S(1)}, bf16[2,192,384]{2,1,0:T(8,128)(2,1)S(1)}, u32[]{:S(2)}, u32[]{:S(2)}) collective-permute-start(bf16[2,192,384]{2,1,0:T(8,128)(2,1)S(1)} %select_bitcast_fusion), channel_id=1, source_target_pairs={{0,132},{4,136},{8,140},{12,144},{16,148},{20,152},{24,156},{28,16... | collective-permute-start | bytes 884744 | tf_op jit(solution)/shard_map/ppermute | solution.py:12
  799.4 1.5 collective-permute-start.8
  800.9 2.8 fusion.40
  803.7 10.4 %collective-permute-done.15 = bf16[2,192,384]{2,1,0:T(8,128)(2,1)S(1)} collective-permute-done((bf16[2,192,384]{2,1,0:T(8,128)(2,1)S(1)}, bf16[2,192,384]{2,1,0:T(8,128)(2,1)S(1)}, u32[]{:S(2)}, u32[]{:S(2)}) %collective-permute-start.15) | collective-permute-done | bytes 294944 | tf_op jit(solution)/shard_map/ppermute | solution.py:12
  814.1 2.2 collective-permute-done.8
  816.3 1.9 fusion.21
  819.9 1.4 multiply_reduce_fusion.1
  821.8 2.1 convolution_add_fusion.1
  824.6 1.2 copy.114
  825.9 1.7 copy.113
  827.6 39.9 %reduce-scatter.9.cloned.1.call-done = bf16[384,192]{1,0:T(8,128)(2,1)} async-done(((bf16[1536,192]{1,0:T(8,128)(2,1)}), bf16[384,192]{1,0:T(8,128)(2,1)}) %reduce-scatter.9.cloned.1.call-update) | async-done | bytes 147472
  867.5 1.7 copy.115
  (141 shorter events, 23.4 us)
Async XLA Ops:
  7.2 113.6 %copy-start = (bf16[192,1536]{1,0:T(8,128)(2,1)S(1)}, bf16[192,1536]{1,0:T(8,128)(2,1)}, u32[]{:S(2)}) copy-start(bf16[192,1536]{1,0:T(8,128)(2,1)} %param.11) | copy-start | bytes 1769476
  7.2 111.4 %all-gather.11.cloned.1.call-start = ((), (), s32[]{:S(2)}) async-start(), calls=%async_computation.2 | async-start | bytes 1585152 | tf_op jit(solution)/shard_map/all_gather | solution.py:41
  7.9 213.2 %all-gather.13.cloned.1.call-start = ((), (), s32[]{:S(2)}) async-start(), calls=%async_computation.3 | async-start | bytes 1585152 | tf_op jit(solution)/shard_map/all_gather | solution.py:42
  8.7 444.5 %all-gather.15.cloned.1.call-start = ((), (), s32[]{:S(2)}) async-start(), calls=%async_computation.4 | async-start | bytes 1585152 | tf_op jit(solution)/shard_map/all_gather | solution.py:40
  9.4 456.6 %all-gather.17.cloned.1.call-start = ((), (), s32[]{:S(2)}) async-start(), calls=%async_computation.5 | async-start | bytes 1585152 | tf_op jit(solution)/shard_map/all_gather | solution.py:43
  10.0 815.9 %reduce-scatter.7.cloned.1.call-start = ((), (), s32[]{:S(2)}) async-start(), calls=%async_computation.6 | async-start | bytes 983040
  121.3 1.8 copy-start.10
  121.3 1.7 copy-start.27
  121.4 1.6 copy-start.16
  122.2 0.8 copy-start.17
  223.4 24.1 %copy-start.28 = (bf16[2,1536]{1,0:T(2,128)(2,1)S(1)}, bf16[2,1536]{1,0:T(2,128)(2,1)}, u32[]{:S(2)}) copy-start(bf16[2,1536]{1,0:T(2,128)(2,1)} %param.12) | copy-start | bytes 18436
  224.6 469.3 %collective-permute-start = (bf16[2,192,384]{2,1,0:T(8,128)(2,1)}, bf16[2,192,384]{2,1,0:T(8,128)(2,1)}, u32[]{:S(2)}, u32[]{:S(2)}) collective-permute-start(bf16[2,192,384]{2,1,0:T(8,128)(2,1)} %pad_maximum_fusion.2), channel_id=1, source_target_pairs={{0,132},{4,136},{8,140},{12,144},{16,148},{20,152},{24,156},{28,16... | collective-permute-start | bytes 884744 | tf_op jit(solution)/shard_map/ppermute | solution.py:12
  230.2 466.0 %collective-permute-start.1 = (bf16[2,192,384]{2,1,0:T(8,128)(2,1)}, bf16[2,192,384]{2,1,0:T(8,128)(2,1)}, u32[]{:S(2)}, u32[]{:S(2)}) collective-permute-start(bf16[2,192,384]{2,1,0:T(8,128)(2,1)} %pad_maximum_fusion.2), channel_id=1, source_target_pairs={{0,128},{4,132},{8,136},{12,140},{16,144},{20,148},{24,152},{28,15... | collective-permute-start | bytes 884744 | tf_op jit(solution)/shard_map/ppermute | solution.py:12
  233.3 465.2 %collective-permute-start.2 = (bf16[2,192,384]{2,1,0:T(8,128)(2,1)}, bf16[2,192,384]{2,1,0:T(8,128)(2,1)}, u32[]{:S(2)}, u32[]{:S(2)}) collective-permute-start(bf16[2,192,384]{2,1,0:T(8,128)(2,1)} %pad_maximum_fusion.2), channel_id=1, source_target_pairs={{0,124},{4,128},{8,132},{12,136},{16,140},{20,144},{24,148},{28,15... | collective-permute-start | bytes 884744 | tf_op jit(solution)/shard_map/ppermute | solution.py:12
  235.3 465.7 %collective-permute-start.3 = (bf16[2,192,384]{2,1,0:T(8,128)(2,1)}, bf16[2,192,384]{2,1,0:T(8,128)(2,1)}, u32[]{:S(2)}, u32[]{:S(2)}) collective-permute-start(bf16[2,192,384]{2,1,0:T(8,128)(2,1)} %pad_maximum_fusion.2), channel_id=1, source_target_pairs={{0,4},{4,8},{8,12},{12,16},{16,20},{20,24},{24,28},{28,32},{32,36}... | collective-permute-start | bytes 884744 | tf_op jit(solution)/shard_map/ppermute | solution.py:12
  245.5 456.6 %collective-permute-start.4 = (bf16[2,192,384]{2,1,0:T(8,128)(2,1)}, bf16[2,192,384]{2,1,0:T(8,128)(2,1)}, u32[]{:S(2)}, u32[]{:S(2)}) collective-permute-start(bf16[2,192,384]{2,1,0:T(8,128)(2,1)} %pad_maximum_fusion.2), channel_id=1, source_target_pairs={{4,0},{8,4},{12,8},{16,12},{20,16},{24,20},{28,24},{32,28},{36,32}... | collective-permute-start | bytes 884744 | tf_op jit(solution)/shard_map/ppermute | solution.py:12
  458.2 6.4 copy-start.7
  462.7 1.6 copy-start.24
  469.2 2.6 copy-start.31
  693.9 9.9 %collective-permute-start.5 = (bf16[2,192,384]{2,1,0:T(8,128)(2,1)}, bf16[2,192,384]{2,1,0:T(8,128)(2,1)S(1)}, u32[]{:S(2)}, u32[]{:S(2)}) collective-permute-start(bf16[2,192,384]{2,1,0:T(8,128)(2,1)} %pad_maximum_fusion.2), channel_id=1, source_target_pairs={{124,0},{128,4},{132,8},{136,12},{140,16},{144,20},{148,24},{152,2... | collective-permute-start | bytes 884744 | tf_op jit(solution)/shard_map/ppermute | solution.py:12
  696.2 11.2 %collective-permute-start.6 = (bf16[2,192,384]{2,1,0:T(8,128)(2,1)}, bf16[2,192,384]{2,1,0:T(8,128)(2,1)S(1)}, u32[]{:S(2)}, u32[]{:S(2)}) collective-permute-start(bf16[2,192,384]{2,1,0:T(8,128)(2,1)} %pad_maximum_fusion.2), channel_id=1, source_target_pairs={{128,0},{132,4},{136,8},{140,12},{144,16},{148,20},{152,24},{156,2... | collective-permute-start | bytes 884744 | tf_op jit(solution)/shard_map/ppermute | solution.py:12
  698.5 23.7 %collective-permute-start.7 = (bf16[2,192,384]{2,1,0:T(8,128)(2,1)}, bf16[2,192,384]{2,1,0:T(8,128)(2,1)S(1)}, u32[]{:S(2)}, u32[]{:S(2)}) collective-permute-start(bf16[2,192,384]{2,1,0:T(8,128)(2,1)} %pad_maximum_fusion.2), channel_id=1, source_target_pairs={{132,0},{136,4},{140,8},{144,12},{148,16},{152,20},{156,24},{160,2... | collective-permute-start | bytes 884744 | tf_op jit(solution)/shard_map/ppermute | solution.py:12
  729.2 2.1 copy-start.19
  729.2 2.8 copy-start.20
  729.2 3.6 copy-start.25
  729.2 3.6 copy-start.32
  732.8 3.4 copy-start.21
  736.2 2.6 copy-start.18
  738.9 0.9 copy-start.22
  739.3 3.2 copy-start.12
  740.1 2.3 copy-start.26
  754.6 11.6 %copy-start.3 = (bf16[1,2,192,384]{3,2,1,0:T(8,128)(2,1)}, bf16[1,2,192,384]{3,2,1,0:T(8,128)(2,1)S(1)}, u32[]{:S(2)}) copy-start(bf16[1,2,192,384]{3,2,1,0:T(8,128)(2,1)S(1)} %get-tuple-element.5) | copy-start | bytes 884740
  754.6 11.6 %copy-start.5 = (bf16[1,2,192,384]{3,2,1,0:T(8,128)(2,1)}, bf16[1,2,192,384]{3,2,1,0:T(8,128)(2,1)S(1)}, u32[]{:S(2)}) copy-start(bf16[1,2,192,384]{3,2,1,0:T(8,128)(2,1)S(1)} %get-tuple-element.6) | copy-start | bytes 884740
  755.8 13.8 %copy-start.8 = (f32[192,384]{1,0:T(8,128)S(1)}, f32[192,384]{1,0:T(8,128)}, u32[]{:S(2)}) copy-start(f32[192,384]{1,0:T(8,128)} %copy-done.7) | copy-start | bytes 884740
  755.8 13.8 %copy-start.13 = (bf16[3,192,1024]{2,1,0:T(8,128)(2,1)S(1)}, bf16[3,192,1024]{2,1,0:T(8,128)(2,1)}, u32[]{:S(2)}) copy-start(bf16[3,192,1024]{2,1,0:T(8,128)(2,1)} %copy-done.12) | copy-start | bytes 3538948
  755.8 13.8 %copy-start.30 = (f32[3,128]{1,0:T(4,128)S(1)}, f32[3,128]{1,0:T(4,128)}, u32[]{:S(2)}) copy-start(f32[3,128]{1,0:T(4,128)} %multiply_bitcast_fusion) | copy-start | bytes 4612
  755.8 20.6 %collective-permute-start.12 = (bf16[2,192,384]{2,1,0:T(8,128)(2,1)}, bf16[2,192,384]{2,1,0:T(8,128)(2,1)}, u32[]{:S(2)}, u32[]{:S(2)}) collective-permute-start(bf16[2,192,384]{2,1,0:T(8,128)(2,1)} %get-tuple-element.15), channel_id=1, source_target_pairs={{0,4},{4,8},{8,12},{12,16},{16,20},{20,24},{24,28},{28,32},{32,36}... | collective-permute-start | bytes 884744 | tf_op jit(solution)/shard_map/ppermute | solution.py:12
  757.8 29.5 %collective-permute-start.13 = (bf16[2,192,384]{2,1,0:T(8,128)(2,1)}, bf16[2,192,384]{2,1,0:T(8,128)(2,1)}, u32[]{:S(2)}, u32[]{:S(2)}) collective-permute-start(bf16[2,192,384]{2,1,0:T(8,128)(2,1)} %get-tuple-element.14), channel_id=1, source_target_pairs={{0,124},{4,128},{8,132},{12,136},{16,140},{20,144},{24,148},{28,15... | collective-permute-start | bytes 884744 | tf_op jit(solution)/shard_map/ppermute | solution.py:12
  763.8 35.6 %collective-permute-start.9 = (bf16[2,192,384]{2,1,0:T(8,128)(2,1)}, bf16[2,192,384]{2,1,0:T(8,128)(2,1)}, u32[]{:S(2)}, u32[]{:S(2)}) collective-permute-start(bf16[2,192,384]{2,1,0:T(8,128)(2,1)} %get-tuple-element.13), channel_id=1, source_target_pairs={{128,0},{132,4},{136,8},{140,12},{144,16},{148,20},{152,24},{156,2... | collective-permute-start | bytes 884744 | tf_op jit(solution)/shard_map/ppermute | solution.py:12
  766.2 37.5 %collective-permute-start.10 = (bf16[2,192,384]{2,1,0:T(8,128)(2,1)}, bf16[2,192,384]{2,1,0:T(8,128)(2,1)}, u32[]{:S(2)}, u32[]{:S(2)}) collective-permute-start(bf16[2,192,384]{2,1,0:T(8,128)(2,1)} %get-tuple-element.16), channel_id=1, source_target_pairs={{124,0},{128,4},{132,8},{136,12},{140,16},{144,20},{148,24},{152,2... | collective-permute-start | bytes 884744 | tf_op jit(solution)/shard_map/ppermute | solution.py:12
  767.5 4.4 copy-start.1
  767.5 4.4 copy-start.23
  767.5 36.2 %collective-permute-start.11 = (bf16[2,192,384]{2,1,0:T(8,128)(2,1)}, bf16[2,192,384]{2,1,0:T(8,128)(2,1)}, u32[]{:S(2)}, u32[]{:S(2)}) collective-permute-start(bf16[2,192,384]{2,1,0:T(8,128)(2,1)} %get-tuple-element.17), channel_id=1, source_target_pairs={{4,0},{8,4},{12,8},{16,12},{20,16},{24,20},{28,24},{32,28},{36,32}... | collective-permute-start | bytes 884744 | tf_op jit(solution)/shard_map/ppermute | solution.py:12
  776.2 24.7 %copy-start.29 = (f32[192,3]{0,1:T(4,128)S(1)}, f32[192,3]{0,1:T(4,128)}, u32[]{:S(2)}) copy-start(f32[192,3]{0,1:T(4,128)} %multiply_multiply_fusion.1) | copy-start | bytes 6916
  776.2 91.3 %reduce-scatter.9.cloned.1.call-start = ((), (), s32[]{:S(2)}) async-start(), calls=%async_computation.7 | async-start | bytes 983040
  776.2 24.7 %copy-start.2 = (bf16[1536,384]{1,0:T(8,128)(2,1)S(1)}, bf16[1536,384]{1,0:T(8,128)(2,1)}, u32[]{:S(2)}) copy-start(bf16[1536,384]{1,0:T(8,128)(2,1)} %reshape.212) | copy-start | bytes 3538948
  776.3 24.7 %copy-start.9 = (f32[192,384]{1,0:T(8,128)S(1)}, f32[192,384]{1,0:T(8,128)}, u32[]{:S(2)}) copy-start(f32[192,384]{1,0:T(8,128)} %copy-done.7) | copy-start | bytes 884740
  776.4 27.4 %collective-permute-start.14 = (bf16[2,192,384]{2,1,0:T(8,128)(2,1)}, bf16[2,192,384]{2,1,0:T(8,128)(2,1)S(1)}, u32[]{:S(2)}, u32[]{:S(2)}) collective-permute-start(bf16[2,192,384]{2,1,0:T(8,128)(2,1)} %get-tuple-element.18), channel_id=1, source_target_pairs={{0,128},{4,132},{8,136},{12,140},{16,144},{20,148},{24,152},{28,15... | collective-permute-start | bytes 884744 | tf_op jit(solution)/shard_map/ppermute | solution.py:12
  787.3 26.8 %collective-permute-start.15 = (bf16[2,192,384]{2,1,0:T(8,128)(2,1)S(1)}, bf16[2,192,384]{2,1,0:T(8,128)(2,1)S(1)}, u32[]{:S(2)}, u32[]{:S(2)}) collective-permute-start(bf16[2,192,384]{2,1,0:T(8,128)(2,1)S(1)} %select_bitcast_fusion), channel_id=1, source_target_pairs={{0,132},{4,136},{8,140},{12,144},{16,148},{20,152},{24,156},{28,16... | collective-permute-start | bytes 884744 | tf_op jit(solution)/shard_map/ppermute | solution.py:12
  799.4 16.9 %collective-permute-start.8 = (bf16[2,192,384]{2,1,0:T(8,128)(2,1)}, bf16[2,192,384]{2,1,0:T(8,128)(2,1)S(1)}, u32[]{:S(2)}, u32[]{:S(2)}) collective-permute-start(bf16[2,192,384]{2,1,0:T(8,128)(2,1)} %get-tuple-element.2), channel_id=1, source_target_pairs={{132,0},{136,4},{140,8},{144,12},{148,16},{152,20},{156,24},{160,2... | collective-permute-start | bytes 884744 | tf_op jit(solution)/shard_map/ppermute | solution.py:12
  800.9 15.4 %copy-start.4 = (bf16[1,2,192,384]{3,2,1,0:T(8,128)(2,1)S(1)}, bf16[1,2,192,384]{3,2,1,0:T(8,128)(2,1)}, u32[]{:S(2)}) copy-start(bf16[1,2,192,384]{3,2,1,0:T(8,128)(2,1)} %copy-done.3) | copy-start | bytes 884740
  800.9 15.4 %copy-start.6 = (bf16[1,2,192,384]{3,2,1,0:T(8,128)(2,1)S(1)}, bf16[1,2,192,384]{3,2,1,0:T(8,128)(2,1)}, u32[]{:S(2)}) copy-start(bf16[1,2,192,384]{3,2,1,0:T(8,128)(2,1)} %copy-done.5) | copy-start | bytes 884740
  818.2 0.8 copy-start.14
  819.0 2.8 copy-start.11
  821.8 2.2 copy-start.15
Sparse Core Ops, SparseCore 0:
  12.1 106.3 all-gather.10
  122.6 98.4 all-gather.12
  225.2 106.3 all-gather.14
  335.6 98.1 all-gather.16
  776.3 49.5 reduce-scatter.6
  828.6 38.8 reduce-scatter.8
where the time goes:
time: 879 us; the launch traced here: 876 us
  blocking collectives  426 us (48%)
  waiting for transfers between devices  274 us (31%)
  starting transfers between devices  64.2 us (7%)
  local copies, waits for them, and re-layouts  52.6 us (6%)
  matrix products  26.2 us (3%)
  between operations  17.5 us (2%)
  other arithmetic  15.5 us (2%)
    all_gather x1, blocking collectives, per_device(): lax.all_gather(text_vb, 'seq', axis=0, tiled=True)  221 us
    all_gather x1, blocking collectives, per_device(): lax.all_gather(text_kn, 'seq', axis=0, tiled=True)  204 us
    all_gather x1, waiting for transfers between devices, per_device(): lax.all_gather(w_key, 'seq', axis=0, tiled=True)  102 us
    all_gather x1, waiting for transfers between devices, per_device(): lax.all_gather(w_value, 'seq', axis=0, tiled=True)  98.1 us
    ppermute x16, starting transfers between devices, from_behind(): return lax.ppermute(shard, axis, pairs)  64 us
    unnamed x8, waiting for transfers between devices  42.6 us
    ppermute x16, waiting for transfers between devices, from_behind(): return lax.ppermute(shard, axis, pairs)  31.6 us
    unnamed x85, local copies, waits for them, and re-layouts  30.1 us
  transfers between devices with their start and end apart: 22, of which 9 were waited for; matrix products, arithmetic and copies ran while one was open for 7% of the time, Pallas kernels for 0%

commit v1 on v0

v1 whole, which is shorter than its diff:
```python
import functools

import jax
import jax.numpy as jnp
from jax import lax
from jax.experimental import pallas as pl
from jax.experimental.pallas import tpu as pltpu
from jax.sharding import PartitionSpec as P

HD = 128
NH = 3
W = NH * HD
ROWS = 192
TEXT = 256
EPS = 1e-6
SCALE = HD**-0.5
ZH_ORDER = (0, 1, 3, 2)
F32 = jnp.float32
BF16 = jnp.bfloat16
NT = (((1,), (1,)), ((), ()))
TN = (((0,), (0,)), ((), ()))


def place_of(x, zh, y, core):
    return ((x * 4 + zh) * 4 + y) * 2 + core


def all_places():
    return [(x, z, y, c) for x in range(4) for z in range(4) for y in range(4) for c in range(2)]


def seq_move(value, target):
    pairs = []
    for at in all_places():
        to = target(*at)
        if to is not None:
            pairs.append((place_of(*at), place_of(*to)))
    return lax.ppermute(value, "seq", pairs)


def along_x(value, rel):
    return seq_move(value, lambda x, z, y, c: ((x - rel) % 4, z, y, c))


def along_y(value, rel):
    return seq_move(value, lambda x, z, y, c: (x, z, (y - rel) % 4, c))


def across_zh(value, mask):
    return seq_move(value, lambda x, z, y, c: (x, z ^ mask, y, c))


def core_mate(value):
    return seq_move(value, lambda x, z, y, c: (x, z, y, 1 - c))


def next_chip(value):
    def target(x, z, y, c):
        col = (z * 4 + y) * 2 + c
        col = col + 1 if c == 1 else col - 1
        if not 0 <= col < 32:
            return None
        return (x, col // 8, col // 2 % 4, col % 2)

    return seq_move(value, target)


def row_even(value):
    return seq_move(value, lambda x, z, y, c: (x ^ 1, z, y, c))


def row_odd(value):
    return seq_move(value, lambda x, z, y, c: (3 - x, z, y, c) if x in (1, 2) else None)


def dot(a, b, dims=(((1,), (0,)), ((), ()))):
    return lax.dot_general(a, b, dims, preferred_element_type=F32)


def norm_rows(a, gain):
    r = lax.rsqrt(jnp.mean(a * a, axis=-1, keepdims=True) + EPS)
    return a * r * gain


def norm_pull(a, gain, dy):
    r = lax.rsqrt(jnp.mean(a * a, axis=-1, keepdims=True) + EPS)
    t = dy * gain
    return r * t - a * (r * r * r * jnp.mean(t * a, axis=-1, keepdims=True))


def head(h):
    return slice(h * HD, (h + 1) * HD)


def val(h):
    return slice(W + h * HD, W + (h + 1) * HD)


def call(kernel, outs, scratch=(), mib=32, flops=10**9):
    return pl.pallas_call(
        kernel,
        out_shape=outs,
        scratch_shapes=scratch,
        compiler_params=pltpu.CompilerParams(vmem_limit_bytes=mib * 2**20),
        cost_estimate=pl.CostEstimate(flops=flops, bytes_accessed=8 * 10**6, transcendentals=0),
    )


def shape(dims, dtype):
    return jax.ShapeDtypeStruct(dims, dtype)


def kv_kernel(xp, wo, wt, gain, kv, kraw):
    half = wo.shape[0]
    acc = dot(xp[:, :half], wo[...]) + dot(xp[:, half:], wt[...])
    kraw[...] = acc[:, :W]
    for h in range(NH):
        kv[:, head(h)] = norm_rows(acc[:, head(h)], gain[:, head(h)]).astype(BF16)
    kv[:, W:] = acc[:, W:].astype(BF16)


def q_kernel(xp, gp, tp, ao, at, bo, bt, q_gain, k_gain, qraw, qn, d_att, tkv):
    half = bo.shape[0]
    q = dot(xp[:, :half], bo[:, :W]) + dot(xp[:, half:], bt[:, :W])
    qraw[...] = q
    for h in range(NH):
        qn[:, head(h)] = norm_rows(q[:, head(h)], q_gain[:, head(h)]).astype(BF16)
    d = dot(gp[:, :half], bo[:, W:]) + dot(gp[:, half:], bt[:, W:])
    d_att[...] = d.astype(BF16)
    t = dot(tp[:, :half], ao[...]) + dot(tp[:, half:], at[...])
    for h in range(NH):
        tkv[:, head(h)] = norm_rows(t[:, head(h)], k_gain[:, head(h)]).astype(BF16)
    tkv[:, W:] = t[:, W:].astype(BF16)


def attend_kernel(qn, d_att, qraw, q_gain, pair, far, tkv, bias, att, dq, near_t, far_t, keys):
    n = 4 * ROWS
    keys[: 2 * ROWS, :] = pair[...]
    keys[2 * ROWS : n, :] = far[...]
    keys[n:, :] = tkv[...]
    for h in range(NH):
        qh = qn[:, head(h)]
        dh = d_att[:, head(h)]
        kh = keys[:, head(h)]
        vh = keys[:, val(h)]
        s = dot(qh, kh, NT) * SCALE + bias[...]
        e = jnp.exp(s - jnp.max(s, axis=-1, keepdims=True))
        p = e * (1.0 / jnp.sum(e, axis=-1, keepdims=True))
        pb = p.astype(BF16)
        att[:, head(h)] = dot(pb, vh).astype(BF16)
        dp = dot(dh, vh, NT)
        ds = (p * (dp - jnp.sum(p * dp, axis=-1, keepdims=True))).astype(BF16)
        d_q = dot(ds, kh) * SCALE
        dq[:, head(h)] = norm_pull(qraw[:, head(h)], q_gain[:, head(h)], d_q).astype(BF16)
        kt = (dot(ds[:, :n], qh, TN) * SCALE).astype(BF16)
        vt = dot(pb[:, :n], dh, TN).astype(BF16)
        near_t[:, head(h)] = kt[: 2 * ROWS]
        far_t[:, head(h)] = kt[2 * ROWS :]
        near_t[:, val(h)] = vt[: 2 * ROWS]
        far_t[:, val(h)] = vt[2 * ROWS :]


def out_kernel(att, dq, bo, bt, perm, out, gq):
    for j in range(4):
        rows = slice(j * ROWS, (j + 1) * ROWS)
        o = dot(att[...], bo[rows, W:], NT).astype(BF16)
        t = dot(att[...], bt[rows, W:], NT).astype(BF16)
        out[j] = (dot(o, perm[:, :ROWS], NT) + dot(t, perm[:, ROWS:], NT)).astype(BF16)
        gq[0, j] = dot(dq[...], bo[rows, :W], NT)
        gq[1, j] = dot(dq[...], bt[rows, :W], NT)


def grad_kernel(own, in_a, in_b, kraw, k_gain, gq, ao, at, perm, out):
    total = own[...].astype(F32) + in_a[...].astype(F32) + in_b[...].astype(F32)
    parts = [
        norm_pull(kraw[:, head(h)], k_gain[:, head(h)], total[:, head(h)]).astype(BF16)
        for h in range(NH)
    ]
    d = jnp.concatenate(parts + [total[:, W:].astype(BF16)], axis=1)
    for j in range(4):
        rows = slice(j * ROWS, (j + 1) * ROWS)
        o = (gq[0, j] + dot(d, ao[rows, :], NT)).astype(BF16)
        t = (gq[1, j] + dot(d, at[rows, :], NT)).astype(BF16)
        out[j] = (dot(o, perm[:, :ROWS], NT) + dot(t, perm[:, ROWS:], NT)).astype(BF16)


def spread(value, move):
    return [value, move(value, 1), move(value, 2), move(value, 3)]


def head_sum(blocks, x, me):
    def block(to):
        return lax.dynamic_index_in_dim(blocks, (to - x) % 4, 0, keepdims=False)

    total = block(me).astype(F32)
    for by in (1, 2, 3):
        pairs = [(i, (i + by) % 4) for i in range(4)]
        total = total + lax.ppermute(block((me + by) % 4), "heads", pairs).astype(F32)
    return total.astype(BF16)


def per_device(
    x_tiles, x_text, w_query, w_key, w_value, w_output, q_gain, k_gain, text_mask, windows, grad_out
):
    place = lax.axis_index("seq")
    me = lax.axis_index("heads")
    core, y, zh, x = place % 2, place // 2 % 4, place // 8 % 4, place // 32
    col = place % 32
    start = lax.dynamic_slice(windows, (place, jnp.int32(0)), (1, 2))
    want_down = start[0, 0] == x
    want_right = start[0, 1] == col
    use_even = want_down == (x % 2 == 0)
    use_core = want_right == (core == 0)
    q_gain = q_gain[None, :]
    k_gain = k_gain[None, :]

    order = jnp.arange(1536, dtype=jnp.int32)
    r = order % 12
    zr = jnp.array(ZH_ORDER, jnp.int32)[order // 12 % 4] ^ zh
    yr = (order // 48 + y) % 4
    xr = (order // 192 + x) % 4
    cr = (order // 768) ^ core
    natural = place_of(xr, zr, yr, cr) * 12 + r
    perm = (lax.broadcasted_iota(jnp.int32, (1536, 1536), 0) == natural[None, :]).astype(BF16)
    xg = dot(jnp.concatenate([x_tiles, grad_out]), perm).astype(BF16)
    xp, gp = xg[:ROWS], xg[ROWS:]
    first = jnp.concatenate([natural[:ROWS], natural[768 : 768 + ROWS]]) - 384 * x
    small = (lax.broadcasted_iota(jnp.int32, (384, 384), 0) == first[None, :]).astype(BF16)
    t = jnp.arange(TEXT, dtype=jnp.int32)
    tz = jnp.array(ZH_ORDER, jnp.int32)[t // 2 % 4] ^ zh
    token = place_of((t // 32 + x) % 4, tz, (t // 8 + y) % 4, (t // 128) ^ core) * 2 + t % 2
    valid = jnp.sum(
        jnp.where(t[:, None] == token[None, :], text_mask[:, None], 0), axis=0
    )
    bias = jnp.concatenate(
        [jnp.zeros((4 * ROWS,), F32), jnp.where(valid == 1, 0.0, -1e30).astype(F32)]
    )[None, :]

    mine = jnp.concatenate([w_key, w_value, w_query, w_output], axis=1)
    mine = jnp.concatenate([mine, x_text], axis=0)
    two = jnp.stack([mine, across_zh(mine, 1)])
    four = jnp.concatenate([two, across_zh(two, 3)])
    rows = four[:, :12].reshape(48, 1536)
    text = four[:, 12:].reshape(8, 1536)
    a0 = rows[:, :768]
    b0 = jnp.concatenate([rows[:, 768:], text[:, :768], text[:, 768:]], axis=0)
    a1 = jnp.concatenate(spread(a0, along_y))
    ao = jnp.concatenate(spread(a1, along_x))
    at = core_mate(ao)
    b1 = jnp.stack(spread(b0, along_x))
    b2 = jnp.stack(spread(b1, along_y)).transpose(1, 0, 2, 3)
    b3 = core_mate(b2)
    bo = b2[:, :, :48].reshape(768, 768)
    bt = b3[:, :, :48].reshape(768, 768)
    texts = jnp.stack([b2[:, :, 48:], b3[:, :, 48:]]).reshape(2, 4, 4, 2, 8, 768)
    texts = texts.transpose(0, 1, 2, 4, 3, 5).reshape(TEXT, 1536)
    tp = dot(texts, perm).astype(BF16)

    kv, kraw = call(kv_kernel, (shape((ROWS, 768), BF16), shape((ROWS, W), F32)))(
        xp, ao, at, k_gain
    )
    near = jnp.where(use_core, core_mate(kv), next_chip(kv))
    pair = jnp.concatenate([kv, near])
    far = jnp.where(use_even, row_even(pair), row_odd(pair))
    qraw, qn, d_att, tkv = call(
        q_kernel,
        (
            shape((ROWS, W), F32),
            shape((ROWS, W), BF16),
            shape((ROWS, W), BF16),
            shape((TEXT, 768), BF16),
        ),
    )(xp, gp, tp, ao, at, bo, bt, q_gain, k_gain)
    att, dq, near_t, far_t = call(
        attend_kernel,
        (
            shape((ROWS, W), BF16),
            shape((ROWS, W), BF16),
            shape((2 * ROWS, 768), BF16),
            shape((2 * ROWS, 768), BF16),
        ),
        [pltpu.VMEM((1024, 768), BF16)],
    )(qn, d_att, qraw, q_gain, pair, far, tkv, bias)

    zero = jnp.zeros_like(far_t)
    got_even = row_even(jnp.where(use_even, far_t, zero))
    got_odd = row_odd(jnp.where(use_even, zero, far_t))
    summed = (near_t.astype(F32) + got_even.astype(F32) + got_odd.astype(F32)).astype(BF16)
    own_t, side_t = summed[:ROWS], summed[ROWS:]
    zero = jnp.zeros_like(side_t)
    got_core = core_mate(jnp.where(use_core, side_t, zero))
    got_next = next_chip(jnp.where(use_core, zero, side_t))

    out, gq = call(out_kernel, (shape((4, ROWS, W), BF16), shape((2, 4, ROWS, ROWS), F32)))(
        att, dq, bo, bt, small
    )
    out_tiles = head_sum(out, x, me)
    grad = call(grad_kernel, shape((4, ROWS, W), BF16))(
        own_t, got_core, got_next, kraw, k_gain, gq, ao, at, small
    )
    grad_tiles = head_sum(grad, x, me)
    return (out_tiles, grad_tiles)


def solution(mesh):
    in_specs = (
        P("seq", None),
        P("seq", None),
        P("seq", "heads"),
        P("seq", "heads"),
        P("seq", "heads"),
        P("seq", "heads"),
        P("heads"),
        P("heads"),
        P(),
        P(),
        P("seq", None),
    )
    out_specs = (P("seq", "heads"), P("seq", "heads"))
    return jax.shard_map(
        per_device, mesh=mesh, in_specs=in_specs, out_specs=out_specs, check_vma=False
    )
```

time: 879 us -> 204 us (0.23)
  blocking collectives: 426 us -> 0 us
  waiting for transfers between devices: 274 us -> 50.3 us
  starting transfers between devices: 64.2 us -> 110 us
  local copies, waits for them, and re-layouts: 52.6 us -> 10.9 us
  matrix products: 26.2 us -> 6.42 us
  between operations: 17.5 us -> 3.04 us
  Pallas kernels: 0 us -> 9.44 us
    all_gather x2 -> x0, blocking collectives: 426 us -> none  [the longest x1 221 us: per_device(): lax.all_gather(text_vb, 'seq', axis=0, tiled=True)]
    all_gather x4 -> x0, waiting for transfers between devices: 200 us -> none  [the longest x1 102 us: per_device(): lax.all_gather(w_key, 'seq', axis=0, tiled=True)]
    ppermute x16 -> x30, starting transfers between devices: 64 us -> 110 us  [the longest x24 84.1 us: seq_move(): return lax.ppermute(value, 'seq', pairs)]
    unnamed x8 -> x0, waiting for transfers between devices: 42.6 us -> none
    unnamed x85 -> x58, local copies, waits for them, and re-layouts: 30.1 us -> 2.87 us
    ppermute x16 -> x30, waiting for transfers between devices: 31.6 us -> 50.3 us  [the longest x24 44.1 us: seq_move(): return lax.ppermute(value, 'seq', pairs)]
    dot_general x15 -> x2, matrix products: 22.8 us -> 6.42 us  [dot(): return lax.dot_general(a, b, dims, preferred_element_type=F32)]
    pallas_call x0 -> x5, Pallas kernels: none -> 9.44 us  [the longest x1 3.7 us: per_device(): call(attend_kernel, (shape((ROWS, W), BF16), shape((ROWS, W), BF16), shap...]
  transfers between devices with their start and end apart: 22 -> 30, of which waited for: 9 -> 8; matrix products, arithmetic and copies ran while one was open for 7% -> 11% of each run, Pallas kernels for 0% -> 2%
where the time goes in v1:
time: 204 us; the launch traced here: 203 us
  starting transfers between devices  110 us (54%)
  waiting for transfers between devices  50.3 us (25%)
  other arithmetic  12.1 us (6%)
  local copies, waits for them, and re-layouts  10.9 us (5%)
  Pallas kernels  9.44 us (5%)
  matrix products  6.42 us (3%)
  between operations  3.04 us (1%)
    ppermute x24, starting transfers between devices, seq_move(): return lax.ppermute(value, 'seq', pairs)  84.1 us
    ppermute x24, waiting for transfers between devices, seq_move(): return lax.ppermute(value, 'seq', pairs)  44.1 us
    ppermute x6, starting transfers between devices, head_sum(): lax.ppermute(block((me + by) % 4), 'heads', pairs).astype(F32)  26.4 us
    dot_general x2, matrix products, dot(): return lax.dot_general(a, b, dims, preferred_element_type=F32)  6.42 us
    ppermute x6, waiting for transfers between devices, head_sum(): lax.ppermute(block((me + by) % 4), 'heads', pairs).astype(F32)  6.24 us
  transfers between devices with their start and end apart: 30, of which 8 were waited for; matrix products, arithmetic and copies ran while one was open for 11% of the time, Pallas kernels for 2%

profile of v1, /device:TPU:25, one launch (start us, length us, event | category | flops | bytes accessed | tf_op | source)
XLA Modules:
  0.0 202.7 jit_solution(11033149580414963256)
XLA Ops:
  0.6 0.8 pad_maximum_fusion.7
  1.4 8.8 %collective-permute-start = (bf16[14,1536]{1,0:T(8,128)(2,1)S(1)}, bf16[14,1536]{1,0:T(8,128)(2,1)S(1)}, u32[]{:S(2)}, u32[]{:S(2)}) collective-permute-start(bf16[14,1536]{1,0:T(8,128)(2,1)S(1)} %pad_maximum_fusion.7), channel_id=1, source_target_pairs={{0,32},{4,36},{8,40},{12,44},{16,48},{20,52},{24,56},{28,60},{32,0... | collective-permute-start | bytes 129032 | tf_op jit(solution)/shard_map/ppermute | solution.py:38
  10.5 4.4 %fusion.4 = bf16[384,1536]{1,0:T(8,128)(2,1)} fusion(s32[1536]{0:T(1024)S(1)} %fusion.21, bf16[192,1536]{1,0:T(8,128)(2,1)} %param.23, bf16[192,1536]{1,0:T(8,128)(2,1)} %param.13), kind=kOutput, calls=%fused_computation.5 | convolution fusion | flops 1817247744 | bytes 2365440 | tf_op jit(solution)/shard_map/dot_general | solution.py:77
  15.0 8.8 %collective-permute-start.1 = (bf16[2,14,1536]{2,1,0:T(8,128)(2,1)S(1)}, bf16[2,14,1536]{2,1,0:T(8,128)(2,1)S(1)}, u32[]{:S(2)}, u32[]{:S(2)}) collective-permute-start(bf16[2,14,1536]{2,1,0:T(8,128)(2,1)S(1)} %pad_maximum_fusion.5), channel_id=1, source_target_pairs={{0,96},{4,100},{8,104},{12,108},{16,112},{20,116},{24,120},{28,124... | collective-permute-start | bytes 258056 | tf_op jit(solution)/shard_map/ppermute | solution.py:38
  23.9 8.1 %collective-permute-done.1 = bf16[2,14,1536]{2,1,0:T(8,128)(2,1)S(1)} collective-permute-done((bf16[2,14,1536]{2,1,0:T(8,128)(2,1)S(1)}, bf16[2,14,1536]{2,1,0:T(8,128)(2,1)S(1)}, u32[]{:S(2)}, u32[]{:S(2)}) %collective-permute-start.1) | collective-permute-done | bytes 86048 | tf_op jit(solution)/shard_map/ppermute | solution.py:38
  32.1 2.4 %collective-permute-start.9 = (bf16[48,768]{1,0:T(8,128)(2,1)S(1)}, bf16[48,768]{1,0:T(8,128)(2,1)S(1)}, u32[]{:S(2)}, u32[]{:S(2)}) collective-permute-start(bf16[48,768]{1,0:T(8,128)(2,1)S(1)} %get-tuple-element.41), channel_id=1, source_target_pairs={{0,24},{4,28},{8,0},{12,4},{16,8},{20,12},{24,16},{28,20},{32,56},... | collective-permute-start | bytes 221192 | tf_op jit(solution)/shard_map/ppermute | solution.py:38
  34.5 2.6 %collective-permute-start.10 = (bf16[48,768]{1,0:T(8,128)(2,1)S(1)}, bf16[48,768]{1,0:T(8,128)(2,1)S(1)}, u32[]{:S(2)}, u32[]{:S(2)}) collective-permute-start(bf16[48,768]{1,0:T(8,128)(2,1)S(1)} %get-tuple-element.41), channel_id=1, source_target_pairs={{0,16},{4,20},{8,24},{12,28},{16,0},{20,4},{24,8},{28,12},{32,48},... | collective-permute-start | bytes 221192 | tf_op jit(solution)/shard_map/ppermute | solution.py:38
  37.1 3.8 %collective-permute-start.11 = (bf16[48,768]{1,0:T(8,128)(2,1)S(1)}, bf16[48,768]{1,0:T(8,128)(2,1)S(1)}, u32[]{:S(2)}, u32[]{:S(2)}) collective-permute-start(bf16[48,768]{1,0:T(8,128)(2,1)S(1)} %get-tuple-element.41), channel_id=1, source_target_pairs={{0,8},{4,12},{8,16},{12,20},{16,24},{20,28},{24,0},{28,4},{32,40},... | collective-permute-start | bytes 221192 | tf_op jit(solution)/shard_map/ppermute | solution.py:38
  41.0 3.1 %collective-permute-start.4 = (bf16[64,768]{1,0:T(8,128)(2,1)S(1)}, bf16[64,768]{1,0:T(8,128)(2,1)S(1)}, u32[]{:S(2)}, u32[]{:S(2)}) collective-permute-start(bf16[64,768]{1,0:T(8,128)(2,1)S(1)} %get-tuple-element.45), channel_id=1, source_target_pairs={{0,128},{4,132},{8,136},{12,140},{16,144},{20,148},{24,152},{28,15... | collective-permute-start | bytes 294920 | tf_op jit(solution)/shard_map/ppermute | solution.py:38
  44.1 4.4 %collective-permute-start.3 = (bf16[64,768]{1,0:T(8,128)(2,1)S(1)}, bf16[64,768]{1,0:T(8,128)(2,1)S(1)}, u32[]{:S(2)}, u32[]{:S(2)}) collective-permute-start(bf16[64,768]{1,0:T(8,128)(2,1)S(1)} %get-tuple-element.45), channel_id=1, source_target_pairs={{0,256},{4,260},{8,264},{12,268},{16,272},{20,276},{24,280},{28,28... | collective-permute-start | bytes 294920 | tf_op jit(solution)/shard_map/ppermute | solution.py:38
  48.5 3.1 %collective-permute-start.2 = (bf16[64,768]{1,0:T(8,128)(2,1)S(1)}, bf16[64,768]{1,0:T(8,128)(2,1)S(1)}, u32[]{:S(2)}, u32[]{:S(2)}) collective-permute-start(bf16[64,768]{1,0:T(8,128)(2,1)S(1)} %get-tuple-element.45), channel_id=1, source_target_pairs={{0,384},{4,388},{8,392},{12,396},{16,400},{20,404},{24,408},{28,41... | collective-permute-start | bytes 294920 | tf_op jit(solution)/shard_map/ppermute | solution.py:38
  51.6 1.9 collective-permute-start.12
  53.5 4.0 %collective-permute-start.13 = (bf16[192,768]{1,0:T(8,128)(2,1)S(1)}, bf16[192,768]{1,0:T(8,128)(2,1)S(1)}, u32[]{:S(2)}, u32[]{:S(2)}) collective-permute-start(bf16[192,768]{1,0:T(8,128)(2,1)S(1)} %pad_maximum_fusion.3), channel_id=1, source_target_pairs={{0,256},{4,260},{8,264},{12,268},{16,272},{20,276},{24,280},{28,28... | collective-permute-start | bytes 884744 | tf_op jit(solution)/shard_map/ppermute | solution.py:38
  57.6 1.9 collective-permute-start.14
  59.6 0.8 fusion.57
  60.4 2.7 %collective-permute-start.7 = (bf16[4,64,768]{2,1,0:T(8,128)(2,1)}, bf16[4,64,768]{2,1,0:T(8,128)(2,1)S(1)}, u32[]{:S(2)}, u32[]{:S(2)}) collective-permute-start(bf16[4,64,768]{2,1,0:T(8,128)(2,1)} %get-tuple-element.40), channel_id=1, source_target_pairs={{0,8},{4,12},{8,16},{12,20},{16,24},{20,28},{24,0},{28,4},{32,40},... | collective-permute-start | bytes 1179656 | tf_op jit(solution)/shard_map/ppermute | solution.py:38
  63.1 3.2 %collective-permute-start.6 = (bf16[4,64,768]{2,1,0:T(8,128)(2,1)}, bf16[4,64,768]{2,1,0:T(8,128)(2,1)S(1)}, u32[]{:S(2)}, u32[]{:S(2)}) collective-permute-start(bf16[4,64,768]{2,1,0:T(8,128)(2,1)} %get-tuple-element.40), channel_id=1, source_target_pairs={{0,16},{4,20},{8,24},{12,28},{16,0},{20,4},{24,8},{28,12},{32,48},... | collective-permute-start | bytes 1179656 | tf_op jit(solution)/shard_map/ppermute | solution.py:38
  66.4 2.8 %collective-permute-start.5 = (bf16[4,64,768]{2,1,0:T(8,128)(2,1)}, bf16[4,64,768]{2,1,0:T(8,128)(2,1)}, u32[]{:S(2)}, u32[]{:S(2)}) collective-permute-start(bf16[4,64,768]{2,1,0:T(8,128)(2,1)} %get-tuple-element.40), channel_id=1, source_target_pairs={{0,24},{4,28},{8,0},{12,4},{16,8},{20,12},{24,16},{28,20},{32,56},... | collective-permute-start | bytes 1179656 | tf_op jit(solution)/shard_map/ppermute | solution.py:38
  69.2 1.3 collective-permute-done.14
  70.6 4.8 %collective-permute-start.15 = (bf16[768,768]{1,0:T(8,128)(2,1)S(1)}, bf16[768,768]{1,0:T(8,128)(2,1)S(1)}, u32[]{:S(2)}, u32[]{:S(2)}) collective-permute-start(bf16[768,768]{1,0:T(8,128)(2,1)S(1)} %constant_dynamic-update-slice_fusion.ao.wo), channel_id=1, source_target_pairs={{0,4},{4,0},{8,12},{12,8},{16,20},{20,16},{24,28},{28,24},{32,36},... | collective-permute-start | bytes 3538952 | tf_op jit(solution)/shard_map/ppermute | solution.py:38
  75.6 9.3 %collective-permute-done.5 = bf16[4,64,768]{2,1,0:T(8,128)(2,1)} collective-permute-done((bf16[4,64,768]{2,1,0:T(8,128)(2,1)}, bf16[4,64,768]{2,1,0:T(8,128)(2,1)}, u32[]{:S(2)}, u32[]{:S(2)}) %collective-permute-start.5) | collective-permute-done | bytes 393248 | tf_op jit(solution)/shard_map/ppermute | solution.py:38
  84.9 2.5 %maximum_bitcast_fusion = bf16[4,4,64,768]{3,2,0,1:T(8,128)(2,1)} fusion(bf16[1,4,64,768]{3,2,1,0:T(8,128)(2,1)S(1)} %bitcast.60, bf16[1,4,64,768]{3,2,1,0:T(8,128)(2,1)S(1)} %bitcast.61, bf16[1,4,64,768]{3,2,1,0:T(8,128)(2,1)} %bitcast.7, bf16[1,4,64,768]{3,2,1,0:T(8,128)(2,1)S(1)} %get-tuple-element.39), kind=kLoop, calls=%fused_computation.7 | loop fusion | flops 2359296 | bytes 3145728 | tf_op jit(solution)/shard_map/transpose | solution.py:251
  87.4 3.8 %collective-permute-start.8 = (bf16[4,4,64,768]{3,2,0,1:T(8,128)(2,1)}, bf16[4,4,64,768]{3,2,0,1:T(8,128)(2,1)}, u32[]{:S(2)}, u32[]{:S(2)}) collective-permute-start(bf16[4,4,64,768]{3,2,0,1:T(8,128)(2,1)} %maximum_bitcast_fusion), channel_id=1, source_target_pairs={{0,4},{4,0},{8,12},{12,8},{16,20},{20,16},{24,28},{28,24},{32,36},... | collective-permute-start | bytes 4718600 | tf_op jit(solution)/shard_map/ppermute | solution.py:38
  91.3 0.9 fusion.58
  92.3 0.7 shard_map.141
  93.4 0.7 copy-done.9
  94.2 1.9 collective-permute-start.16
  96.1 1.9 collective-permute-start.17
  98.0 0.5 fusion.62
  99.9 1.4 slice.91
  101.2 1.0 slice_bitcast_fusion.1
  102.7 10.3 %collective-permute-done.17 = bf16[192,768]{1,0:T(8,128)(2,1)} collective-permute-done((bf16[192,768]{1,0:T(8,128)(2,1)S(1)}, bf16[192,768]{1,0:T(8,128)(2,1)}, u32[]{:S(2)}, u32[]{:S(2)}) %collective-permute-start.17) | collective-permute-done | bytes 294944 | tf_op jit(solution)/shard_map/ppermute | solution.py:38
  113.0 1.0 broadcast_select_fusion.5
  114.1 2.6 %collective-permute-start.18 = (bf16[384,768]{1,0:T(8,128)(2,1)S(1)}, bf16[384,768]{1,0:T(8,128)(2,1)S(1)}, u32[]{:S(2)}, u32[]{:S(2)}) collective-permute-start(bf16[384,768]{1,0:T(8,128)(2,1)S(1)} %pad_maximum_fusion.1.pair), channel_id=1, source_target_pairs={{0,128},{4,132},{8,136},{12,140},{16,144},{20,148},{24,152},{28,15... | collective-permute-start | bytes 1769480 | tf_op jit(solution)/shard_map/ppermute | solution.py:38
  116.7 0.9 collective-permute-start.19
  117.6 1.0 slice_bitcast_fusion
  119.0 1.1 pad_maximum_fusion
  120.2 1.4 slice.92
  121.6 0.6 copy-done.22
  122.2 2.0 %fusion.5.tp = bf16[256,1536]{1,0:T(8,128)(2,1)S(1)} fusion(bf16[256,1536]{1,0:T(8,128)(2,1)S(1)} %bitcast.55, s32[1536]{0:T(1024)S(1)} %copy-done.22), kind=kOutput, calls=%fused_computation.6 | convolution fusion | flops 1210712064 | bytes 1579008 | tf_op jit(solution)/shard_map/dot_general | solution.py:77
  124.3 1.4 shard_map.140
  125.8 3.7 %shard_map.142 = (bf16[192,384]{1,0:T(8,128)(2,1)S(1)}, bf16[192,384]{1,0:T(8,128)(2,1)S(1)}, bf16[384,768]{1,0:T(8,128)(2,1)S(1)}, bf16[384,768]{1,0:T(8,128)(2,1)S(1)}) custom-call(bf16[192,384]{1,0:T(8,128)(2,1)S(1)} %get-tuple-element.14.qn, bf16[192,384]{1,0:T(8,128)(2,1)S(1)} %get-tuple-element.15.d_att, f32[192,384]{1,0:T(8,128)S(1)} %get-tuple-element.16.qraw, ...), custom_call_target="tpu_custom_call" | custom-call | flops 1000000000 | bytes 8000000 | tf_op jit(solution)/shard_map/pallas_call | solution.py:274
  129.5 0.8 copy-done.8
  130.3 1.1 broadcast_select_fusion.1
  131.5 1.5 collective-permute-start.24
  132.9 6.8 %collective-permute-start.23 = (bf16[384,768]{1,0:T(8,128)(2,1)}, bf16[384,768]{1,0:T(8,128)(2,1)}, u32[]{:S(2)}, u32[]{:S(2)}) collective-permute-start(bf16[384,768]{1,0:T(8,128)(2,1)} %get-tuple-element.34), channel_id=1, source_target_pairs={{0,128},{4,132},{8,136},{12,140},{16,144},{20,148},{24,152},{28,15... | collective-permute-start | bytes 1769480 | tf_op jit(solution)/shard_map/ppermute | solution.py:38
  139.9 0.8 fusion.61
  140.7 6.6 %collective-permute-done.23 = bf16[384,768]{1,0:T(8,128)(2,1)} collective-permute-done((bf16[384,768]{1,0:T(8,128)(2,1)}, bf16[384,768]{1,0:T(8,128)(2,1)}, u32[]{:S(2)}, u32[]{:S(2)}) %collective-permute-start.23) | collective-permute-done | bytes 589856 | tf_op jit(solution)/shard_map/ppermute | solution.py:38
  147.3 1.6 add_convert_fusion
  149.1 2.1 %collective-permute-start.25 = (bf16[192,768]{1,0:T(8,128)(2,1)S(1)}, bf16[192,768]{1,0:T(8,128)(2,1)S(1)}, u32[]{:S(2)}, u32[]{:S(2)}) collective-permute-start(bf16[192,768]{1,0:T(8,128)(2,1)S(1)} %get-tuple-element.33), channel_id=1, source_target_pairs={{0,4},{4,0},{8,12},{12,8},{16,20},{20,16},{24,28},{28,24},{32,36},... | collective-permute-start | bytes 884744 | tf_op jit(solution)/shard_map/ppermute | solution.py:38
  151.1 4.3 %collective-permute-start.26 = (bf16[192,768]{1,0:T(8,128)(2,1)S(1)}, bf16[192,768]{1,0:T(8,128)(2,1)S(1)}, u32[]{:S(2)}, u32[]{:S(2)}) collective-permute-start(bf16[192,768]{1,0:T(8,128)(2,1)S(1)} %get-tuple-element.31), channel_id=1, source_target_pairs={{4,8},{8,4},{12,16},{16,12},{20,24},{24,20},{28,32},{32,28},{36,40... | collective-permute-start | bytes 884744 | tf_op jit(solution)/shard_map/ppermute | solution.py:38
  155.5 1.8 shard_map.143
  157.4 8.3 %collective-permute-done.26.in_b = bf16[192,768]{1,0:T(8,128)(2,1)S(1)} collective-permute-done((bf16[192,768]{1,0:T(8,128)(2,1)S(1)}, bf16[192,768]{1,0:T(8,128)(2,1)S(1)}, u32[]{:S(2)}, u32[]{:S(2)}) %collective-permute-start.26) | collective-permute-done | bytes 294944 | tf_op jit(solution)/shard_map/ppermute | solution.py:38
  165.7 1.8 shard_map.144
  167.6 10.5 %collective-permute-start.22 = (bf16[192,384]{1,0:T(8,128)(2,1)S(1)}, bf16[192,384]{1,0:T(8,128)(2,1)S(1)}, u32[]{:S(2)}, u32[]{:S(2)}) collective-permute-start(bf16[192,384]{1,0:T(8,128)(2,1)S(1)} %get-tuple-element.53), channel_id=1, source_target_pairs={{0,3},{1,0},{2,1},{3,2},{4,7},{5,4},{6,5},{7,6},{8,11},{9,8},{10,9... | collective-permute-start | bytes 442376 | tf_op jit(solution)/shard_map/ppermute | solution.py:198
  178.1 4.7 %collective-permute-start.21 = (bf16[192,384]{1,0:T(8,128)(2,1)S(1)}, bf16[192,384]{1,0:T(8,128)(2,1)S(1)}, u32[]{:S(2)}, u32[]{:S(2)}) collective-permute-start(bf16[192,384]{1,0:T(8,128)(2,1)S(1)} %get-tuple-element.52), channel_id=1, source_target_pairs={{0,2},{1,3},{2,0},{3,1},{4,6},{5,7},{6,4},{7,5},{8,10},{9,11},{10,... | collective-permute-start | bytes 442376 | tf_op jit(solution)/shard_map/ppermute | solution.py:198
  182.8 3.4 %collective-permute-start.20 = (bf16[192,384]{1,0:T(8,128)(2,1)S(1)}, bf16[192,384]{1,0:T(8,128)(2,1)S(1)}, u32[]{:S(2)}, u32[]{:S(2)}) collective-permute-start(bf16[192,384]{1,0:T(8,128)(2,1)S(1)} %get-tuple-element.54), channel_id=1, source_target_pairs={{0,1},{1,2},{2,3},{3,0},{4,5},{5,6},{6,7},{7,4},{8,9},{9,10},{10,1... | collective-permute-start | bytes 442376 | tf_op jit(solution)/shard_map/ppermute | solution.py:198
  186.2 3.7 %collective-permute-start.29 = (bf16[192,384]{1,0:T(8,128)(2,1)S(1)}, bf16[192,384]{1,0:T(8,128)(2,1)S(1)}, u32[]{:S(2)}, u32[]{:S(2)}) collective-permute-start(bf16[192,384]{1,0:T(8,128)(2,1)S(1)} %get-tuple-element.29), channel_id=1, source_target_pairs={{0,3},{1,0},{2,1},{3,2},{4,7},{5,4},{6,5},{7,6},{8,11},{9,8},{10,9... | collective-permute-start | bytes 442376 | tf_op jit(solution)/shard_map/ppermute | solution.py:198
  190.0 1.9 collective-permute-start.28
  191.9 2.2 %collective-permute-start.27 = (bf16[192,384]{1,0:T(8,128)(2,1)S(1)}, bf16[192,384]{1,0:T(8,128)(2,1)S(1)}, u32[]{:S(2)}, u32[]{:S(2)}) collective-permute-start(bf16[192,384]{1,0:T(8,128)(2,1)S(1)} %get-tuple-element.28), channel_id=1, source_target_pairs={{0,1},{1,2},{2,3},{3,0},{4,5},{5,6},{6,7},{7,4},{8,9},{9,10},{10,1... | collective-permute-start | bytes 442376 | tf_op jit(solution)/shard_map/ppermute | solution.py:198
  194.1 3.2 %collective-permute-done.21 = bf16[192,384]{1,0:T(8,128)(2,1)S(1)} collective-permute-done((bf16[192,384]{1,0:T(8,128)(2,1)S(1)}, bf16[192,384]{1,0:T(8,128)(2,1)S(1)}, u32[]{:S(2)}, u32[]{:S(2)}) %collective-permute-start.21) | collective-permute-done | bytes 147488 | tf_op jit(solution)/shard_map/ppermute | solution.py:198
  197.3 1.7 fusion.15
  199.0 3.0 %collective-permute-done.28 = bf16[192,384]{1,0:T(8,128)(2,1)S(1)} collective-permute-done((bf16[192,384]{1,0:T(8,128)(2,1)S(1)}, bf16[192,384]{1,0:T(8,128)(2,1)S(1)}, u32[]{:S(2)}, u32[]{:S(2)}) %collective-permute-start.28) | collective-permute-done | bytes 147488 | tf_op jit(solution)/shard_map/ppermute | solution.py:198
  202.0 0.7 fusion.12
  (108 shorter events, 2.6 us)
Async XLA Ops:
  0.6 90.6 %copy-start = (s32[128,2]{0,1:T(2,128)S(1)}, s32[128,2]{0,1:T(2,128)}, u32[]{:S(2)}) copy-start(s32[128,2]{0,1:T(2,128)} %param.22) | copy-start | bytes 3076
  1.4 13.5 %collective-permute-start = (bf16[14,1536]{1,0:T(8,128)(2,1)S(1)}, bf16[14,1536]{1,0:T(8,128)(2,1)S(1)}, u32[]{:S(2)}, u32[]{:S(2)}) collective-permute-start(bf16[14,1536]{1,0:T(8,128)(2,1)S(1)} %pad_maximum_fusion.7), channel_id=1, source_target_pairs={{0,32},{4,36},{8,40},{12,44},{16,48},{20,52},{24,56},{28,60},{32,0... | collective-permute-start | bytes 129032 | tf_op jit(solution)/shard_map/ppermute | solution.py:38
  10.5 4.5 %copy-start.21 = (s32[1536]{0:T(1024)}, s32[1536]{0:T(1024)S(1)}, u32[]{:S(2)}) copy-start(s32[1536]{0:T(1024)S(1)} %fusion.21) | copy-start | bytes 18436
  10.5 4.5 %copy-start.16 = (bf16[12,384]{1,0:T(8,128)(2,1)S(1)}, bf16[12,384]{1,0:T(8,128)(2,1)}, u32[]{:S(2)}) copy-start(bf16[12,384]{1,0:T(8,128)(2,1)} %param.18) | copy-start | bytes 27652
  10.5 4.4 %copy-start.17 = (bf16[12,384]{1,0:T(8,128)(2,1)S(1)}, bf16[12,384]{1,0:T(8,128)(2,1)}, u32[]{:S(2)}) copy-start(bf16[12,384]{1,0:T(8,128)(2,1)} %param.15) | copy-start | bytes 27652
  10.5 4.4 %copy-start.18 = (bf16[12,384]{1,0:T(8,128)(2,1)S(1)}, bf16[12,384]{1,0:T(8,128)(2,1)}, u32[]{:S(2)}) copy-start(bf16[12,384]{1,0:T(8,128)(2,1)} %param.17) | copy-start | bytes 27652
  10.5 4.4 %copy-start.19 = (bf16[12,384]{1,0:T(8,128)(2,1)S(1)}, bf16[12,384]{1,0:T(8,128)(2,1)}, u32[]{:S(2)}) copy-start(bf16[12,384]{1,0:T(8,128)(2,1)} %param.16) | copy-start | bytes 27652
  10.5 4.4 %copy-start.20 = (bf16[2,1536]{1,0:T(2,128)(2,1)S(1)}, bf16[2,1536]{1,0:T(2,128)(2,1)}, u32[]{:S(2)}) copy-start(bf16[2,1536]{1,0:T(2,128)(2,1)} %param.14) | copy-start | bytes 18436
  15.0 17.0 %collective-permute-start.1 = (bf16[2,14,1536]{2,1,0:T(8,128)(2,1)S(1)}, bf16[2,14,1536]{2,1,0:T(8,128)(2,1)S(1)}, u32[]{:S(2)}, u32[]{:S(2)}) collective-permute-start(bf16[2,14,1536]{2,1,0:T(8,128)(2,1)S(1)} %pad_maximum_fusion.5), channel_id=1, source_target_pairs={{0,96},{4,100},{8,104},{12,108},{16,112},{20,116},{24,120},{28,124... | collective-permute-start | bytes 258056 | tf_op jit(solution)/shard_map/ppermute | solution.py:38
  32.1 16.4 %collective-permute-start.9 = (bf16[48,768]{1,0:T(8,128)(2,1)S(1)}, bf16[48,768]{1,0:T(8,128)(2,1)S(1)}, u32[]{:S(2)}, u32[]{:S(2)}) collective-permute-start(bf16[48,768]{1,0:T(8,128)(2,1)S(1)} %get-tuple-element.41), channel_id=1, source_target_pairs={{0,24},{4,28},{8,0},{12,4},{16,8},{20,12},{24,16},{28,20},{32,56},... | collective-permute-start | bytes 221192 | tf_op jit(solution)/shard_map/ppermute | solution.py:38
  34.5 17.1 %collective-permute-start.10 = (bf16[48,768]{1,0:T(8,128)(2,1)S(1)}, bf16[48,768]{1,0:T(8,128)(2,1)S(1)}, u32[]{:S(2)}, u32[]{:S(2)}) collective-permute-start(bf16[48,768]{1,0:T(8,128)(2,1)S(1)} %get-tuple-element.41), channel_id=1, source_target_pairs={{0,16},{4,20},{8,24},{12,28},{16,0},{20,4},{24,8},{28,12},{32,48},... | collective-permute-start | bytes 221192 | tf_op jit(solution)/shard_map/ppermute | solution.py:38
  37.1 14.5 %collective-permute-start.11 = (bf16[48,768]{1,0:T(8,128)(2,1)S(1)}, bf16[48,768]{1,0:T(8,128)(2,1)S(1)}, u32[]{:S(2)}, u32[]{:S(2)}) collective-permute-start(bf16[48,768]{1,0:T(8,128)(2,1)S(1)} %get-tuple-element.41), channel_id=1, source_target_pairs={{0,8},{4,12},{8,16},{12,20},{16,24},{20,28},{24,0},{28,4},{32,40},... | collective-permute-start | bytes 221192 | tf_op jit(solution)/shard_map/ppermute | solution.py:38
  41.0 16.6 %collective-permute-start.4 = (bf16[64,768]{1,0:T(8,128)(2,1)S(1)}, bf16[64,768]{1,0:T(8,128)(2,1)S(1)}, u32[]{:S(2)}, u32[]{:S(2)}) collective-permute-start(bf16[64,768]{1,0:T(8,128)(2,1)S(1)} %get-tuple-element.45), channel_id=1, source_target_pairs={{0,128},{4,132},{8,136},{12,140},{16,144},{20,148},{24,152},{28,15... | collective-permute-start | bytes 294920 | tf_op jit(solution)/shard_map/ppermute | solution.py:38
  44.1 15.4 %collective-permute-start.3 = (bf16[64,768]{1,0:T(8,128)(2,1)S(1)}, bf16[64,768]{1,0:T(8,128)(2,1)S(1)}, u32[]{:S(2)}, u32[]{:S(2)}) collective-permute-start(bf16[64,768]{1,0:T(8,128)(2,1)S(1)} %get-tuple-element.45), channel_id=1, source_target_pairs={{0,256},{4,260},{8,264},{12,268},{16,272},{20,276},{24,280},{28,28... | collective-permute-start | bytes 294920 | tf_op jit(solution)/shard_map/ppermute | solution.py:38
  48.5 11.1 %collective-permute-start.2 = (bf16[64,768]{1,0:T(8,128)(2,1)S(1)}, bf16[64,768]{1,0:T(8,128)(2,1)S(1)}, u32[]{:S(2)}, u32[]{:S(2)}) collective-permute-start(bf16[64,768]{1,0:T(8,128)(2,1)S(1)} %get-tuple-element.45), channel_id=1, source_target_pairs={{0,384},{4,388},{8,392},{12,396},{16,400},{20,404},{24,408},{28,41... | collective-permute-start | bytes 294920 | tf_op jit(solution)/shard_map/ppermute | solution.py:38
  51.6 14.8 %collective-permute-start.12 = (bf16[192,768]{1,0:T(8,128)(2,1)S(1)}, bf16[192,768]{1,0:T(8,128)(2,1)S(1)}, u32[]{:S(2)}, u32[]{:S(2)}) collective-permute-start(bf16[192,768]{1,0:T(8,128)(2,1)S(1)} %pad_maximum_fusion.3), channel_id=1, source_target_pairs={{0,384},{4,388},{8,392},{12,396},{16,400},{20,404},{24,408},{28,41... | collective-permute-start | bytes 884744 | tf_op jit(solution)/shard_map/ppermute | solution.py:38
  53.5 15.6 %collective-permute-start.13 = (bf16[192,768]{1,0:T(8,128)(2,1)S(1)}, bf16[192,768]{1,0:T(8,128)(2,1)S(1)}, u32[]{:S(2)}, u32[]{:S(2)}) collective-permute-start(bf16[192,768]{1,0:T(8,128)(2,1)S(1)} %pad_maximum_fusion.3), channel_id=1, source_target_pairs={{0,256},{4,260},{8,264},{12,268},{16,272},{20,276},{24,280},{28,28... | collective-permute-start | bytes 884744 | tf_op jit(solution)/shard_map/ppermute | solution.py:38
  57.6 12.9 %collective-permute-start.14 = (bf16[192,768]{1,0:T(8,128)(2,1)S(1)}, bf16[192,768]{1,0:T(8,128)(2,1)S(1)}, u32[]{:S(2)}, u32[]{:S(2)}) collective-permute-start(bf16[192,768]{1,0:T(8,128)(2,1)S(1)} %pad_maximum_fusion.3), channel_id=1, source_target_pairs={{0,128},{4,132},{8,136},{12,140},{16,144},{20,148},{24,152},{28,15... | collective-permute-start | bytes 884744 | tf_op jit(solution)/shard_map/ppermute | solution.py:38
  60.4 15.0 %copy-start.25 = (s32[256]{0:T(256)S(1)}, s32[256]{0:T(256)}, u32[]{:S(2)}) copy-start(s32[256]{0:T(256)} %param.21) | copy-start | bytes 3076
  60.4 15.2 %collective-permute-start.7 = (bf16[4,64,768]{2,1,0:T(8,128)(2,1)}, bf16[4,64,768]{2,1,0:T(8,128)(2,1)S(1)}, u32[]{:S(2)}, u32[]{:S(2)}) collective-permute-start(bf16[4,64,768]{2,1,0:T(8,128)(2,1)} %get-tuple-element.40), channel_id=1, source_target_pairs={{0,8},{4,12},{8,16},{12,20},{16,24},{20,28},{24,0},{28,4},{32,40},... | collective-permute-start | bytes 1179656 | tf_op jit(solution)/shard_map/ppermute | solution.py:38
  63.1 12.4 %collective-permute-start.6 = (bf16[4,64,768]{2,1,0:T(8,128)(2,1)}, bf16[4,64,768]{2,1,0:T(8,128)(2,1)S(1)}, u32[]{:S(2)}, u32[]{:S(2)}) collective-permute-start(bf16[4,64,768]{2,1,0:T(8,128)(2,1)} %get-tuple-element.40), channel_id=1, source_target_pairs={{0,16},{4,20},{8,24},{12,28},{16,0},{20,4},{24,8},{28,12},{32,48},... | collective-permute-start | bytes 1179656 | tf_op jit(solution)/shard_map/ppermute | solution.py:38
  66.4 18.5 %collective-permute-start.5 = (bf16[4,64,768]{2,1,0:T(8,128)(2,1)}, bf16[4,64,768]{2,1,0:T(8,128)(2,1)}, u32[]{:S(2)}, u32[]{:S(2)}) collective-permute-start(bf16[4,64,768]{2,1,0:T(8,128)(2,1)} %get-tuple-element.40), channel_id=1, source_target_pairs={{0,24},{4,28},{8,0},{12,4},{16,8},{20,12},{24,16},{28,20},{32,56},... | collective-permute-start | bytes 1179656 | tf_op jit(solution)/shard_map/ppermute | solution.py:38
  70.6 21.7 %collective-permute-start.15 = (bf16[768,768]{1,0:T(8,128)(2,1)S(1)}, bf16[768,768]{1,0:T(8,128)(2,1)S(1)}, u32[]{:S(2)}, u32[]{:S(2)}) collective-permute-start(bf16[768,768]{1,0:T(8,128)(2,1)S(1)} %constant_dynamic-update-slice_fusion.ao.wo), channel_id=1, source_target_pairs={{0,4},{4,0},{8,12},{12,8},{16,20},{20,16},{24,28},{28,24},{32,36},... | collective-permute-start | bytes 3538952 | tf_op jit(solution)/shard_map/ppermute | solution.py:38
  84.9 6.4 %copy-start.23 = (f32[384]{0:T(512)S(1)}, f32[384]{0:T(512)}, u32[]{:S(2)}) copy-start(f32[384]{0:T(512)} %param.20) | copy-start | bytes 4612
  84.9 6.4 %copy-start.15 = (bf16[384,1536]{1,0:T(8,128)(2,1)S(1)}, bf16[384,1536]{1,0:T(8,128)(2,1)}, u32[]{:S(2)}) copy-start(bf16[384,1536]{1,0:T(8,128)(2,1)} %fusion.4) | copy-start | bytes 3538948
  87.4 30.2 %collective-permute-start.8 = (bf16[4,4,64,768]{3,2,0,1:T(8,128)(2,1)}, bf16[4,4,64,768]{3,2,0,1:T(8,128)(2,1)}, u32[]{:S(2)}, u32[]{:S(2)}) collective-permute-start(bf16[4,4,64,768]{3,2,0,1:T(8,128)(2,1)} %maximum_bitcast_fusion), channel_id=1, source_target_pairs={{0,4},{4,0},{8,12},{12,8},{16,20},{20,16},{24,28},{28,24},{32,36},... | collective-permute-start | bytes 4718600 | tf_op jit(solution)/shard_map/ppermute | solution.py:38
  92.2 0.8 copy-start.5
  92.3 1.2 copy-start.1
  92.3 6.3 %copy-start.24 = (f32[384]{0:T(512)S(1)}, f32[384]{0:T(512)}, u32[]{:S(2)}) copy-start(f32[384]{0:T(512)} %param.19) | copy-start | bytes 4612
  93.4 0.7 copy-start.9
  94.2 8.5 %collective-permute-start.16 = (bf16[192,768]{1,0:T(8,128)(2,1)S(1)}, bf16[192,768]{1,0:T(8,128)(2,1)}, u32[]{:S(2)}, u32[]{:S(2)}) collective-permute-start(bf16[192,768]{1,0:T(8,128)(2,1)S(1)} %get-tuple-element.17), channel_id=1, source_target_pairs={{0,4},{4,0},{8,12},{12,8},{16,20},{20,16},{24,28},{28,24},{32,36},... | collective-permute-start | bytes 884744 | tf_op jit(solution)/shard_map/ppermute | solution.py:38
  96.1 16.9 %collective-permute-start.17 = (bf16[192,768]{1,0:T(8,128)(2,1)S(1)}, bf16[192,768]{1,0:T(8,128)(2,1)}, u32[]{:S(2)}, u32[]{:S(2)}) collective-permute-start(bf16[192,768]{1,0:T(8,128)(2,1)S(1)} %get-tuple-element.17), channel_id=1, source_target_pairs={{4,8},{8,4},{12,16},{16,12},{20,24},{24,20},{28,32},{32,28},{36,40... | collective-permute-start | bytes 884744 | tf_op jit(solution)/shard_map/ppermute | solution.py:38
  114.1 11.7 %collective-permute-start.18 = (bf16[384,768]{1,0:T(8,128)(2,1)S(1)}, bf16[384,768]{1,0:T(8,128)(2,1)S(1)}, u32[]{:S(2)}, u32[]{:S(2)}) collective-permute-start(bf16[384,768]{1,0:T(8,128)(2,1)S(1)} %pad_maximum_fusion.1.pair), channel_id=1, source_target_pairs={{0,128},{4,132},{8,136},{12,140},{16,144},{20,148},{24,152},{28,15... | collective-permute-start | bytes 1769480 | tf_op jit(solution)/shard_map/ppermute | solution.py:38
  116.7 9.0 %collective-permute-start.19 = (bf16[384,768]{1,0:T(8,128)(2,1)S(1)}, bf16[384,768]{1,0:T(8,128)(2,1)S(1)}, u32[]{:S(2)}, u32[]{:S(2)}) collective-permute-start(bf16[384,768]{1,0:T(8,128)(2,1)S(1)} %pad_maximum_fusion.1.pair), channel_id=1, source_target_pairs={{128,256},{132,260},{136,264},{140,268},{144,272},{148,276},{152,2... | collective-permute-start | bytes 1769480 | tf_op jit(solution)/shard_map/ppermute | solution.py:38
  121.5 0.7 copy-start.22
  122.2 2.0 %copy-start.2 = (bf16[768,768]{1,0:T(8,128)(2,1)S(1)}, bf16[768,768]{1,0:T(8,128)(2,1)}, u32[]{:S(2)}) copy-start(bf16[768,768]{1,0:T(8,128)(2,1)} %copy-done.1) | copy-start | bytes 3538948
  122.2 2.1 %copy-start.4 = (bf16[192,1536]{1,0:T(8,128)(2,1)S(1)}, bf16[192,1536]{1,0:T(8,128)(2,1)}, u32[]{:S(2)}) copy-start(bf16[192,1536]{1,0:T(8,128)(2,1)} %get-tuple-element.26.gp) | copy-start | bytes 1769476
  122.2 2.1 %copy-start.6 = (bf16[192,1536]{1,0:T(8,128)(2,1)S(1)}, bf16[192,1536]{1,0:T(8,128)(2,1)}, u32[]{:S(2)}) copy-start(bf16[192,1536]{1,0:T(8,128)(2,1)} %copy-done.5) | copy-start | bytes 1769476
  129.5 0.8 copy-start.8
  130.3 1.1 copy-start.11
  130.3 1.1 copy-start.13
  131.5 9.2 %collective-permute-start.24 = (bf16[384,768]{1,0:T(8,128)(2,1)}, bf16[384,768]{1,0:T(8,128)(2,1)}, u32[]{:S(2)}, u32[]{:S(2)}) collective-permute-start(bf16[384,768]{1,0:T(8,128)(2,1)} %get-tuple-element.35), channel_id=1, source_target_pairs={{128,256},{132,260},{136,264},{140,268},{144,272},{148,276},{152,2... | collective-permute-start | bytes 1769480 | tf_op jit(solution)/shard_map/ppermute | solution.py:38
  132.9 14.4 %collective-permute-start.23 = (bf16[384,768]{1,0:T(8,128)(2,1)}, bf16[384,768]{1,0:T(8,128)(2,1)}, u32[]{:S(2)}, u32[]{:S(2)}) collective-permute-start(bf16[384,768]{1,0:T(8,128)(2,1)} %get-tuple-element.34), channel_id=1, source_target_pairs={{0,128},{4,132},{8,136},{12,140},{16,144},{20,148},{24,152},{28,15... | collective-permute-start | bytes 1769480 | tf_op jit(solution)/shard_map/ppermute | solution.py:38
  149.0 6.5 %copy-start.12 = (bf16[192,384]{1,0:T(8,128)(2,1)S(1)}, bf16[192,384]{1,0:T(8,128)(2,1)}, u32[]{:S(2)}) copy-start(bf16[192,384]{1,0:T(8,128)(2,1)} %copy-done.11) | copy-start | bytes 442372
  149.0 6.5 %copy-start.14 = (bf16[192,384]{1,0:T(8,128)(2,1)S(1)}, bf16[192,384]{1,0:T(8,128)(2,1)}, u32[]{:S(2)}) copy-start(bf16[192,384]{1,0:T(8,128)(2,1)} %copy-done.13) | copy-start | bytes 442372
  149.1 8.3 %collective-permute-start.25 = (bf16[192,768]{1,0:T(8,128)(2,1)S(1)}, bf16[192,768]{1,0:T(8,128)(2,1)S(1)}, u32[]{:S(2)}, u32[]{:S(2)}) collective-permute-start(bf16[192,768]{1,0:T(8,128)(2,1)S(1)} %get-tuple-element.33), channel_id=1, source_target_pairs={{0,4},{4,0},{8,12},{12,8},{16,20},{20,16},{24,28},{28,24},{32,36},... | collective-permute-start | bytes 884744 | tf_op jit(solution)/shard_map/ppermute | solution.py:38
  151.1 14.6 %collective-permute-start.26 = (bf16[192,768]{1,0:T(8,128)(2,1)S(1)}, bf16[192,768]{1,0:T(8,128)(2,1)S(1)}, u32[]{:S(2)}, u32[]{:S(2)}) collective-permute-start(bf16[192,768]{1,0:T(8,128)(2,1)S(1)} %get-tuple-element.31), channel_id=1, source_target_pairs={{4,8},{8,4},{12,16},{16,12},{20,24},{24,20},{28,32},{32,28},{36,40... | collective-permute-start | bytes 884744 | tf_op jit(solution)/shard_map/ppermute | solution.py:38
  155.5 10.2 %copy-start.3 = (bf16[768,768]{1,0:T(8,128)(2,1)S(1)}, bf16[768,768]{1,0:T(8,128)(2,1)}, u32[]{:S(2)}) copy-start(bf16[768,768]{1,0:T(8,128)(2,1)} %copy-done.1) | copy-start | bytes 3538948
  155.5 10.2 %copy-start.10 = (f32[192,384]{1,0:T(8,128)S(1)}, f32[192,384]{1,0:T(8,128)}, u32[]{:S(2)}) copy-start(f32[192,384]{1,0:T(8,128)} %copy-done.9) | copy-start | bytes 884740
  157.4 10.1 %copy-start.7 = (bf16[4,192,384]{2,1,0:T(8,128)(2,1)}, bf16[4,192,384]{2,1,0:T(8,128)(2,1)S(1)}, u32[]{:S(2)}) copy-start(bf16[4,192,384]{2,1,0:T(8,128)(2,1)S(1)} %get-tuple-element.21) | copy-start | bytes 1769476
  167.6 24.3 %collective-permute-start.22 = (bf16[192,384]{1,0:T(8,128)(2,1)S(1)}, bf16[192,384]{1,0:T(8,128)(2,1)S(1)}, u32[]{:S(2)}, u32[]{:S(2)}) collective-permute-start(bf16[192,384]{1,0:T(8,128)(2,1)S(1)} %get-tuple-element.53), channel_id=1, source_target_pairs={{0,3},{1,0},{2,1},{3,2},{4,7},{5,4},{6,5},{7,6},{8,11},{9,8},{10,9... | collective-permute-start | bytes 442376 | tf_op jit(solution)/shard_map/ppermute | solution.py:198
  178.1 19.2 %collective-permute-start.21 = (bf16[192,384]{1,0:T(8,128)(2,1)S(1)}, bf16[192,384]{1,0:T(8,128)(2,1)S(1)}, u32[]{:S(2)}, u32[]{:S(2)}) collective-permute-start(bf16[192,384]{1,0:T(8,128)(2,1)S(1)} %get-tuple-element.52), channel_id=1, source_target_pairs={{0,2},{1,3},{2,0},{3,1},{4,6},{5,7},{6,4},{7,5},{8,10},{9,11},{10,... | collective-permute-start | bytes 442376 | tf_op jit(solution)/shard_map/ppermute | solution.py:198
  182.8 14.5 %collective-permute-start.20 = (bf16[192,384]{1,0:T(8,128)(2,1)S(1)}, bf16[192,384]{1,0:T(8,128)(2,1)S(1)}, u32[]{:S(2)}, u32[]{:S(2)}) collective-permute-start(bf16[192,384]{1,0:T(8,128)(2,1)S(1)} %get-tuple-element.54), channel_id=1, source_target_pairs={{0,1},{1,2},{2,3},{3,0},{4,5},{5,6},{6,7},{7,4},{8,9},{9,10},{10,1... | collective-permute-start | bytes 442376 | tf_op jit(solution)/shard_map/ppermute | solution.py:198
  186.2 12.8 %collective-permute-start.29 = (bf16[192,384]{1,0:T(8,128)(2,1)S(1)}, bf16[192,384]{1,0:T(8,128)(2,1)S(1)}, u32[]{:S(2)}, u32[]{:S(2)}) collective-permute-start(bf16[192,384]{1,0:T(8,128)(2,1)S(1)} %get-tuple-element.29), channel_id=1, source_target_pairs={{0,3},{1,0},{2,1},{3,2},{4,7},{5,4},{6,5},{7,6},{8,11},{9,8},{10,9... | collective-permute-start | bytes 442376 | tf_op jit(solution)/shard_map/ppermute | solution.py:198
  190.0 12.0 %collective-permute-start.28 = (bf16[192,384]{1,0:T(8,128)(2,1)S(1)}, bf16[192,384]{1,0:T(8,128)(2,1)S(1)}, u32[]{:S(2)}, u32[]{:S(2)}) collective-permute-start(bf16[192,384]{1,0:T(8,128)(2,1)S(1)} %get-tuple-element.30), channel_id=1, source_target_pairs={{0,2},{1,3},{2,0},{3,1},{4,6},{5,7},{6,4},{7,5},{8,10},{9,11},{10,... | collective-permute-start | bytes 442376 | tf_op jit(solution)/shard_map/ppermute | solution.py:198
  191.9 10.1 %collective-permute-start.27 = (bf16[192,384]{1,0:T(8,128)(2,1)S(1)}, bf16[192,384]{1,0:T(8,128)(2,1)S(1)}, u32[]{:S(2)}, u32[]{:S(2)}) collective-permute-start(bf16[192,384]{1,0:T(8,128)(2,1)S(1)} %get-tuple-element.28), channel_id=1, source_target_pairs={{0,1},{1,2},{2,3},{3,0},{4,5},{5,6},{6,7},{7,4},{8,9},{9,10},{10,1... | collective-permute-start | bytes 442376 | tf_op jit(solution)/shard_map/ppermute | solution.py:198

commit v2 on v1

v2 whole, which is shorter than its diff:
```python
import functools

import jax
import jax.numpy as jnp
from jax import lax
from jax.experimental import pallas as pl
from jax.experimental.pallas import tpu as pltpu
from jax.sharding import PartitionSpec as P

HD = 128
NH = 3
W = NH * HD
ROWS = 192
TEXT = 256
EPS = 1e-6
SCALE = HD**-0.5
BLOCK = 56
PART = 4 * BLOCK
F32 = jnp.float32
BF16 = jnp.bfloat16
NT = (((1,), (1,)), ((), ()))
TN = (((0,), (0,)), ((), ()))


def place_of(x, zh, y, core):
    return ((x * 4 + zh) * 4 + y) * 2 + core


def all_places():
    return [(x, z, y, c) for x in range(4) for z in range(4) for y in range(4) for c in range(2)]


def seq_move(value, target):
    pairs = []
    for at in all_places():
        to = target(*at)
        if to is not None:
            pairs.append((place_of(*at), place_of(*to)))
    return lax.ppermute(value, "seq", pairs)


def core_mate(value):
    return seq_move(value, lambda x, z, y, c: (x, z, y, 1 - c))


def next_chip(value):
    def target(x, z, y, c):
        col = (z * 4 + y) * 2 + c
        col = col + 1 if c == 1 else col - 1
        if not 0 <= col < 32:
            return None
        return (x, col // 8, col // 2 % 4, col % 2)

    return seq_move(value, target)


def row_even(value):
    return seq_move(value, lambda x, z, y, c: (x ^ 1, z, y, c))


def row_odd(value):
    return seq_move(value, lambda x, z, y, c: (3 - x, z, y, c) if x in (1, 2) else None)


def give_all(value, groups):
    copies = jnp.broadcast_to(value[None], (len(groups[0]),) + value.shape)
    return lax.all_to_all(copies, "seq", 0, 0, axis_index_groups=groups)


def over_zh(value):
    four = range(4)
    return give_all(
        value,
        [[place_of(x, z, y, c) for z in four] for x in four for y in four for c in range(2)],
    )


def over_xy(value):
    four = range(4)
    return give_all(
        value,
        [[place_of(x, z, y, c) for x in four for y in four] for z in four for c in range(2)],
    )


def dot(a, b, dims=(((1,), (0,)), ((), ()))):
    return lax.dot_general(a, b, dims, preferred_element_type=F32)


def norm_rows(a, gain):
    r = lax.rsqrt(jnp.mean(a * a, axis=-1, keepdims=True) + EPS)
    return a * r * gain


def norm_pull(a, gain, dy):
    r = lax.rsqrt(jnp.mean(a * a, axis=-1, keepdims=True) + EPS)
    t = dy * gain
    return r * t - a * (r * r * r * jnp.mean(t * a, axis=-1, keepdims=True))


def head(h):
    return slice(h * HD, (h + 1) * HD)


def val(h):
    return slice(W + h * HD, W + (h + 1) * HD)


def call(kernel, outs, scratch=(), mib=32, flops=10**9):
    return pl.pallas_call(
        kernel,
        out_shape=outs,
        scratch_shapes=scratch,
        compiler_params=pltpu.CompilerParams(vmem_limit_bytes=mib * 2**20),
        cost_estimate=pl.CostEstimate(flops=flops, bytes_accessed=8 * 10**6, transcendentals=0),
    )


def shape(dims, dtype):
    return jax.ShapeDtypeStruct(dims, dtype)


def project(rows, pick, w, cols):
    acc = None
    for j in range(4):
        xs = dot(rows[:, j * W : (j + 1) * W], pick[...]).astype(BF16)
        term = dot(xs, w[j * PART : (j + 1) * PART, cols])
        acc = term if acc is None else acc + term
    return acc


def kv_own_kernel(x0, x1, x2, pick, w, acc):
    for n, rows in enumerate((x0, x1, x2)):
        acc[n] = project(rows, pick, w, slice(0, 2 * W))


def kv_kernel(x0, x1, x2, pick, w, acc, gain, kv, kraw):
    for n, rows in enumerate((x0, x1, x2)):
        full = acc[n] + project(rows, pick, w, slice(0, 2 * W))
        if n == 0:
            kraw[...] = full[:, :W]
        for h in range(NH):
            kv[n, :, head(h)] = norm_rows(full[:, head(h)], gain[:, head(h)]).astype(BF16)
        kv[n, :, W:] = full[:, W:].astype(BF16)


def q_kernel(x, g, t, pick_o, pick_t, wo, wt, q_gain, k_gain, qraw, qn, d_att, tkv):
    q = project(x, pick_o, wo, slice(2 * W, 3 * W)) + project(x, pick_t, wt, slice(2 * W, 3 * W))
    qraw[...] = q
    for h in range(NH):
        qn[:, head(h)] = norm_rows(q[:, head(h)], q_gain[:, head(h)]).astype(BF16)
    last = slice(3 * W, 4 * W)
    d_att[...] = (project(g, pick_o, wo, last) + project(g, pick_t, wt, last)).astype(BF16)
    both = slice(0, 2 * W)
    s = project(t, pick_o, wo, both) + project(t, pick_t, wt, both)
    for h in range(NH):
        tkv[:, head(h)] = norm_rows(s[:, head(h)], k_gain[:, head(h)]).astype(BF16)
    tkv[:, W:] = s[:, W:].astype(BF16)


def attend_kernel(
    qn, d_att, qraw, q_gain, own, far, side, tkv, bias, att, dq, near_t, far_t, keys
):
    n = 4 * ROWS
    keys[:ROWS, :] = own[...]
    keys[ROWS : 2 * ROWS, :] = far[...]
    keys[2 * ROWS : n, :] = side[...]
    keys[n:, :] = tkv[...]
    for h in range(NH):
        qh = qn[:, head(h)]
        dh = d_att[:, head(h)]
        kh = keys[:, head(h)]
        vh = keys[:, val(h)]
        s = dot(qh, kh, NT) * SCALE + bias[...]
        e = jnp.exp(s - jnp.max(s, axis=-1, keepdims=True))
        p = e * (1.0 / jnp.sum(e, axis=-1, keepdims=True))
        pb = p.astype(BF16)
        att[:, head(h)] = dot(pb, vh).astype(BF16)
        dp = dot(dh, vh, NT)
        ds = (p * (dp - jnp.sum(p * dp, axis=-1, keepdims=True))).astype(BF16)
        d_q = dot(ds, kh) * SCALE
        dq[:, head(h)] = norm_pull(qraw[:, head(h)], q_gain[:, head(h)], d_q).astype(BF16)
        kt = (dot(ds[:, :n], qh, TN) * SCALE).astype(BF16)
        vt = dot(pb[:, :n], dh, TN).astype(BF16)
        near_t[:, head(h)] = kt[: 2 * ROWS]
        far_t[:, head(h)] = kt[2 * ROWS :]
        near_t[:, val(h)] = vt[: 2 * ROWS]
        far_t[:, val(h)] = vt[2 * ROWS :]


def out_kernel(att, dq, wo, wt, pick_o, pick_t, out, gq):
    for j in range(4):
        rows = slice(j * PART, (j + 1) * PART)
        o = dot(att[...], wo[rows, 3 * W :], NT).astype(BF16)
        t = dot(att[...], wt[rows, 3 * W :], NT).astype(BF16)
        out[j] = (dot(o, pick_o[...], NT) + dot(t, pick_t[...], NT)).astype(BF16)
        gq[0, j] = dot(dq[...], wo[rows, 2 * W : 3 * W], NT)
        gq[1, j] = dot(dq[...], wt[rows, 2 * W : 3 * W], NT)


def grad_kernel(own, in_a, in_b, kraw, k_gain, gq, wo, wt, pick_o, pick_t, o0, o1, o2, o3, out, res):
    total = own[...] + in_a[...].astype(F32) + in_b[...].astype(F32)
    parts = [
        norm_pull(kraw[:, head(h)], k_gain[:, head(h)], total[:, head(h)]).astype(BF16)
        for h in range(NH)
    ]
    d = jnp.concatenate(parts + [total[:, W:].astype(BF16)], axis=1)
    for j in range(4):
        rows = slice(j * PART, (j + 1) * PART)
        o = (gq[0, j] + dot(d, wo[rows, : 2 * W], NT)).astype(BF16)
        t = (gq[1, j] + dot(d, wt[rows, : 2 * W], NT)).astype(BF16)
        out[j] = (dot(o, pick_o[...], NT) + dot(t, pick_t[...], NT)).astype(BF16)
    res[...] = (
        o0[...].astype(F32) + o1[...].astype(F32) + o2[...].astype(F32) + o3[...].astype(F32)
    ).astype(BF16)


def to_heads(blocks, me):
    def block(to):
        return lax.dynamic_index_in_dim(blocks, to % 4, 0, keepdims=False)

    parts = [block(me)]
    for by in (1, 2, 3):
        pairs = [(i, (i + by) % 4) for i in range(4)]
        parts.append(lax.ppermute(block(me + by), "heads", pairs))
    return parts


def f32_sum(*terms):
    total = terms[0].astype(F32)
    for term in terms[1:]:
        total = total + term.astype(F32)
    return total


def per_device(
    x_tiles, x_text, w_query, w_key, w_value, w_output, q_gain, k_gain, text_mask, windows, grad_out
):
    place = lax.axis_index("seq")
    me = lax.axis_index("heads")
    core, x, col = place % 2, place // 32, place % 32
    beside = jnp.clip(jnp.where(core == 1, place + 1, place - 1), 0, 127)

    def far_even(who):
        row = lax.dynamic_index_in_dim(windows[:, 0], who, 0, keepdims=False)
        return (row == x) == (x % 2 == 0)

    mine_even, mate_even, beside_even = far_even(place), far_even(place ^ 1), far_even(beside)
    first_col = lax.dynamic_index_in_dim(windows[:, 1], place, 0, keepdims=False)
    use_core = (first_col == col) == (core == 0)
    q_gain = q_gain[None, :]
    k_gain = k_gain[None, :]

    at = jnp.arange(PART, dtype=jnp.int32)
    inner = at % BLOCK
    feature = lax.broadcasted_iota(jnp.int32, (W, PART), 0)

    def pick(which):
        natural = ((inner // 12 * 4 + at // BLOCK) * 2 + which) * 12 + inner % 12
        hit = (feature == natural[None, :]) & (inner < 48)[None, :]
        return hit.astype(BF16)

    pick_o, pick_t = pick(core), pick(1 - core)
    t = jnp.arange(TEXT, dtype=jnp.int32)
    token = place_of(t // 32 % 4, t // 2 % 4, t // 8 % 4, (t // 128) ^ core) * 2 + t % 2
    valid = jnp.sum(jnp.where(t[:, None] == token[None, :], text_mask[:, None], 0), axis=0)
    bias = jnp.concatenate(
        [jnp.zeros((4 * ROWS,), F32), jnp.where(valid == 1, 0.0, -1e30).astype(F32)]
    )[None, :]

    x_even, x_odd = row_even(x_tiles), row_odd(x_tiles)
    mine = jnp.concatenate([w_key, w_value, w_query, w_output], axis=1)
    four = over_zh(jnp.concatenate([mine, x_text], axis=0))
    block = jnp.concatenate([four[:, :12].reshape(48, 1536), four[:, 12:].reshape(8, 1536)], axis=0)
    wo = over_xy(block).reshape(16 * BLOCK, 1536)
    wt = core_mate(wo)
    texts = jnp.stack([wo, wt]).reshape(2, 16, BLOCK, 1536)[:, :, 48:].reshape(TEXT, 1536)

    acc = call(kv_own_kernel, shape((3, ROWS, 768), F32))(x_tiles, x_even, x_odd, pick_o, wo)
    kv, kraw = call(kv_kernel, (shape((3, ROWS, 768), BF16), shape((ROWS, W), F32)))(
        x_tiles, x_even, x_odd, pick_t, wt, acc, k_gain
    )
    own, even, odd = kv[0], kv[1], kv[2]
    from_mate = core_mate(jnp.concatenate([own, jnp.where(mate_even, even, odd)]))
    from_next = next_chip(jnp.concatenate([own, jnp.where(beside_even, even, odd)]))
    far = jnp.where(mine_even, even, odd)
    qraw, qn, d_att, tkv = call(
        q_kernel,
        (
            shape((ROWS, W), F32),
            shape((ROWS, W), BF16),
            shape((ROWS, W), BF16),
            shape((TEXT, 768), BF16),
        ),
    )(x_tiles, grad_out, texts, pick_o, pick_t, wo, wt, q_gain, k_gain)
    side = jnp.where(use_core, from_mate, from_next)
    att, dq, near_t, side_t = call(
        attend_kernel,
        (
            shape((ROWS, W), BF16),
            shape((ROWS, W), BF16),
            shape((2 * ROWS, 768), BF16),
            shape((2 * ROWS, 768), BF16),
        ),
        [pltpu.VMEM((1024, 768), BF16)],
    )(qn, d_att, qraw, q_gain, own, far, side, tkv, bias)

    zero = jnp.zeros_like(side_t)
    mate_t = core_mate(jnp.where(use_core, side_t, zero))
    next_t = next_chip(jnp.where(use_core, zero, side_t))
    out, gq = call(out_kernel, (shape((4, ROWS, W), BF16), shape((2, 4, ROWS, PART), F32)))(
        att, dq, wo, wt, pick_o, pick_t
    )
    outs = to_heads(out, me)
    zero = jnp.zeros((ROWS, 768), BF16)
    far_terms = (
        (mine_even, near_t[ROWS:]),
        (mate_even, mate_t[ROWS:]),
        (beside_even, next_t[ROWS:]),
    )
    to_even = f32_sum(*[jnp.where(flag, term, zero) for flag, term in far_terms]).astype(BF16)
    to_odd = f32_sum(*[jnp.where(flag, zero, term) for flag, term in far_terms]).astype(BF16)
    got_even, got_odd = row_even(to_even), row_odd(to_odd)
    own_t = f32_sum(near_t[:ROWS], mate_t[:ROWS], next_t[:ROWS])
    grad, out_tiles = call(
        grad_kernel, (shape((4, ROWS, W), BF16), shape((ROWS, W), BF16))
    )(own_t, got_even, got_odd, kraw, k_gain, gq, wo, wt, pick_o, pick_t, *outs)
    grad_tiles = f32_sum(*to_heads(grad, me)).astype(BF16)
    return (out_tiles, grad_tiles)


def solution(mesh):
    in_specs = (
        P("seq", None),
        P("seq", None),
        P("seq", "heads"),
        P("seq", "heads"),
        P("seq", "heads"),
        P("seq", "heads"),
        P("heads"),
        P("heads"),
        P(),
        P(),
        P("seq", None),
    )
    out_specs = (P("seq", "heads"), P("seq", "heads"))
    return jax.shard_map(
        per_device, mesh=mesh, in_specs=in_specs, out_specs=out_specs, check_vma=False
    )
```

time: 204 us -> 232 us (1.14)
  blocking collectives: 0 us -> 63 us
  starting transfers between devices: 110 us -> 65.1 us
  Pallas kernels: 9.44 us -> 27.4 us
  waiting for transfers between devices: 50.3 us -> 59.7 us
  local copies, waits for them, and re-layouts: 10.9 us -> 2.79 us
  matrix products: 6.42 us -> 0 us
  other arithmetic: 12.1 us -> 8.91 us
    all_to_all x0 -> x2, blocking collectives: none -> 63 us  [give_all(): return lax.all_to_all(copies, 'seq', 0, 0, axis_index_groups=groups)]
    ppermute x24 -> x9, starting transfers between devices: 84.1 us -> 27.7 us  [seq_move(): return lax.ppermute(value, 'seq', pairs)]
    pallas_call x3 -> x4, Pallas kernels: 4.33 us -> 16.8 us  [the longest x1 4.82 us: per_device(): call(kv_kernel, (shape((3, ROWS, 768), BF16), shape((ROWS, W), F32)))]
    ppermute x6, starting transfers between devices: 26.4 us -> 37.5 us  [to_heads(): parts.append(lax.ppermute(block(me + by), 'heads', pairs))]
    ppermute x24 -> x9, waiting for transfers between devices: 44.1 us -> 50.6 us  [seq_move(): return lax.ppermute(value, 'seq', pairs)]
    dot_general x2 -> x0, matrix products: 6.42 us -> none  [dot(): return lax.dot_general(a, b, dims, preferred_element_type=F32)]
    pallas_call x1, Pallas kernels: 1.41 us -> 7 us  [per_device(): call(q_kernel, (shape((ROWS, W), F32), shape((ROWS, W), BF16), shape((ROW...]
    slice x9 -> x2, local copies, waits for them, and re-layouts: 5.1 us -> 0.03 us  [the longest x1 0.03 us: per_device(): four[:, 12:].reshape(8, 1536)]
  transfers between devices with their start and end apart: 30 -> 15, of which waited for: 8 -> 8; matrix products, arithmetic and copies ran while one was open for 11% -> 1% of each run, Pallas kernels for 2% -> 6%
where the time goes in v2:
time: 232 us; the launch traced here: 231 us
  starting transfers between devices  65.1 us (28%)
  blocking collectives  63 us (27%)
  waiting for transfers between devices  59.7 us (26%)
  Pallas kernels  27.4 us (12%)
  other arithmetic  8.91 us (4%)
  between operations  3.81 us (2%)
  local copies, waits for them, and re-layouts  2.79 us (1%)
    all_to_all x2, blocking collectives, give_all(): return lax.all_to_all(copies, 'seq', 0, 0, axis_index_groups=groups)  63 us
    ppermute x9, waiting for transfers between devices, seq_move(): return lax.ppermute(value, 'seq', pairs)  50.6 us
    ppermute x6, starting transfers between devices, to_heads(): parts.append(lax.ppermute(block(me + by), 'heads', pairs))  37.5 us
    ppermute x9, starting transfers between devices, seq_move(): return lax.ppermute(value, 'seq', pairs)  27.7 us
    ppermute x6, waiting for transfers between devices, to_heads(): parts.append(lax.ppermute(block(me + by), 'heads', pairs))  9.16 us
    pallas_call x1, Pallas kernels, per_device(): call(q_kernel, (shape((ROWS, W), F32), shape((ROWS, W), BF16), shape((ROW...  7 us
    pallas_call x1, Pallas kernels, per_device(): call(kv_kernel, (shape((3, ROWS, 768), BF16), shape((ROWS, W), F32)))  4.82 us
  transfers between devices with their start and end apart: 15, of which 8 were waited for; matrix products, arithmetic and copies ran while one was open for 1% of the time, Pallas kernels for 6%

profile of v2, /device:TPU:25, one launch (start us, length us, event | category | flops | bytes accessed | tf_op | source)
XLA Modules:
  0.0 230.8 jit_solution(7225049453032462458)
XLA Ops:
  0.6 0.8 pad_maximum_fusion.4
  1.4 27.7 %all_to_all.10 = bf16[4,14,1536]{2,1,0:T(8,128)(2,1)S(1)} all-to-all(bf16[4,14,1536]{2,1,0:T(8,128)(2,1)S(1)} %broadcast_in_dim.55), channel_id=1, replica_groups={{0,32,64,96},{4,36,68,100},{8,40,72,104},{12,44,76,108},{16,48,80,112},..., dimensions={0} | all-to-all | bytes 344064 | tf_op jit(solution)/shard_map/all_to_all | solution.py:67
  29.2 0.2 broadcast_in_dim.56
  29.4 0.0 copy-start
  29.4 0.0 copy-start.14
  29.4 0.0 copy-start.11
  29.4 35.3 %all_to_all.11 = bf16[16,56,1536]{2,1,0:T(8,128)(2,1)S(1)} all-to-all(bf16[16,56,1536]{2,1,0:T(8,128)(2,1)S(1)} %broadcast_in_dim.56), channel_id=1, replica_groups={{0,8,16,24,128,136,144,152,256,264,272,280,384,392,400,408},{4,12,20,28..., dimensions={0} | all-to-all | bytes 5505024 | tf_op jit(solution)/shard_map/all_to_all | solution.py:67
  64.7 8.0 %collective-permute-start = (bf16[896,1536]{1,0:T(8,128)(2,1)S(1)}, bf16[896,1536]{1,0:T(8,128)(2,1)}, u32[]{:S(2)}, u32[]{:S(2)}) collective-permute-start(bf16[896,1536]{1,0:T(8,128)(2,1)S(1)} %bitcast.35), channel_id=1, source_target_pairs={{0,4},{4,0},{8,12},{12,8},{16,20},{20,16},{24,28},{28,24},{32,36},... | collective-permute-start | bytes 8257544 | tf_op jit(solution)/shard_map/ppermute | solution.py:39
  72.7 1.5 collective-permute-start.2
  74.2 2.9 %collective-permute-start.1 = (bf16[192,1536]{1,0:T(8,128)(2,1)S(1)}, bf16[192,1536]{1,0:T(8,128)(2,1)}, u32[]{:S(2)}, u32[]{:S(2)}) collective-permute-start(bf16[192,1536]{1,0:T(8,128)(2,1)S(1)} %copy-done), channel_id=1, source_target_pairs={{0,128},{4,132},{8,136},{12,140},{16,144},{20,148},{24,152},{28,15... | collective-permute-start | bytes 1769480 | tf_op jit(solution)/shard_map/ppermute | solution.py:39
  77.2 0.6 constant_dynamic-slice_fusion
  79.9 0.2 fusion.3
  80.0 0.0 collective-permute-done.2.x2
  80.0 11.1 %collective-permute-done.1.x1 = bf16[192,1536]{1,0:T(8,128)(2,1)} collective-permute-done((bf16[192,1536]{1,0:T(8,128)(2,1)S(1)}, bf16[192,1536]{1,0:T(8,128)(2,1)}, u32[]{:S(2)}, u32[]{:S(2)}) %collective-permute-start.1) | collective-permute-done | bytes 589856 | tf_op jit(solution)/shard_map/ppermute | solution.py:39
  91.1 3.9 %shard_map.123.acc = f32[3,192,768]{2,1,0:T(8,128)S(1)} custom-call(bf16[192,1536]{1,0:T(8,128)(2,1)S(1)} %copy-done, bf16[192,1536]{1,0:T(8,128)(2,1)} %collective-permute-done.1.x1, bf16[192,1536]{1,0:T(8,128)(2,1)} %collective-permute-done.2.x2, bf16[384,224]{1,0:T(8,128)(2,1)S(1)} %get-tuple-element.54.pick_o.pick, bf16[896,1536]{1,0:T(8,128)(2,1)S(1)} %bitcast.36), custom_call_target="tpu_custom_call" | custom-call | flops 1000000000 | bytes 8000000 | tf_op jit(solution)/shard_map/pallas_call | solution.py:279
  95.0 0.0 copy-done.1
  95.0 0.0 collective-permute-done.wt.w
  95.0 4.8 %shard_map.124 = (bf16[3,192,768]{2,1,0:T(8,128)(2,1)S(1)}, f32[192,384]{1,0:T(8,128)S(1)}) custom-call(bf16[192,1536]{1,0:T(8,128)(2,1)S(1)} %copy-done, bf16[192,1536]{1,0:T(8,128)(2,1)} %collective-permute-done.1.x1, bf16[192,1536]{1,0:T(8,128)(2,1)} %collective-permute-done.2.x2, bf16[384,224]{1,0:T(8,128)(2,1)S(1)} %get-tuple-element.53.pick_t.pick, ...), custom_call_target="tpu_custom_call" | custom-call | flops 1000000000 | bytes 8000000 | tf_op jit(solution)/shard_map/pallas_call | solution.py:280
  99.9 0.0 copy-start.13
  99.9 0.0 copy-start.12
  99.9 0.8 select_bitcast_fusion
  100.7 1.1 pad_maximum_fusion.1
  101.8 0.7 copy-done.4
  102.5 3.8 %collective-permute-start.4 = (bf16[384,768]{1,0:T(8,128)(2,1)}, bf16[384,768]{1,0:T(8,128)(2,1)}, u32[]{:S(2)}, u32[]{:S(2)}) collective-permute-start(bf16[384,768]{1,0:T(8,128)(2,1)} %get-tuple-element.46), channel_id=1, source_target_pairs={{4,8},{8,4},{12,16},{16,12},{20,24},{24,20},{28,32},{32,28},{36,40... | collective-permute-start | bytes 1769480 | tf_op jit(solution)/shard_map/ppermute | solution.py:39
  106.3 1.9 collective-permute-start.3
  108.2 0.1 select_reduce_fusion
  109.0 0.0 copy-start.2
  109.0 0.0 copy-start.6
  109.0 1.1 pad_maximum_fusion
  110.2 0.1 copy-done.6
  110.3 7.0 %shard_map.122 = (f32[192,384]{1,0:T(8,128)S(1)}, bf16[192,384]{1,0:T(8,128)(2,1)S(1)}, bf16[192,384]{1,0:T(8,128)(2,1)S(1)}, bf16[256,768]{1,0:T(8,128)(2,1)S(1)}) custom-call(bf16[192,1536]{1,0:T(8,128)(2,1)S(1)} %copy-done, bf16[192,1536]{1,0:T(8,128)(2,1)S(1)} %copy-done.6, bf16[256,1536]{1,0:T(8,128)(2,1)S(1)} %bitcast.41, ...), custom_call_target="tpu_custom_call" | custom-call | flops 1000000000 | bytes 8000000 | tf_op jit(solution)/shard_map/pallas_call | solution.py:287
  117.3 21.6 %collective-permute-done.4 = bf16[384,768]{1,0:T(8,128)(2,1)} collective-permute-done((bf16[384,768]{1,0:T(8,128)(2,1)}, bf16[384,768]{1,0:T(8,128)(2,1)}, u32[]{:S(2)}, u32[]{:S(2)}) %collective-permute-start.4) | collective-permute-done | bytes 589856 | tf_op jit(solution)/shard_map/ppermute | solution.py:39
  139.0 0.0 collective-permute-done.3
  139.0 1.1 broadcast_select_fusion.2.side
  140.1 0.0 copy-done.5
  140.1 0.0 copy-done.10
  140.1 3.6 %shard_map.125 = (bf16[192,384]{1,0:T(8,128)(2,1)S(1)}, bf16[192,384]{1,0:T(8,128)(2,1)S(1)}, bf16[384,768]{1,0:T(8,128)(2,1)S(1)}, bf16[384,768]{1,0:T(8,128)(2,1)S(1)}) custom-call(bf16[192,384]{1,0:T(8,128)(2,1)S(1)} %get-tuple-element.16.qn, bf16[192,384]{1,0:T(8,128)(2,1)S(1)} %get-tuple-element.17.d_att, f32[192,384]{1,0:T(8,128)S(1)} %get-tuple-element.18.qraw, ...), custom_call_target="tpu_custom_call" | custom-call | flops 1000000000 | bytes 8000000 | tf_op jit(solution)/shard_map/pallas_call | solution.py:297
  143.8 0.8 copy-done.7
  144.6 1.1 broadcast_select_fusion.1
  145.7 2.0 collective-permute-start.5
  147.8 1.9 collective-permute-start.6
  149.8 0.3 collective-permute-done.5
  150.1 17.5 %collective-permute-done.6 = bf16[384,768]{1,0:T(8,128)(2,1)} collective-permute-done((bf16[384,768]{1,0:T(8,128)(2,1)}, bf16[384,768]{1,0:T(8,128)(2,1)}, u32[]{:S(2)}, u32[]{:S(2)}) %collective-permute-start.6) | collective-permute-done | bytes 589856 | tf_op jit(solution)/shard_map/ppermute | solution.py:39
  167.6 1.8 add_convert_fusion
  169.4 0.7 collective-permute-start.8
  170.1 5.0 %collective-permute-start.7 = (bf16[192,768]{1,0:T(8,128)(2,1)S(1)}, bf16[192,768]{1,0:T(8,128)(2,1)S(1)}, u32[]{:S(2)}, u32[]{:S(2)}) collective-permute-start(bf16[192,768]{1,0:T(8,128)(2,1)S(1)} %get-tuple-element.32), channel_id=1, source_target_pairs={{0,128},{4,132},{8,136},{12,140},{16,144},{20,148},{24,152},{28,15... | collective-permute-start | bytes 884744 | tf_op jit(solution)/shard_map/ppermute | solution.py:39
  175.1 3.8 %shard_map.126 = (bf16[4,192,384]{2,1,0:T(8,128)(2,1)S(1)}, f32[2,4,192,224]{3,2,1,0:T(8,128)S(1)}) custom-call(bf16[192,384]{1,0:T(8,128)(2,1)S(1)} %get-tuple-element.24.att, bf16[192,384]{1,0:T(8,128)(2,1)S(1)} %get-tuple-element.25.dq, bf16[896,1536]{1,0:T(8,128)(2,1)S(1)} %bitcast.39, bf16[896,1536]{1,0:T(8,128)(2,1)} %collective-permute-done.wt.w, ...), custom_call_target="tpu_custom_call" | custom-call | flops 1000000000 | bytes 8000000 | tf_op jit(solution)/shard_map/pallas_call | solution.py:311
  178.9 0.1 dynamic-slice_bitcast_fusion.3
  179.0 10.5 %collective-permute-start.11 = (bf16[192,384]{1,0:T(8,128)(2,1)S(1)}, bf16[192,384]{1,0:T(8,128)(2,1)S(1)}, u32[]{:S(2)}, u32[]{:S(2)}) collective-permute-start(bf16[192,384]{1,0:T(8,128)(2,1)S(1)} %get-tuple-element.40), channel_id=1, source_target_pairs={{0,3},{1,0},{2,1},{3,2},{4,7},{5,4},{6,5},{7,6},{8,11},{9,8},{10,9... | collective-permute-start | bytes 442376 | tf_op jit(solution)/shard_map/ppermute | solution.py:225
  189.5 14.6 %collective-permute-start.10 = (bf16[192,384]{1,0:T(8,128)(2,1)S(1)}, bf16[192,384]{1,0:T(8,128)(2,1)S(1)}, u32[]{:S(2)}, u32[]{:S(2)}) collective-permute-start(bf16[192,384]{1,0:T(8,128)(2,1)S(1)} %get-tuple-element.41), channel_id=1, source_target_pairs={{0,2},{1,3},{2,0},{3,1},{4,6},{5,7},{6,4},{7,5},{8,10},{9,11},{10,... | collective-permute-start | bytes 442376 | tf_op jit(solution)/shard_map/ppermute | solution.py:225
  204.1 3.4 %collective-permute-start.9 = (bf16[192,384]{1,0:T(8,128)(2,1)S(1)}, bf16[192,384]{1,0:T(8,128)(2,1)S(1)}, u32[]{:S(2)}, u32[]{:S(2)}) collective-permute-start(bf16[192,384]{1,0:T(8,128)(2,1)S(1)} %get-tuple-element.42), channel_id=1, source_target_pairs={{0,1},{1,2},{2,3},{3,0},{4,5},{5,6},{6,7},{7,4},{8,9},{9,10},{10,1... | collective-permute-start | bytes 442376 | tf_op jit(solution)/shard_map/ppermute | solution.py:225
  207.4 0.0 collective-permute-done.11.o3
  207.5 1.7 collective-permute-done.10.o2
  209.1 2.6 %collective-permute-done.9.o1 = bf16[192,384]{1,0:T(8,128)(2,1)S(1)} collective-permute-done((bf16[192,384]{1,0:T(8,128)(2,1)S(1)}, bf16[192,384]{1,0:T(8,128)(2,1)S(1)}, u32[]{:S(2)}, u32[]{:S(2)}) %collective-permute-start.9) | collective-permute-done | bytes 147488 | tf_op jit(solution)/shard_map/ppermute | solution.py:225
  211.8 0.0 collective-permute-done.8.in_b
  211.8 0.0 collective-permute-done.7.in_a
  211.8 4.3 %shard_map.127 = (bf16[4,192,384]{2,1,0:T(8,128)(2,1)S(1)}, bf16[192,384]{1,0:T(8,128)(2,1)}) custom-call(f32[192,768]{1,0:T(8,128)S(1)} %get-tuple-element.31.own, bf16[192,768]{1,0:T(8,128)(2,1)S(1)} %collective-permute-done.7.in_a, bf16[192,768]{1,0:T(8,128)(2,1)S(1)} %collective-permute-done.8.in_b, f32[192,384]{1,0:T(8,128)S(1)} %copy-done.9, ...), custom_call_target="tpu_custom_call" | custom-call | flops 1000000000 | bytes 8000000 | tf_op jit(solution)/shard_map/pallas_call | solution.py:325
  216.2 1.9 collective-permute-start.12
  218.1 5.2 %collective-permute-start.14 = (bf16[192,384]{1,0:T(8,128)(2,1)S(1)}, bf16[192,384]{1,0:T(8,128)(2,1)S(1)}, u32[]{:S(2)}, u32[]{:S(2)}) collective-permute-start(bf16[192,384]{1,0:T(8,128)(2,1)S(1)} %get-tuple-element.38), channel_id=1, source_target_pairs={{0,3},{1,0},{2,1},{3,2},{4,7},{5,4},{6,5},{7,6},{8,11},{9,8},{10,9... | collective-permute-start | bytes 442376 | tf_op jit(solution)/shard_map/ppermute | solution.py:225
  223.3 1.9 collective-permute-start.13
  225.2 0.0 collective-permute-done.12
  225.2 0.2 collective-permute-done.14
  225.4 4.6 %collective-permute-done.13 = bf16[192,384]{1,0:T(8,128)(2,1)S(1)} collective-permute-done((bf16[192,384]{1,0:T(8,128)(2,1)S(1)}, bf16[192,384]{1,0:T(8,128)(2,1)S(1)}, u32[]{:S(2)}, u32[]{:S(2)}) %collective-permute-start.13) | collective-permute-done | bytes 147488 | tf_op jit(solution)/shard_map/ppermute | solution.py:225
  230.0 0.7 fusion.6
  (31 shorter events, 0.3 us)
Async XLA Ops:
  29.4 43.3 %copy-start = (bf16[192,1536]{1,0:T(8,128)(2,1)S(1)}, bf16[192,1536]{1,0:T(8,128)(2,1)}, u32[]{:S(2)}) copy-start(bf16[192,1536]{1,0:T(8,128)(2,1)} %x0.3) | copy-start | bytes 1769476
  29.4 47.7 %copy-start.14 = (s32[128,2]{0,1:T(2,128)S(1)}, s32[128,2]{0,1:T(2,128)}, u32[]{:S(2)}) copy-start(s32[128,2]{0,1:T(2,128)} %param.20) | copy-start | bytes 3076
  29.4 50.3 %copy-start.11 = (f32[384]{0:T(512)S(1)}, f32[384]{0:T(512)}, u32[]{:S(2)}) copy-start(f32[384]{0:T(512)} %param.18) | copy-start | bytes 4612
  64.7 30.3 %collective-permute-start = (bf16[896,1536]{1,0:T(8,128)(2,1)S(1)}, bf16[896,1536]{1,0:T(8,128)(2,1)}, u32[]{:S(2)}, u32[]{:S(2)}) collective-permute-start(bf16[896,1536]{1,0:T(8,128)(2,1)S(1)} %bitcast.35), channel_id=1, source_target_pairs={{0,4},{4,0},{8,12},{12,8},{16,20},{20,16},{24,28},{28,24},{32,36},... | collective-permute-start | bytes 8257544 | tf_op jit(solution)/shard_map/ppermute | solution.py:39
  72.7 7.3 %collective-permute-start.2 = (bf16[192,1536]{1,0:T(8,128)(2,1)S(1)}, bf16[192,1536]{1,0:T(8,128)(2,1)}, u32[]{:S(2)}, u32[]{:S(2)}) collective-permute-start(bf16[192,1536]{1,0:T(8,128)(2,1)S(1)} %copy-done), channel_id=1, source_target_pairs={{128,256},{132,260},{136,264},{140,268},{144,272},{148,276},{152,2... | collective-permute-start | bytes 1769480 | tf_op jit(solution)/shard_map/ppermute | solution.py:39
  74.2 16.9 %collective-permute-start.1 = (bf16[192,1536]{1,0:T(8,128)(2,1)S(1)}, bf16[192,1536]{1,0:T(8,128)(2,1)}, u32[]{:S(2)}, u32[]{:S(2)}) collective-permute-start(bf16[192,1536]{1,0:T(8,128)(2,1)S(1)} %copy-done), channel_id=1, source_target_pairs={{0,128},{4,132},{8,136},{12,140},{16,144},{20,148},{24,152},{28,15... | collective-permute-start | bytes 1769480 | tf_op jit(solution)/shard_map/ppermute | solution.py:39
  80.0 15.0 %copy-start.1 = (bf16[384,224]{1,0:T(8,128)(2,1)}, bf16[384,224]{1,0:T(8,128)(2,1)S(1)}, u32[]{:S(2)}) copy-start(bf16[384,224]{1,0:T(8,128)(2,1)S(1)} %get-tuple-element.54.pick_o.pick) | copy-start | bytes 516100
  99.9 1.9 copy-start.8
  99.9 8.3 %copy-start.13 = (s32[256]{0:T(256)S(1)}, s32[256]{0:T(256)}, u32[]{:S(2)}) copy-start(s32[256]{0:T(256)} %param.19) | copy-start | bytes 3076
  99.9 8.5 %copy-start.12 = (f32[384]{0:T(512)S(1)}, f32[384]{0:T(512)}, u32[]{:S(2)}) copy-start(f32[384]{0:T(512)} %param.17) | copy-start | bytes 4612
  101.8 0.7 copy-start.4
  102.5 36.5 %collective-permute-start.4 = (bf16[384,768]{1,0:T(8,128)(2,1)}, bf16[384,768]{1,0:T(8,128)(2,1)}, u32[]{:S(2)}, u32[]{:S(2)}) collective-permute-start(bf16[384,768]{1,0:T(8,128)(2,1)} %get-tuple-element.46), channel_id=1, source_target_pairs={{4,8},{8,4},{12,16},{16,12},{20,24},{24,20},{28,32},{32,28},{36,40... | collective-permute-start | bytes 1769480 | tf_op jit(solution)/shard_map/ppermute | solution.py:39
  106.3 32.7 %collective-permute-start.3 = (bf16[384,768]{1,0:T(8,128)(2,1)}, bf16[384,768]{1,0:T(8,128)(2,1)}, u32[]{:S(2)}, u32[]{:S(2)}) collective-permute-start(bf16[384,768]{1,0:T(8,128)(2,1)} %get-tuple-element.47), channel_id=1, source_target_pairs={{0,4},{4,0},{8,12},{12,8},{16,20},{20,16},{24,28},{28,24},{32,36},... | collective-permute-start | bytes 1769480 | tf_op jit(solution)/shard_map/ppermute | solution.py:39
  109.0 1.1 copy-start.2
  109.0 1.3 copy-start.6
  117.3 22.8 %copy-start.5 = (bf16[192,768]{1,0:T(8,128)(2,1)S(1)}, bf16[192,768]{1,0:T(8,128)(2,1)}, u32[]{:S(2)}) copy-start(bf16[192,768]{1,0:T(8,128)(2,1)} %copy-done.4) | copy-start | bytes 884740
  117.3 22.8 %copy-start.10 = (bf16[192,768]{1,0:T(8,128)(2,1)S(1)}, bf16[192,768]{1,0:T(8,128)(2,1)}, u32[]{:S(2)}) copy-start(bf16[192,768]{1,0:T(8,128)(2,1)} %get-tuple-element.34.far) | copy-start | bytes 884740
  143.8 0.8 copy-start.7
  145.7 29.4 %copy-start.3 = (bf16[384,224]{1,0:T(8,128)(2,1)S(1)}, bf16[384,224]{1,0:T(8,128)(2,1)}, u32[]{:S(2)}) copy-start(bf16[384,224]{1,0:T(8,128)(2,1)} %copy-done.1) | copy-start | bytes 516100
  145.7 4.4 %collective-permute-start.5 = (bf16[384,768]{1,0:T(8,128)(2,1)}, bf16[384,768]{1,0:T(8,128)(2,1)}, u32[]{:S(2)}, u32[]{:S(2)}) collective-permute-start(bf16[384,768]{1,0:T(8,128)(2,1)} %get-tuple-element.44), channel_id=1, source_target_pairs={{0,4},{4,0},{8,12},{12,8},{16,20},{20,16},{24,28},{28,24},{32,36},... | collective-permute-start | bytes 1769480 | tf_op jit(solution)/shard_map/ppermute | solution.py:39
  147.8 19.8 %collective-permute-start.6 = (bf16[384,768]{1,0:T(8,128)(2,1)}, bf16[384,768]{1,0:T(8,128)(2,1)}, u32[]{:S(2)}, u32[]{:S(2)}) collective-permute-start(bf16[384,768]{1,0:T(8,128)(2,1)} %get-tuple-element.45), channel_id=1, source_target_pairs={{4,8},{8,4},{12,16},{16,12},{20,24},{24,20},{28,32},{32,28},{36,40... | collective-permute-start | bytes 1769480 | tf_op jit(solution)/shard_map/ppermute | solution.py:39
  169.4 42.4 %collective-permute-start.8 = (bf16[192,768]{1,0:T(8,128)(2,1)S(1)}, bf16[192,768]{1,0:T(8,128)(2,1)S(1)}, u32[]{:S(2)}, u32[]{:S(2)}) collective-permute-start(bf16[192,768]{1,0:T(8,128)(2,1)S(1)} %get-tuple-element.30), channel_id=1, source_target_pairs={{128,256},{132,260},{136,264},{140,268},{144,272},{148,276},{152,2... | collective-permute-start | bytes 884744 | tf_op jit(solution)/shard_map/ppermute | solution.py:39
  170.1 41.7 %collective-permute-start.7 = (bf16[192,768]{1,0:T(8,128)(2,1)S(1)}, bf16[192,768]{1,0:T(8,128)(2,1)S(1)}, u32[]{:S(2)}, u32[]{:S(2)}) collective-permute-start(bf16[192,768]{1,0:T(8,128)(2,1)S(1)} %get-tuple-element.32), channel_id=1, source_target_pairs={{0,128},{4,132},{8,136},{12,140},{16,144},{20,148},{24,152},{28,15... | collective-permute-start | bytes 884744 | tf_op jit(solution)/shard_map/ppermute | solution.py:39
  175.1 36.7 %copy-start.9 = (f32[192,384]{1,0:T(8,128)S(1)}, f32[192,384]{1,0:T(8,128)}, u32[]{:S(2)}) copy-start(f32[192,384]{1,0:T(8,128)} %copy-done.8) | copy-start | bytes 884740
  179.0 28.5 %collective-permute-start.11 = (bf16[192,384]{1,0:T(8,128)(2,1)S(1)}, bf16[192,384]{1,0:T(8,128)(2,1)S(1)}, u32[]{:S(2)}, u32[]{:S(2)}) collective-permute-start(bf16[192,384]{1,0:T(8,128)(2,1)S(1)} %get-tuple-element.40), channel_id=1, source_target_pairs={{0,3},{1,0},{2,1},{3,2},{4,7},{5,4},{6,5},{7,6},{8,11},{9,8},{10,9... | collective-permute-start | bytes 442376 | tf_op jit(solution)/shard_map/ppermute | solution.py:225
  189.5 19.7 %collective-permute-start.10 = (bf16[192,384]{1,0:T(8,128)(2,1)S(1)}, bf16[192,384]{1,0:T(8,128)(2,1)S(1)}, u32[]{:S(2)}, u32[]{:S(2)}) collective-permute-start(bf16[192,384]{1,0:T(8,128)(2,1)S(1)} %get-tuple-element.41), channel_id=1, source_target_pairs={{0,2},{1,3},{2,0},{3,1},{4,6},{5,7},{6,4},{7,5},{8,10},{9,11},{10,... | collective-permute-start | bytes 442376 | tf_op jit(solution)/shard_map/ppermute | solution.py:225
  204.1 7.7 %collective-permute-start.9 = (bf16[192,384]{1,0:T(8,128)(2,1)S(1)}, bf16[192,384]{1,0:T(8,128)(2,1)S(1)}, u32[]{:S(2)}, u32[]{:S(2)}) collective-permute-start(bf16[192,384]{1,0:T(8,128)(2,1)S(1)} %get-tuple-element.42), channel_id=1, source_target_pairs={{0,1},{1,2},{2,3},{3,0},{4,5},{5,6},{6,7},{7,4},{8,9},{9,10},{10,1... | collective-permute-start | bytes 442376 | tf_op jit(solution)/shard_map/ppermute | solution.py:225
  216.2 9.0 %collective-permute-start.12 = (bf16[192,384]{1,0:T(8,128)(2,1)S(1)}, bf16[192,384]{1,0:T(8,128)(2,1)S(1)}, u32[]{:S(2)}, u32[]{:S(2)}) collective-permute-start(bf16[192,384]{1,0:T(8,128)(2,1)S(1)} %get-tuple-element.37), channel_id=1, source_target_pairs={{0,1},{1,2},{2,3},{3,0},{4,5},{5,6},{6,7},{7,4},{8,9},{9,10},{10,1... | collective-permute-start | bytes 442376 | tf_op jit(solution)/shard_map/ppermute | solution.py:225
  218.1 7.3 %collective-permute-start.14 = (bf16[192,384]{1,0:T(8,128)(2,1)S(1)}, bf16[192,384]{1,0:T(8,128)(2,1)S(1)}, u32[]{:S(2)}, u32[]{:S(2)}) collective-permute-start(bf16[192,384]{1,0:T(8,128)(2,1)S(1)} %get-tuple-element.38), channel_id=1, source_target_pairs={{0,3},{1,0},{2,1},{3,2},{4,7},{5,4},{6,5},{7,6},{8,11},{9,8},{10,9... | collective-permute-start | bytes 442376 | tf_op jit(solution)/shard_map/ppermute | solution.py:225
  223.3 6.8 %collective-permute-start.13 = (bf16[192,384]{1,0:T(8,128)(2,1)S(1)}, bf16[192,384]{1,0:T(8,128)(2,1)S(1)}, u32[]{:S(2)}, u32[]{:S(2)}) collective-permute-start(bf16[192,384]{1,0:T(8,128)(2,1)S(1)} %get-tuple-element.39), channel_id=1, source_target_pairs={{0,2},{1,3},{2,0},{3,1},{4,6},{5,7},{6,4},{7,5},{8,10},{9,11},{10,... | collective-permute-start | bytes 442376 | tf_op jit(solution)/shard_map/ppermute | solution.py:225

commit v3 on v2

v3 whole, which is shorter than its diff:
```python
import functools

import jax
import jax.numpy as jnp
from jax import lax
from jax.experimental import pallas as pl
from jax.experimental.pallas import tpu as pltpu
from jax.sharding import PartitionSpec as P

HD = 128
NH = 3
W = NH * HD
ROWS = 192
TEXT = 256
EPS = 1e-6
SCALE = HD**-0.5
ZH_ORDER = (0, 1, 3, 2)
BLOCK = 56
PART = 4 * BLOCK
F32 = jnp.float32
BF16 = jnp.bfloat16
NT = (((1,), (1,)), ((), ()))
TN = (((0,), (0,)), ((), ()))


def place_of(x, zh, y, core):
    return ((x * 4 + zh) * 4 + y) * 2 + core


def all_places():
    return [(x, z, y, c) for x in range(4) for z in range(4) for y in range(4) for c in range(2)]


def seq_move(value, target):
    pairs = []
    for at in all_places():
        to = target(*at)
        if to is not None:
            pairs.append((place_of(*at), place_of(*to)))
    return lax.ppermute(value, "seq", pairs)


def core_mate(value):
    return seq_move(value, lambda x, z, y, c: (x, z, y, 1 - c))


def next_chip(value):
    def target(x, z, y, c):
        col = (z * 4 + y) * 2 + c
        col = col + 1 if c == 1 else col - 1
        if not 0 <= col < 32:
            return None
        return (x, col // 8, col // 2 % 4, col % 2)

    return seq_move(value, target)


def row_even(value):
    return seq_move(value, lambda x, z, y, c: (x ^ 1, z, y, c))


def row_odd(value):
    return seq_move(value, lambda x, z, y, c: (3 - x, z, y, c) if x in (1, 2) else None)


def give_all(value, groups):
    copies = jnp.broadcast_to(value[None], (len(groups[0]),) + value.shape)
    return lax.all_to_all(copies, "seq", 0, 0, axis_index_groups=groups)


def across_zh(value, mask):
    return seq_move(value, lambda x, z, y, c: (x, z ^ mask, y, c))


def over_xy(value):
    four = range(4)
    return give_all(
        value,
        [[place_of(x, z, y, c) for x in four for y in four] for z in four for c in range(2)],
    )


def dot(a, b, dims=(((1,), (0,)), ((), ()))):
    return lax.dot_general(a, b, dims, preferred_element_type=F32)


def norm_rows(a, gain):
    r = lax.rsqrt(jnp.mean(a * a, axis=-1, keepdims=True) + EPS)
    return a * r * gain


def norm_pull(a, gain, dy):
    r = lax.rsqrt(jnp.mean(a * a, axis=-1, keepdims=True) + EPS)
    t = dy * gain
    return r * t - a * (r * r * r * jnp.mean(t * a, axis=-1, keepdims=True))


def head(h):
    return slice(h * HD, (h + 1) * HD)


def val(h):
    return slice(W + h * HD, W + (h + 1) * HD)


def call(kernel, outs, scratch=(), mib=32, flops=10**9, flagged=False, count=0):
    spaces = [pltpu.SMEM if flagged and n == 0 else pltpu.VMEM for n in range(count)]
    return pl.pallas_call(
        kernel,
        out_shape=outs,
        in_specs=[pl.BlockSpec(memory_space=space) for space in spaces],
        scratch_shapes=scratch,
        compiler_params=pltpu.CompilerParams(vmem_limit_bytes=mib * 2**20),
        cost_estimate=pl.CostEstimate(flops=flops, bytes_accessed=8 * 10**6, transcendentals=0),
    )


def shape(dims, dtype):
    return jax.ShapeDtypeStruct(dims, dtype)


def project(rows, pick, w, cols):
    acc = None
    for j in range(4):
        xs = dot(rows[:, j * W : (j + 1) * W], pick[...]).astype(BF16)
        term = dot(xs, w[j * PART : (j + 1) * PART, cols])
        acc = term if acc is None else acc + term
    return acc


def project_parts(flags, parts, pick, w):
    acc = None
    for n, part in enumerate(parts):
        at = pl.multiple_of(flags[2 + n] * PART, PART)
        xs = dot(part[...], pick[...]).astype(BF16)
        term = dot(xs, w[pl.ds(at, PART), : 2 * W])
        acc = term if acc is None else acc + term
    return acc


KVQ = slice(0, 3 * W)
KV = slice(0, 2 * W)
LAST = slice(3 * W, 4 * W)


def first_kernel(flags, x, g, p0, p1, p2, p3, pick, w, acc_x, acc_g, acc_p):
    acc_x[...] = project(x, pick, w, KVQ)
    acc_g[...] = project(g, pick, w, LAST)
    acc_p[...] = project_parts(flags, (p0, p1, p2, p3), pick, w)


def attend_kernel(
    flags,
    x,
    g,
    p0,
    p1,
    p2,
    p3,
    text,
    pick_o,
    pick_t,
    wo,
    wt,
    acc_x,
    acc_g,
    acc_p,
    q_gain,
    k_gain,
    bias,
    att,
    dq,
    near_t,
    even_t,
    odd_t,
    kraw,
    keys,
):
    n = 4 * ROWS
    mine = acc_x[...] + project(x, pick_t, wt, KVQ)
    d_att = (acc_g[...] + project(g, pick_t, wt, LAST)).astype(BF16)
    others = acc_p[...] + project_parts(flags, (p0, p1, p2, p3), pick_t, wt)
    words = project(text, pick_o, wo, KV) + project(text, pick_t, wt, KV)
    kraw[...] = mine[:, :W]
    for low, high, values in ((0, ROWS, mine), (ROWS, n, others), (n, n + TEXT, words)):
        for h in range(NH):
            kn = norm_rows(values[:, head(h)], k_gain[:, head(h)])
            keys[low:high, head(h)] = kn.astype(BF16)
        keys[low:high, W:] = values[:, W : 2 * W].astype(BF16)
    even = flags[0].astype(F32)
    odd = 1.0 - even
    for h in range(NH):
        q = mine[:, val(NH + h)]
        qh = norm_rows(q, q_gain[:, head(h)]).astype(BF16)
        dh = d_att[:, head(h)]
        kh = keys[:, head(h)]
        vh = keys[:, val(h)]
        s = dot(qh, kh, NT) * SCALE + bias[...]
        e = jnp.exp(s - jnp.max(s, axis=-1, keepdims=True))
        p = e * (1.0 / jnp.sum(e, axis=-1, keepdims=True))
        pb = p.astype(BF16)
        att[:, head(h)] = dot(pb, vh).astype(BF16)
        dp = dot(dh, vh, NT)
        ds = (p * (dp - jnp.sum(p * dp, axis=-1, keepdims=True))).astype(BF16)
        d_q = dot(ds, kh) * SCALE
        dq[:, head(h)] = norm_pull(q, q_gain[:, head(h)], d_q).astype(BF16)
        kt = dot(ds[:, :n], qh, TN) * SCALE
        vt = dot(pb[:, :n], dh, TN)
        for lanes, term in ((head(h), kt), (val(h), vt)):
            near_t[:, lanes] = term[: 2 * ROWS].astype(BF16)
            even_t[:, lanes] = (term[2 * ROWS :] * even).astype(BF16)
            odd_t[:, lanes] = (term[2 * ROWS :] * odd).astype(BF16)


def out_kernel(att, dq, wo, wt, pick_o, pick_t, out, gq):
    for j in range(4):
        rows = slice(j * PART, (j + 1) * PART)
        o = dot(att[...], wo[rows, 3 * W :], NT).astype(BF16)
        t = dot(att[...], wt[rows, 3 * W :], NT).astype(BF16)
        out[j] = (dot(o, pick_o[...], NT) + dot(t, pick_t[...], NT)).astype(BF16)
        gq[0, j] = dot(dq[...], wo[rows, 2 * W : 3 * W], NT)
        gq[1, j] = dot(dq[...], wt[rows, 2 * W : 3 * W], NT)


def grad_kernel(own, in_a, in_b, kraw, k_gain, gq, wo, wt, pick_o, pick_t, o0, o1, o2, o3, out, res):
    total = own[...] + in_a[...].astype(F32) + in_b[...].astype(F32)
    parts = [
        norm_pull(kraw[:, head(h)], k_gain[:, head(h)], total[:, head(h)]).astype(BF16)
        for h in range(NH)
    ]
    d = jnp.concatenate(parts + [total[:, W:].astype(BF16)], axis=1)
    for j in range(4):
        rows = slice(j * PART, (j + 1) * PART)
        o = (gq[0, j] + dot(d, wo[rows, : 2 * W], NT)).astype(BF16)
        t = (gq[1, j] + dot(d, wt[rows, : 2 * W], NT)).astype(BF16)
        out[j] = (dot(o, pick_o[...], NT) + dot(t, pick_t[...], NT)).astype(BF16)
    res[...] = (
        o0[...].astype(F32) + o1[...].astype(F32) + o2[...].astype(F32) + o3[...].astype(F32)
    ).astype(BF16)


def to_heads(blocks, me):
    def block(to):
        return lax.dynamic_index_in_dim(blocks, to % 4, 0, keepdims=False)

    return [block(me)] + [head_shift(block(me + by), by) for by in (1, 2, 3)]


def f32_sum(*terms):
    total = terms[0].astype(F32)
    for term in terms[1:]:
        total = total + term.astype(F32)
    return total


def head_shift(value, by):
    return lax.ppermute(value, "heads", [(i, (i + by) % 4) for i in range(4)])


def per_device(
    x_tiles, x_text, w_query, w_key, w_value, w_output, q_gain, k_gain, text_mask, windows, grad_out
):
    place = lax.axis_index("seq")
    me = lax.axis_index("heads")
    core, zh, x, col = place % 2, place // 8 % 4, place // 32, place % 32
    window = lax.dynamic_slice(windows, (place, jnp.int32(0)), (1, 2))
    use_even = (window[0, 0] == x) == (x % 2 == 0)
    use_core = (window[0, 1] == col) == (core == 0)
    q_gain = q_gain[None, :]
    k_gain = k_gain[None, :]
    blocks = [(me - by) % 4 for by in range(4)]
    flags = jnp.stack([use_even.astype(jnp.int32), use_core.astype(jnp.int32)] + blocks)

    mine = jnp.concatenate([w_key, w_value, w_query, w_output], axis=1)
    mine = jnp.concatenate([mine, x_text], axis=0)
    quarter = lax.dynamic_slice(x_tiles, (jnp.int32(0), me * W), (ROWS, W))
    two = jnp.stack([mine, across_zh(mine, 1)])
    side = jnp.where(use_core, core_mate(quarter), next_chip(quarter))
    four = jnp.concatenate([two, across_zh(two, 3)])
    pair = jnp.concatenate([quarter, side])
    far = jnp.where(use_even, row_even(pair), row_odd(pair))
    others = jnp.concatenate([side, far])
    block = jnp.concatenate([four[:, :12].reshape(48, 1536), four[:, 12:].reshape(8, 1536)], axis=0)
    block, others = lax.optimization_barrier((block, others))
    parts = [others] + [head_shift(others, by) for by in (1, 2, 3)]
    wo = over_xy(block).reshape(16 * BLOCK, 1536)
    wo, *parts = lax.optimization_barrier((wo, *parts))
    wt = core_mate(wo)

    at = jnp.arange(PART, dtype=jnp.int32)
    inner = at % BLOCK
    feature = lax.broadcasted_iota(jnp.int32, (W, PART), 0)
    z_order = jnp.array(ZH_ORDER, jnp.int32)

    def pick(which):
        natural = (((z_order[inner // 12 % 4] ^ zh) * 4 + at // BLOCK) * 2 + which) * 12 + inner % 12
        hit = (feature == natural[None, :]) & (inner < 48)[None, :]
        return hit.astype(BF16)

    pick_o, pick_t = pick(core), pick(1 - core)
    t = jnp.arange(TEXT, dtype=jnp.int32)
    token = place_of(t // 32 % 4, z_order[t // 2 % 4] ^ zh, t // 8 % 4, (t // 128) ^ core) * 2 + t % 2
    valid = jnp.sum(jnp.where(t[:, None] == token[None, :], text_mask[:, None], 0), axis=0)
    bias = jnp.concatenate(
        [jnp.zeros((4 * ROWS,), F32), jnp.where(valid == 1, 0.0, -1e30).astype(F32)]
    )[None, :]

    accs = call(
        first_kernel,
        (shape((ROWS, 3 * W), F32), shape((ROWS, W), F32), shape((3 * ROWS, 2 * W), F32)),
        flagged=True,
        count=9,
    )(flags, x_tiles, grad_out, *parts, pick_o, wo)
    texts = jnp.stack([wo, wt]).reshape(2, 16, BLOCK, 1536)[:, :, 48:].reshape(TEXT, 1536)
    att, dq, near_t, even_t, odd_t, kraw = call(
        attend_kernel,
        (
            shape((ROWS, W), BF16),
            shape((ROWS, W), BF16),
            shape((2 * ROWS, 768), BF16),
            shape((2 * ROWS, 768), BF16),
            shape((2 * ROWS, 768), BF16),
            shape((ROWS, W), F32),
        ),
        [pltpu.VMEM((1024, 768), BF16)],
        mib=40,
        flagged=True,
        count=18,
    )(flags, x_tiles, grad_out, *parts, texts, pick_o, pick_t, wo, wt, *accs, q_gain, k_gain, bias)

    got_even, got_odd = row_even(even_t), row_odd(odd_t)
    out, gq = call(
        out_kernel, (shape((4, ROWS, W), BF16), shape((2, 4, ROWS, PART), F32)), count=6
    )(att, dq, wo, wt, pick_o, pick_t)
    outs = to_heads(out, me)
    own_t = f32_sum(near_t[:ROWS], got_even[:ROWS], got_odd[:ROWS])
    side_t = f32_sum(near_t[ROWS:], got_even[ROWS:], got_odd[ROWS:]).astype(BF16)
    zero = jnp.zeros((ROWS, 768), BF16)
    mate_t = core_mate(jnp.where(use_core, side_t, zero))
    next_t = next_chip(jnp.where(use_core, zero, side_t))
    grad, out_tiles = call(
        grad_kernel, (shape((4, ROWS, W), BF16), shape((ROWS, W), BF16)), count=14
    )(own_t, mate_t, next_t, kraw, k_gain, gq, wo, wt, pick_o, pick_t, *outs)
    grad_tiles = f32_sum(*to_heads(grad, me)).astype(BF16)
    return (out_tiles, grad_tiles)


def solution(mesh):
    in_specs = (
        P("seq", None),
        P("seq", None),
        P("seq", "heads"),
        P("seq", "heads"),
        P("seq", "heads"),
        P("seq", "heads"),
        P("heads"),
        P("heads"),
        P(),
        P(),
        P("seq", None),
    )
    out_specs = (P("seq", "heads"), P("seq", "heads"))
    return jax.shard_map(
        per_device, mesh=mesh, in_specs=in_specs, out_specs=out_specs, check_vma=False
    )
```

time: 232 us -> 206 us (0.89)
  the two profiles are of different devices: /device:TPU:25 before, /device:TPU:155 now
where the time goes in v3:
time: 206 us; the launch traced here: 204 us
  starting transfers between devices  85.7 us (42%)
  waiting for transfers between devices  69.4 us (34%)
  Pallas kernels  24.6 us (12%)
  local copies, waits for them, and re-layouts  15.6 us (8%)
  other arithmetic  6.61 us (3%)
  between operations  2.63 us (1%)
    ppermute x9, waiting for transfers between devices, head_shift(): return lax.ppermute(value, 'heads', [(i, (i + by) % 4) for i in range(4)])  41.2 us
    ppermute x11, starting transfers between devices, seq_move(): return lax.ppermute(value, 'seq', pairs)  40.7 us
    ppermute x9, starting transfers between devices, head_shift(): return lax.ppermute(value, 'heads', [(i, (i + by) % 4) for i in range(4)])  38.4 us
    ppermute x11, waiting for transfers between devices, seq_move(): return lax.ppermute(value, 'seq', pairs)  28.1 us
    pallas_call x1, Pallas kernels, per_device(): call(attend_kernel, (shape((ROWS, W), BF16), shape((ROWS, W), BF16), shap...  12.3 us
    unnamed x54, local copies, waits for them, and re-layouts  12.1 us
    all_to_all x1, starting transfers between devices, give_all(): return lax.all_to_all(copies, 'seq', 0, 0, axis_index_groups=groups)  6.49 us
    pallas_call x1, Pallas kernels, per_device(): call(grad_kernel, (shape((4, ROWS, W), BF16), shape((ROWS, W), BF16)), co...  4.35 us
  transfers between devices with their start and end apart: 21, of which 13 were waited for; matrix products, arithmetic and copies ran while one was open for 2% of the time, Pallas kernels for 4%

profile of v3, /device:TPU:155, one launch (start us, length us, event | category | flops | bytes accessed | tf_op | source)
XLA Modules:
  0.0 204.5 jit_solution(12065974968396172655)
XLA Ops:
  0.7 0.9 constant_dynamic-slice_fusion
  1.6 2.6 %collective-permute-start.2 = (bf16[192,384]{1,0:T(8,128)(2,1)S(1)}, bf16[192,384]{1,0:T(8,128)(2,1)S(1)}, u32[]{:S(2)}, u32[]{:S(2)}) collective-permute-start(bf16[192,384]{1,0:T(8,128)(2,1)S(1)} %constant_dynamic-slice_fusion), channel_id=1, source_target_pairs={{0,4},{4,0},{8,12},{12,8},{16,20},{20,16},{24,28},{28,24},{32,36},... | collective-permute-start | bytes 442376 | tf_op jit(solution)/shard_map/ppermute | solution.py:40
  4.2 8.4 %collective-permute-start.3 = (bf16[192,384]{1,0:T(8,128)(2,1)S(1)}, bf16[192,384]{1,0:T(8,128)(2,1)S(1)}, u32[]{:S(2)}, u32[]{:S(2)}) collective-permute-start(bf16[192,384]{1,0:T(8,128)(2,1)S(1)} %constant_dynamic-slice_fusion), channel_id=1, source_target_pairs={{4,8},{8,4},{12,16},{16,12},{20,24},{24,20},{28,32},{32,28},{36,40... | collective-permute-start | bytes 442376 | tf_op jit(solution)/shard_map/ppermute | solution.py:40
  12.6 0.8 pad_maximum_fusion.6
  13.4 1.9 collective-permute-start
  15.3 0.8 fusion.27
  16.2 6.2 %collective-permute-done = bf16[14,1536]{1,0:T(8,128)(2,1)S(1)} collective-permute-done((bf16[14,1536]{1,0:T(8,128)(2,1)S(1)}, bf16[14,1536]{1,0:T(8,128)(2,1)S(1)}, u32[]{:S(2)}, u32[]{:S(2)}) %collective-permute-start) | collective-permute-done | bytes 43040 | tf_op jit(solution)/shard_map/ppermute | solution.py:40
  22.4 7.1 %collective-permute-start.1 = (bf16[2,14,1536]{2,1,0:T(8,128)(2,1)S(1)}, bf16[2,14,1536]{2,1,0:T(8,128)(2,1)S(1)}, u32[]{:S(2)}, u32[]{:S(2)}) collective-permute-start(bf16[2,14,1536]{2,1,0:T(8,128)(2,1)S(1)} %pad_maximum_fusion.5), channel_id=1, source_target_pairs={{0,96},{4,100},{8,104},{12,108},{16,112},{20,116},{24,120},{28,124... | collective-permute-start | bytes 258056 | tf_op jit(solution)/shard_map/ppermute | solution.py:40
  29.5 0.5 fusion.26
  31.3 7.3 %collective-permute-done.1 = bf16[2,14,1536]{2,1,0:T(8,128)(2,1)S(1)} collective-permute-done((bf16[2,14,1536]{2,1,0:T(8,128)(2,1)S(1)}, bf16[2,14,1536]{2,1,0:T(8,128)(2,1)S(1)}, u32[]{:S(2)}, u32[]{:S(2)}) %collective-permute-start.1) | collective-permute-done | bytes 86048 | tf_op jit(solution)/shard_map/ppermute | solution.py:40
  38.8 2.2 %collective-permute-start.4 = (bf16[384,384]{1,0:T(8,128)(2,1)S(1)}, bf16[384,384]{1,0:T(8,128)(2,1)S(1)}, u32[]{:S(2)}, u32[]{:S(2)}) collective-permute-start(bf16[384,384]{1,0:T(8,128)(2,1)S(1)} %pad_maximum_fusion.2), channel_id=1, source_target_pairs={{0,128},{4,132},{8,136},{12,140},{16,144},{20,148},{24,152},{28,15... | collective-permute-start | bytes 884744 | tf_op jit(solution)/shard_map/ppermute | solution.py:40
  40.9 3.8 %collective-permute-start.5 = (bf16[384,384]{1,0:T(8,128)(2,1)S(1)}, bf16[384,384]{1,0:T(8,128)(2,1)S(1)}, u32[]{:S(2)}, u32[]{:S(2)}) collective-permute-start(bf16[384,384]{1,0:T(8,128)(2,1)S(1)} %pad_maximum_fusion.2), channel_id=1, source_target_pairs={{128,256},{132,260},{136,264},{140,268},{144,272},{148,276},{152,2... | collective-permute-start | bytes 884744 | tf_op jit(solution)/shard_map/ppermute | solution.py:40
  44.9 4.0 %collective-permute-done.4 = bf16[384,384]{1,0:T(8,128)(2,1)S(1)} collective-permute-done((bf16[384,384]{1,0:T(8,128)(2,1)S(1)}, bf16[384,384]{1,0:T(8,128)(2,1)S(1)}, u32[]{:S(2)}, u32[]{:S(2)}) %collective-permute-start.4) | collective-permute-done | bytes 294944 | tf_op jit(solution)/shard_map/ppermute | solution.py:40
  48.8 2.6 %collective-permute-done.5 = bf16[384,384]{1,0:T(8,128)(2,1)S(1)} collective-permute-done((bf16[384,384]{1,0:T(8,128)(2,1)S(1)}, bf16[384,384]{1,0:T(8,128)(2,1)S(1)}, u32[]{:S(2)}, u32[]{:S(2)}) %collective-permute-start.5) | collective-permute-done | bytes 294944 | tf_op jit(solution)/shard_map/ppermute | solution.py:40
  51.5 1.7 broadcast_in_dim.30
  53.2 6.5 %all-to-all-start = ((bf16[16,56,1536]{2,1,0:T(8,128)(2,1)}), bf16[16,56,1536]{2,1,0:T(8,128)(2,1)S(1)}, u32[]{:S(2)}, u32[]{:S(2)}) async-start(bf16[16,56,1536]{2,1,0:T(8,128)(2,1)} %broadcast_in_dim.30), calls=%async_computation | async-start | bytes 5505024 | tf_op jit(solution)/shard_map/all_to_all | solution.py:68
  59.7 1.9 collective-permute-start.6
  61.6 1.9 collective-permute-start.7
  63.5 5.2 %collective-permute-start.8 = (bf16[576,384]{1,0:T(8,128)(2,1)S(1)}, bf16[576,384]{1,0:T(8,128)(2,1)S(1)}, u32[]{:S(2)}, u32[]{:S(2)}) collective-permute-start(bf16[576,384]{1,0:T(8,128)(2,1)S(1)} %pad_maximum_fusion.1.p0), channel_id=1, source_target_pairs={{0,3},{1,0},{2,1},{3,2},{4,7},{5,4},{6,5},{7,6},{8,11},{9,8},{10,9... | collective-permute-start | bytes 1327112 | tf_op jit(solution)/shard_map/ppermute | solution.py:257
  68.7 4.2 %collective-permute-done.6.p1 = bf16[576,384]{1,0:T(8,128)(2,1)S(1)} collective-permute-done((bf16[576,384]{1,0:T(8,128)(2,1)S(1)}, bf16[576,384]{1,0:T(8,128)(2,1)S(1)}, u32[]{:S(2)}, u32[]{:S(2)}) %collective-permute-start.6) | collective-permute-done | bytes 442400 | tf_op jit(solution)/shard_map/ppermute | solution.py:257
  72.9 0.8 copy-done.7
  73.7 20.8 %collective-permute-done.7.p2 = bf16[576,384]{1,0:T(8,128)(2,1)S(1)} collective-permute-done((bf16[576,384]{1,0:T(8,128)(2,1)S(1)}, bf16[576,384]{1,0:T(8,128)(2,1)S(1)}, u32[]{:S(2)}, u32[]{:S(2)}) %collective-permute-start.7) | collective-permute-done | bytes 442400 | tf_op jit(solution)/shard_map/ppermute | solution.py:257
  94.5 0.8 copy-done.10
  95.2 0.8 copy-done.13
  96.0 2.5 %collective-permute-start.9 = (bf16[896,1536]{1,0:T(8,128)(2,1)S(1)}, bf16[896,1536]{1,0:T(8,128)(2,1)}, u32[]{:S(2)}, u32[]{:S(2)}) collective-permute-start(bf16[896,1536]{1,0:T(8,128)(2,1)S(1)} %bitcast.36), channel_id=1, source_target_pairs={{0,4},{4,0},{8,12},{12,8},{16,20},{20,16},{24,28},{28,24},{32,36},... | collective-permute-start | bytes 8257544 | tf_op jit(solution)/shard_map/ppermute | solution.py:40
  99.1 0.2 fusion.3
  99.2 1.1 copy-done.3
  100.4 1.1 copy-done.5
  101.4 1.0 copy-done.8
  102.4 1.0 copy-done.11
  103.5 1.0 copy-done.14
  104.5 4.2 %shard_map.131 = (f32[192,1152]{1,0:T(8,128)S(1)}, f32[192,384]{1,0:T(8,128)S(1)}, f32[576,768]{1,0:T(8,128)S(1)}) custom-call(s32[6]{0:T(128)S(1)} %stack.53.flags, bf16[192,1536]{1,0:T(8,128)(2,1)S(1)} %copy-done.3, bf16[192,1536]{1,0:T(8,128)(2,1)S(1)} %copy-done.5, bf16[576,384]{1,0:T(8,128)(2,1)S(1)} %pad_maximum_fusion.1.p0, ...), custom_call_target="tpu_custom_call" | custom-call | flops 1000000000 | bytes 8000000 | tf_op jit(solution)/shard_map/pallas_call | solution.py:308
  108.7 1.2 pad_maximum_fusion
  110.0 0.1 copy-done.9
  110.1 0.1 copy-done.12
  110.3 0.1 copy-done.15
  110.4 12.3 %shard_map.132 = (bf16[192,384]{1,0:T(8,128)(2,1)S(1)}, bf16[192,384]{1,0:T(8,128)(2,1)S(1)}, bf16[384,768]{1,0:T(8,128)(2,1)S(1)}, bf16[384,768]{1,0:T(8,128)(2...) custom-call(s32[6]{0:T(128)S(1)} %copy-done.23, bf16[192,1536]{1,0:T(8,128)(2,1)S(1)} %copy-done.4, ...), custom_call_target="tpu_custom_call" | custom-call | flops 1000000000 | bytes 8000000 | tf_op jit(solution)/shard_map/pallas_call | solution.py:315
  122.7 0.8 copy-done.16
  123.5 0.7 copy-done.18
  124.3 0.7 copy-done.20
  124.9 2.2 %collective-permute-start.10 = (bf16[384,768]{1,0:T(8,128)(2,1)}, bf16[384,768]{1,0:T(8,128)(2,1)}, u32[]{:S(2)}, u32[]{:S(2)}) collective-permute-start(bf16[384,768]{1,0:T(8,128)(2,1)} %get-tuple-element.33), channel_id=1, source_target_pairs={{0,128},{4,132},{8,136},{12,140},{16,144},{20,148},{24,152},{28,15... | collective-permute-start | bytes 1769480 | tf_op jit(solution)/shard_map/ppermute | solution.py:40
  127.1 3.7 %collective-permute-start.11 = (bf16[384,768]{1,0:T(8,128)(2,1)}, bf16[384,768]{1,0:T(8,128)(2,1)}, u32[]{:S(2)}, u32[]{:S(2)}) collective-permute-start(bf16[384,768]{1,0:T(8,128)(2,1)} %get-tuple-element.34), channel_id=1, source_target_pairs={{128,256},{132,260},{136,264},{140,268},{144,272},{148,276},{152,2... | collective-permute-start | bytes 1769480 | tf_op jit(solution)/shard_map/ppermute | solution.py:40
  130.9 0.9 copy-done.2
  131.8 0.9 copy-done.21
  132.7 3.8 %shard_map.133 = (bf16[4,192,384]{2,1,0:T(8,128)(2,1)S(1)}, f32[2,4,192,224]{3,2,1,0:T(8,128)S(1)}) custom-call(bf16[192,384]{1,0:T(8,128)(2,1)S(1)} %get-tuple-element.36.att, bf16[192,384]{1,0:T(8,128)(2,1)S(1)} %copy-done.21, bf16[896,1536]{1,0:T(8,128)(2,1)S(1)} %bitcast.40, bf16[896,1536]{1,0:T(8,128)(2,1)} %collective-permute-done.9.wt, ...), custom_call_target="tpu_custom_call" | custom-call | flops 1000000000 | bytes 8000000 | tf_op jit(solution)/shard_map/pallas_call | solution.py:332
  136.6 5.5 %collective-permute-done.10 = bf16[384,768]{1,0:T(8,128)(2,1)} collective-permute-done((bf16[384,768]{1,0:T(8,128)(2,1)}, bf16[384,768]{1,0:T(8,128)(2,1)}, u32[]{:S(2)}, u32[]{:S(2)}) %collective-permute-start.10) | collective-permute-done | bytes 589856 | tf_op jit(solution)/shard_map/ppermute | solution.py:40
  142.1 2.5 %collective-permute-done.11 = bf16[384,768]{1,0:T(8,128)(2,1)} collective-permute-done((bf16[384,768]{1,0:T(8,128)(2,1)}, bf16[384,768]{1,0:T(8,128)(2,1)}, u32[]{:S(2)}, u32[]{:S(2)}) %collective-permute-start.11) | collective-permute-done | bytes 589856 | tf_op jit(solution)/shard_map/ppermute | solution.py:40
  144.6 1.2 broadcast_select_fusion
  145.9 2.7 %collective-permute-start.12 = (bf16[192,768]{1,0:T(8,128)(2,1)S(1)}, bf16[192,768]{1,0:T(8,128)(2,1)S(1)}, u32[]{:S(2)}, u32[]{:S(2)}) collective-permute-start(bf16[192,768]{1,0:T(8,128)(2,1)S(1)} %get-tuple-element.45), channel_id=1, source_target_pairs={{0,4},{4,0},{8,12},{12,8},{16,20},{20,16},{24,28},{28,24},{32,36},... | collective-permute-start | bytes 884744 | tf_op jit(solution)/shard_map/ppermute | solution.py:40
  148.6 3.8 %collective-permute-start.13 = (bf16[192,768]{1,0:T(8,128)(2,1)S(1)}, bf16[192,768]{1,0:T(8,128)(2,1)S(1)}, u32[]{:S(2)}, u32[]{:S(2)}) collective-permute-start(bf16[192,768]{1,0:T(8,128)(2,1)S(1)} %get-tuple-element.44), channel_id=1, source_target_pairs={{4,8},{8,4},{12,16},{16,12},{20,24},{24,20},{28,32},{32,28},{36,40... | collective-permute-start | bytes 884744 | tf_op jit(solution)/shard_map/ppermute | solution.py:40
  152.4 10.8 %collective-permute-start.14 = (bf16[192,384]{1,0:T(8,128)(2,1)S(1)}, bf16[192,384]{1,0:T(8,128)(2,1)S(1)}, u32[]{:S(2)}, u32[]{:S(2)}) collective-permute-start(bf16[192,384]{1,0:T(8,128)(2,1)S(1)} %get-tuple-element.51), channel_id=1, source_target_pairs={{0,1},{1,2},{2,3},{3,0},{4,5},{5,6},{6,7},{7,4},{8,9},{9,10},{10,1... | collective-permute-start | bytes 442376 | tf_op jit(solution)/shard_map/ppermute | solution.py:257
  163.2 1.9 collective-permute-start.15
  165.2 4.0 %collective-permute-start.16 = (bf16[192,384]{1,0:T(8,128)(2,1)S(1)}, bf16[192,384]{1,0:T(8,128)(2,1)S(1)}, u32[]{:S(2)}, u32[]{:S(2)}) collective-permute-start(bf16[192,384]{1,0:T(8,128)(2,1)S(1)} %get-tuple-element.49), channel_id=1, source_target_pairs={{0,3},{1,0},{2,1},{3,2},{4,7},{5,4},{6,5},{7,6},{8,11},{9,8},{10,9... | collective-permute-start | bytes 442376 | tf_op jit(solution)/shard_map/ppermute | solution.py:257
  169.2 1.2 convert_add_fusion.own
  170.3 1.8 collective-permute-done.14.o1
  172.1 4.1 %collective-permute-done.15.o2 = bf16[192,384]{1,0:T(8,128)(2,1)S(1)} collective-permute-done((bf16[192,384]{1,0:T(8,128)(2,1)S(1)}, bf16[192,384]{1,0:T(8,128)(2,1)S(1)}, u32[]{:S(2)}, u32[]{:S(2)}) %collective-permute-start.15) | collective-permute-done | bytes 147488 | tf_op jit(solution)/shard_map/ppermute | solution.py:257
  176.3 3.2 %collective-permute-done.16.o3 = bf16[192,384]{1,0:T(8,128)(2,1)S(1)} collective-permute-done((bf16[192,384]{1,0:T(8,128)(2,1)S(1)}, bf16[192,384]{1,0:T(8,128)(2,1)S(1)}, u32[]{:S(2)}, u32[]{:S(2)}) %collective-permute-start.16) | collective-permute-done | bytes 147488 | tf_op jit(solution)/shard_map/ppermute | solution.py:257
  179.5 4.4 %shard_map.134 = (bf16[4,192,384]{2,1,0:T(8,128)(2,1)S(1)}, bf16[192,384]{1,0:T(8,128)(2,1)}) custom-call(f32[192,768]{1,0:T(8,128)S(1)} %convert_add_fusion.own, bf16[192,768]{1,0:T(8,128)(2,1)S(1)} %collective-permute-done.12.in_a, bf16[192,768]{1,0:T(8,128)(2,1)S(1)} %collective-permute-done.13.in_b, f32[192,384]{1,0:T(8,128)S(1)} %copy-done.19, ...), custom_call_target="tpu_custom_call" | custom-call | flops 1000000000 | bytes 8000000 | tf_op jit(solution)/shard_map/pallas_call | solution.py:341
  183.9 6.1 %collective-permute-start.17 = (bf16[192,384]{1,0:T(8,128)(2,1)S(1)}, bf16[192,384]{1,0:T(8,128)(2,1)S(1)}, u32[]{:S(2)}, u32[]{:S(2)}) collective-permute-start(bf16[192,384]{1,0:T(8,128)(2,1)S(1)} %get-tuple-element.46), channel_id=1, source_target_pairs={{0,1},{1,2},{2,3},{3,0},{4,5},{5,6},{6,7},{7,4},{8,9},{9,10},{10,1... | collective-permute-start | bytes 442376 | tf_op jit(solution)/shard_map/ppermute | solution.py:257
  190.0 4.7 %collective-permute-start.18 = (bf16[192,384]{1,0:T(8,128)(2,1)S(1)}, bf16[192,384]{1,0:T(8,128)(2,1)S(1)}, u32[]{:S(2)}, u32[]{:S(2)}) collective-permute-start(bf16[192,384]{1,0:T(8,128)(2,1)S(1)} %get-tuple-element.48), channel_id=1, source_target_pairs={{0,2},{1,3},{2,0},{3,1},{4,6},{5,7},{6,4},{7,5},{8,10},{9,11},{10,... | collective-permute-start | bytes 442376 | tf_op jit(solution)/shard_map/ppermute | solution.py:257
  194.7 1.9 collective-permute-start.19
  196.6 4.7 %collective-permute-done.18 = bf16[192,384]{1,0:T(8,128)(2,1)S(1)} collective-permute-done((bf16[192,384]{1,0:T(8,128)(2,1)S(1)}, bf16[192,384]{1,0:T(8,128)(2,1)S(1)}, u32[]{:S(2)}, u32[]{:S(2)}) %collective-permute-start.18) | collective-permute-done | bytes 147488 | tf_op jit(solution)/shard_map/ppermute | solution.py:257
  201.4 2.4 %collective-permute-done.19 = bf16[192,384]{1,0:T(8,128)(2,1)S(1)} collective-permute-done((bf16[192,384]{1,0:T(8,128)(2,1)S(1)}, bf16[192,384]{1,0:T(8,128)(2,1)S(1)}, u32[]{:S(2)}, u32[]{:S(2)}) %collective-permute-start.19) | collective-permute-done | bytes 147488 | tf_op jit(solution)/shard_map/ppermute | solution.py:257
  203.7 0.7 fusion.6
  (71 shorter events, 1.0 us)
Async XLA Ops:
  0.6 15.5 %copy-start = (s32[128,2]{0,1:T(2,128)S(1)}, s32[128,2]{0,1:T(2,128)}, u32[]{:S(2)}) copy-start(s32[128,2]{0,1:T(2,128)} %param.21) | copy-start | bytes 3076
  1.6 37.1 %collective-permute-start.2 = (bf16[192,384]{1,0:T(8,128)(2,1)S(1)}, bf16[192,384]{1,0:T(8,128)(2,1)S(1)}, u32[]{:S(2)}, u32[]{:S(2)}) collective-permute-start(bf16[192,384]{1,0:T(8,128)(2,1)S(1)} %constant_dynamic-slice_fusion), channel_id=1, source_target_pairs={{0,4},{4,0},{8,12},{12,8},{16,20},{20,16},{24,28},{28,24},{32,36},... | collective-permute-start | bytes 442376 | tf_op jit(solution)/shard_map/ppermute | solution.py:40
  4.2 34.5 %collective-permute-start.3 = (bf16[192,384]{1,0:T(8,128)(2,1)S(1)}, bf16[192,384]{1,0:T(8,128)(2,1)S(1)}, u32[]{:S(2)}, u32[]{:S(2)}) collective-permute-start(bf16[192,384]{1,0:T(8,128)(2,1)S(1)} %constant_dynamic-slice_fusion), channel_id=1, source_target_pairs={{4,8},{8,4},{12,16},{16,12},{20,24},{24,20},{28,32},{32,28},{36,40... | collective-permute-start | bytes 442376 | tf_op jit(solution)/shard_map/ppermute | solution.py:40
  13.4 9.0 %collective-permute-start = (bf16[14,1536]{1,0:T(8,128)(2,1)S(1)}, bf16[14,1536]{1,0:T(8,128)(2,1)S(1)}, u32[]{:S(2)}, u32[]{:S(2)}) collective-permute-start(bf16[14,1536]{1,0:T(8,128)(2,1)S(1)} %pad_maximum_fusion.6), channel_id=1, source_target_pairs={{0,32},{4,36},{8,40},{12,44},{16,48},{20,52},{24,56},{28,60},{32,0... | collective-permute-start | bytes 129032 | tf_op jit(solution)/shard_map/ppermute | solution.py:40
  22.4 16.2 %collective-permute-start.1 = (bf16[2,14,1536]{2,1,0:T(8,128)(2,1)S(1)}, bf16[2,14,1536]{2,1,0:T(8,128)(2,1)S(1)}, u32[]{:S(2)}, u32[]{:S(2)}) collective-permute-start(bf16[2,14,1536]{2,1,0:T(8,128)(2,1)S(1)} %pad_maximum_fusion.5), channel_id=1, source_target_pairs={{0,96},{4,100},{8,104},{12,108},{16,112},{20,116},{24,120},{28,124... | collective-permute-start | bytes 258056 | tf_op jit(solution)/shard_map/ppermute | solution.py:40
  38.8 10.1 %collective-permute-start.4 = (bf16[384,384]{1,0:T(8,128)(2,1)S(1)}, bf16[384,384]{1,0:T(8,128)(2,1)S(1)}, u32[]{:S(2)}, u32[]{:S(2)}) collective-permute-start(bf16[384,384]{1,0:T(8,128)(2,1)S(1)} %pad_maximum_fusion.2), channel_id=1, source_target_pairs={{0,128},{4,132},{8,136},{12,140},{16,144},{20,148},{24,152},{28,15... | collective-permute-start | bytes 884744 | tf_op jit(solution)/shard_map/ppermute | solution.py:40
  40.9 10.5 %collective-permute-start.5 = (bf16[384,384]{1,0:T(8,128)(2,1)S(1)}, bf16[384,384]{1,0:T(8,128)(2,1)S(1)}, u32[]{:S(2)}, u32[]{:S(2)}) collective-permute-start(bf16[384,384]{1,0:T(8,128)(2,1)S(1)} %pad_maximum_fusion.2), channel_id=1, source_target_pairs={{128,256},{132,260},{136,264},{140,268},{144,272},{148,276},{152,2... | collective-permute-start | bytes 884744 | tf_op jit(solution)/shard_map/ppermute | solution.py:40
  53.2 45.4 %copy-start.24 = (f32[384]{0:T(512)S(1)}, f32[384]{0:T(512)}, u32[]{:S(2)}) copy-start(f32[384]{0:T(512)} %param.19) | copy-start | bytes 4612
  53.2 45.4 %copy-start.25 = (f32[384]{0:T(512)S(1)}, f32[384]{0:T(512)}, u32[]{:S(2)}) copy-start(f32[384]{0:T(512)} %param.18) | copy-start | bytes 4612
  53.2 45.5 %copy-start.26 = (s32[256]{0:T(256)S(1)}, s32[256]{0:T(256)}, u32[]{:S(2)}) copy-start(s32[256]{0:T(256)} %param.20) | copy-start | bytes 3076
  53.2 42.8 %all-to-all-start = ((bf16[16,56,1536]{2,1,0:T(8,128)(2,1)}), bf16[16,56,1536]{2,1,0:T(8,128)(2,1)S(1)}, u32[]{:S(2)}, u32[]{:S(2)}) async-start(bf16[16,56,1536]{2,1,0:T(8,128)(2,1)} %broadcast_in_dim.30), calls=%async_computation | async-start | bytes 5505024 | tf_op jit(solution)/shard_map/all_to_all | solution.py:68
  59.7 13.2 %collective-permute-start.6 = (bf16[576,384]{1,0:T(8,128)(2,1)S(1)}, bf16[576,384]{1,0:T(8,128)(2,1)S(1)}, u32[]{:S(2)}, u32[]{:S(2)}) collective-permute-start(bf16[576,384]{1,0:T(8,128)(2,1)S(1)} %pad_maximum_fusion.1.p0), channel_id=1, source_target_pairs={{0,1},{1,2},{2,3},{3,0},{4,5},{5,6},{6,7},{7,4},{8,9},{9,10},{10,1... | collective-permute-start | bytes 1327112 | tf_op jit(solution)/shard_map/ppermute | solution.py:257
  61.6 32.9 %collective-permute-start.7 = (bf16[576,384]{1,0:T(8,128)(2,1)S(1)}, bf16[576,384]{1,0:T(8,128)(2,1)S(1)}, u32[]{:S(2)}, u32[]{:S(2)}) collective-permute-start(bf16[576,384]{1,0:T(8,128)(2,1)S(1)} %pad_maximum_fusion.1.p0), channel_id=1, source_target_pairs={{0,2},{1,3},{2,0},{3,1},{4,6},{5,7},{6,4},{7,5},{8,10},{9,11},{10,... | collective-permute-start | bytes 1327112 | tf_op jit(solution)/shard_map/ppermute | solution.py:257
  63.5 31.7 %collective-permute-start.8 = (bf16[576,384]{1,0:T(8,128)(2,1)S(1)}, bf16[576,384]{1,0:T(8,128)(2,1)S(1)}, u32[]{:S(2)}, u32[]{:S(2)}) collective-permute-start(bf16[576,384]{1,0:T(8,128)(2,1)S(1)} %pad_maximum_fusion.1.p0), channel_id=1, source_target_pairs={{0,3},{1,0},{2,1},{3,2},{4,7},{5,4},{6,5},{7,6},{8,11},{9,8},{10,9... | collective-permute-start | bytes 1327112 | tf_op jit(solution)/shard_map/ppermute | solution.py:257
  72.9 0.8 copy-start.7
  94.5 0.8 copy-start.10
  95.2 0.8 copy-start.13
  96.0 12.6 %collective-permute-start.9 = (bf16[896,1536]{1,0:T(8,128)(2,1)S(1)}, bf16[896,1536]{1,0:T(8,128)(2,1)}, u32[]{:S(2)}, u32[]{:S(2)}) collective-permute-start(bf16[896,1536]{1,0:T(8,128)(2,1)S(1)} %bitcast.36), channel_id=1, source_target_pairs={{0,4},{4,0},{8,12},{12,8},{16,20},{20,16},{24,28},{28,24},{32,36},... | collective-permute-start | bytes 8257544 | tf_op jit(solution)/shard_map/ppermute | solution.py:40
  99.0 9.7 %copy-start.22 = (s32[6]{0:T(128)}, s32[6]{0:T(128)S(1)}, u32[]{:S(2)}) copy-start(s32[6]{0:T(128)S(1)} %stack.53.flags) | copy-start | bytes 76
  99.2 10.8 %copy-start.1 = (bf16[384,224]{1,0:T(8,128)(2,1)}, bf16[384,224]{1,0:T(8,128)(2,1)S(1)}, u32[]{:S(2)}) copy-start(bf16[384,224]{1,0:T(8,128)(2,1)S(1)} %get-tuple-element.55.pick_t) | copy-start | bytes 516100
  99.2 1.1 copy-start.3
  100.4 1.1 copy-start.5
  101.4 1.0 copy-start.8
  102.4 1.0 copy-start.11
  103.5 1.0 copy-start.14
  108.7 1.3 copy-start.4
  108.7 1.4 copy-start.6
  108.7 1.5 copy-start.9
  108.7 1.6 copy-start.12
  108.7 1.7 copy-start.15
  108.7 1.7 copy-start.23
  122.7 0.8 copy-start.16
  123.5 0.7 copy-start.18
  124.3 0.7 copy-start.20
  124.9 17.2 %collective-permute-start.10 = (bf16[384,768]{1,0:T(8,128)(2,1)}, bf16[384,768]{1,0:T(8,128)(2,1)}, u32[]{:S(2)}, u32[]{:S(2)}) collective-permute-start(bf16[384,768]{1,0:T(8,128)(2,1)} %get-tuple-element.33), channel_id=1, source_target_pairs={{0,128},{4,132},{8,136},{12,140},{16,144},{20,148},{24,152},{28,15... | collective-permute-start | bytes 1769480 | tf_op jit(solution)/shard_map/ppermute | solution.py:40
  127.1 17.5 %collective-permute-start.11 = (bf16[384,768]{1,0:T(8,128)(2,1)}, bf16[384,768]{1,0:T(8,128)(2,1)}, u32[]{:S(2)}, u32[]{:S(2)}) collective-permute-start(bf16[384,768]{1,0:T(8,128)(2,1)} %get-tuple-element.34), channel_id=1, source_target_pairs={{128,256},{132,260},{136,264},{140,268},{144,272},{148,276},{152,2... | collective-permute-start | bytes 1769480 | tf_op jit(solution)/shard_map/ppermute | solution.py:40
  130.9 0.9 copy-start.2
  131.8 0.9 copy-start.21
  132.7 11.9 %copy-start.17 = (bf16[384,768]{1,0:T(8,128)(2,1)S(1)}, bf16[384,768]{1,0:T(8,128)(2,1)}, u32[]{:S(2)}) copy-start(bf16[384,768]{1,0:T(8,128)(2,1)} %copy-done.16) | copy-start | bytes 1769476
  136.6 42.9 %copy-start.19 = (f32[192,384]{1,0:T(8,128)S(1)}, f32[192,384]{1,0:T(8,128)}, u32[]{:S(2)}) copy-start(f32[192,384]{1,0:T(8,128)} %copy-done.18) | copy-start | bytes 884740
  145.9 33.6 %collective-permute-start.12 = (bf16[192,768]{1,0:T(8,128)(2,1)S(1)}, bf16[192,768]{1,0:T(8,128)(2,1)S(1)}, u32[]{:S(2)}, u32[]{:S(2)}) collective-permute-start(bf16[192,768]{1,0:T(8,128)(2,1)S(1)} %get-tuple-element.45), channel_id=1, source_target_pairs={{0,4},{4,0},{8,12},{12,8},{16,20},{20,16},{24,28},{28,24},{32,36},... | collective-permute-start | bytes 884744 | tf_op jit(solution)/shard_map/ppermute | solution.py:40
  148.6 30.9 %collective-permute-start.13 = (bf16[192,768]{1,0:T(8,128)(2,1)S(1)}, bf16[192,768]{1,0:T(8,128)(2,1)S(1)}, u32[]{:S(2)}, u32[]{:S(2)}) collective-permute-start(bf16[192,768]{1,0:T(8,128)(2,1)S(1)} %get-tuple-element.44), channel_id=1, source_target_pairs={{4,8},{8,4},{12,16},{16,12},{20,24},{24,20},{28,32},{32,28},{36,40... | collective-permute-start | bytes 884744 | tf_op jit(solution)/shard_map/ppermute | solution.py:40
  152.4 19.7 %collective-permute-start.14 = (bf16[192,384]{1,0:T(8,128)(2,1)S(1)}, bf16[192,384]{1,0:T(8,128)(2,1)S(1)}, u32[]{:S(2)}, u32[]{:S(2)}) collective-permute-start(bf16[192,384]{1,0:T(8,128)(2,1)S(1)} %get-tuple-element.51), channel_id=1, source_target_pairs={{0,1},{1,2},{2,3},{3,0},{4,5},{5,6},{6,7},{7,4},{8,9},{9,10},{10,1... | collective-permute-start | bytes 442376 | tf_op jit(solution)/shard_map/ppermute | solution.py:257
  163.2 13.0 %collective-permute-start.15 = (bf16[192,384]{1,0:T(8,128)(2,1)S(1)}, bf16[192,384]{1,0:T(8,128)(2,1)S(1)}, u32[]{:S(2)}, u32[]{:S(2)}) collective-permute-start(bf16[192,384]{1,0:T(8,128)(2,1)S(1)} %get-tuple-element.50), channel_id=1, source_target_pairs={{0,2},{1,3},{2,0},{3,1},{4,6},{5,7},{6,4},{7,5},{8,10},{9,11},{10,... | collective-permute-start | bytes 442376 | tf_op jit(solution)/shard_map/ppermute | solution.py:257
  165.2 14.3 %collective-permute-start.16 = (bf16[192,384]{1,0:T(8,128)(2,1)S(1)}, bf16[192,384]{1,0:T(8,128)(2,1)S(1)}, u32[]{:S(2)}, u32[]{:S(2)}) collective-permute-start(bf16[192,384]{1,0:T(8,128)(2,1)S(1)} %get-tuple-element.49), channel_id=1, source_target_pairs={{0,3},{1,0},{2,1},{3,2},{4,7},{5,4},{6,5},{7,6},{8,11},{9,8},{10,9... | collective-permute-start | bytes 442376 | tf_op jit(solution)/shard_map/ppermute | solution.py:257
  183.9 12.7 %collective-permute-start.17 = (bf16[192,384]{1,0:T(8,128)(2,1)S(1)}, bf16[192,384]{1,0:T(8,128)(2,1)S(1)}, u32[]{:S(2)}, u32[]{:S(2)}) collective-permute-start(bf16[192,384]{1,0:T(8,128)(2,1)S(1)} %get-tuple-element.46), channel_id=1, source_target_pairs={{0,1},{1,2},{2,3},{3,0},{4,5},{5,6},{6,7},{7,4},{8,9},{9,10},{10,1... | collective-permute-start | bytes 442376 | tf_op jit(solution)/shard_map/ppermute | solution.py:257
  190.0 11.4 %collective-permute-start.18 = (bf16[192,384]{1,0:T(8,128)(2,1)S(1)}, bf16[192,384]{1,0:T(8,128)(2,1)S(1)}, u32[]{:S(2)}, u32[]{:S(2)}) collective-permute-start(bf16[192,384]{1,0:T(8,128)(2,1)S(1)} %get-tuple-element.48), channel_id=1, source_target_pairs={{0,2},{1,3},{2,0},{3,1},{4,6},{5,7},{6,4},{7,5},{8,10},{9,11},{10,... | collective-permute-start | bytes 442376 | tf_op jit(solution)/shard_map/ppermute | solution.py:257
  194.7 9.0 %collective-permute-start.19 = (bf16[192,384]{1,0:T(8,128)(2,1)S(1)}, bf16[192,384]{1,0:T(8,128)(2,1)S(1)}, u32[]{:S(2)}, u32[]{:S(2)}) collective-permute-start(bf16[192,384]{1,0:T(8,128)(2,1)S(1)} %get-tuple-element.47), channel_id=1, source_target_pairs={{0,3},{1,0},{2,1},{3,2},{4,7},{5,4},{6,5},{7,6},{8,11},{9,8},{10,9... | collective-permute-start | bytes 442376 | tf_op jit(solution)/shard_map/ppermute | solution.py:257

commit v4 on v3

v4 whole, which is shorter than its diff:
```python
import functools

import jax
import jax.numpy as jnp
from jax import lax
from jax.experimental import pallas as pl
from jax.experimental.pallas import tpu as pltpu
from jax.sharding import PartitionSpec as P

HD = 128
NH = 3
W = NH * HD
ROWS = 192
TEXT = 256
EPS = 1e-6
SCALE = HD**-0.5
OUT_COST = 10**9
GRAD_COST = 10**9
BLOCK = 56
PART = 4 * BLOCK
F32 = jnp.float32
BF16 = jnp.bfloat16
NT = (((1,), (1,)), ((), ()))
TN = (((0,), (0,)), ((), ()))


def place_of(x, zh, y, core):
    return ((x * 4 + zh) * 4 + y) * 2 + core


def all_places():
    return [(x, z, y, c) for x in range(4) for z in range(4) for y in range(4) for c in range(2)]


def seq_move(value, target):
    pairs = []
    for at in all_places():
        to = target(*at)
        if to is not None:
            pairs.append((place_of(*at), place_of(*to)))
    return lax.ppermute(value, "seq", pairs)


def core_mate(value):
    return seq_move(value, lambda x, z, y, c: (x, z, y, 1 - c))


def next_chip(value):
    def target(x, z, y, c):
        col = (z * 4 + y) * 2 + c
        col = col + 1 if c == 1 else col - 1
        if not 0 <= col < 32:
            return None
        return (x, col // 8, col // 2 % 4, col % 2)

    return seq_move(value, target)


def row_even(value):
    return seq_move(value, lambda x, z, y, c: (x ^ 1, z, y, c))


def row_odd(value):
    return seq_move(value, lambda x, z, y, c: (3 - x, z, y, c) if x in (1, 2) else None)


def give_all(value, groups):
    copies = jnp.broadcast_to(value[None], (len(groups[0]),) + value.shape)
    return lax.all_to_all(copies, "seq", 0, 0, axis_index_groups=groups)


def over_zh(value):
    four = range(4)
    return give_all(
        value,
        [[place_of(x, z, y, c) for z in four] for x in four for y in four for c in range(2)],
    )


def over_xy(value):
    four = range(4)
    return give_all(
        value,
        [[place_of(x, z, y, c) for x in four for y in four] for z in four for c in range(2)],
    )


def dot(a, b, dims=(((1,), (0,)), ((), ()))):
    return lax.dot_general(a, b, dims, preferred_element_type=F32)


def norm_rows(a, gain):
    r = lax.rsqrt(jnp.mean(a * a, axis=-1, keepdims=True) + EPS)
    return a * r * gain


def norm_pull(a, gain, dy):
    r = lax.rsqrt(jnp.mean(a * a, axis=-1, keepdims=True) + EPS)
    t = dy * gain
    return r * t - a * (r * r * r * jnp.mean(t * a, axis=-1, keepdims=True))


def head(h):
    return slice(h * HD, (h + 1) * HD)


def val(h):
    return slice(W + h * HD, W + (h + 1) * HD)


def call(kernel, outs, spaces, scratch=(), mib=16, flops=10**9):
    place = {"s": pltpu.SMEM, "h": pltpu.HBM, "v": pltpu.VMEM}
    return pl.pallas_call(
        kernel,
        out_shape=outs,
        in_specs=[pl.BlockSpec(memory_space=place[space]) for space in spaces],
        scratch_shapes=scratch,
        compiler_params=pltpu.CompilerParams(vmem_limit_bytes=mib * 2**20),
        cost_estimate=pl.CostEstimate(flops=flops, bytes_accessed=8 * 10**6, transcendentals=0),
    )


def shape(dims, dtype):
    return jax.ShapeDtypeStruct(dims, dtype)


KVQ = slice(0, 3 * W)
KV = slice(0, 2 * W)
LAST = slice(3 * W, 4 * W)
HALF_TEXT = TEXT // 2


def pick_rows(rows, pick, out):
    for j in range(4):
        out[j] = dot(rows[:, j * W : (j + 1) * W], pick[...]).astype(BF16)


def pick_kernel(*refs):
    n = (len(refs) - 2) // 3
    pick_o, pick_t = refs[n], refs[n + 1]
    for i in range(n):
        pick_rows(refs[i], pick_o, refs[n + 2 + 2 * i])
        pick_rows(refs[i], pick_t, refs[n + 3 + 2 * i])


def pick_parts_kernel(p0, p1, p2, p3, pick_o, pick_t, out_o, out_t):
    for n, part in enumerate((p0, p1, p2, p3)):
        out_o[n] = dot(part[...], pick_o[...]).astype(BF16)
        out_t[n] = dot(part[...], pick_t[...]).astype(BF16)


def project(picked, w, cols, order=(0, 1, 2, 3)):
    acc = None
    for n, j in enumerate(order):
        if isinstance(j, int):
            rows = w[j * PART : (j + 1) * PART, cols]
        else:
            rows = w[pl.ds(pl.multiple_of(j * PART, PART), PART), cols]
        term = dot(picked[n], rows)
        acc = term if acc is None else acc + term
    return acc


def picked_value(rows, pick):
    return [dot(rows[:, j * W : (j + 1) * W], pick[...]).astype(BF16) for j in range(4)]


def part_order(flags):
    return [flags[2 + n] for n in range(4)]


def first_kernel(
    flags, x, g, f, p, pick_o, pick_t, lines, w, acc_x, acc_g, acc_f, acc_p, acc_t, text
):
    acc_x[...] = project(x, w, KVQ)
    acc_g[...] = project(g, w, LAST)
    acc_f[...] = project(f, w, KV)
    acc_p[...] = project(p, w, KV, part_order(flags))
    t = dot(lines[...], w[...]).astype(BF16)
    acc_t[...] = project(picked_value(t, pick_o), w, KV)
    pick_rows(t, pick_t, text)


def attend_kernel(
    flags,
    x,
    g,
    f,
    p,
    text,
    pick_o,
    pick_t,
    lines,
    wo,
    wt,
    acc_x,
    acc_g,
    acc_f,
    acc_p,
    acc_t,
    q_gain,
    k_gain,
    bias,
    att,
    dq,
    near_t,
    even_t,
    odd_t,
    kraw,
    keys,
):
    n = 4 * ROWS
    mine = acc_x[...] + project(x, wt, KVQ)
    d_att = (acc_g[...] + project(g, wt, LAST)).astype(BF16)
    behind = acc_f[...] + project(f, wt, KV)
    beside = acc_p[...] + project(p, wt, KV, part_order(flags))
    words = acc_t[...] + project(text, wt, KV)
    t = dot(lines[...], wt[...]).astype(BF16)
    more = project(picked_value(t, pick_o), wo, KV) + project(picked_value(t, pick_t), wt, KV)
    kraw[...] = mine[:, :W]
    low = 0
    for values in (mine, beside[:ROWS], behind, beside[ROWS:], words, more):
        high = low + values.shape[0]
        for h in range(NH):
            kn = norm_rows(values[:, head(h)], k_gain[:, head(h)])
            keys[low:high, head(h)] = kn.astype(BF16)
        keys[low:high, W:] = values[:, W : 2 * W].astype(BF16)
        low = high
    even = flags[0].astype(F32)
    odd = 1.0 - even
    for h in range(NH):
        q = mine[:, val(NH + h)]
        qh = norm_rows(q, q_gain[:, head(h)]).astype(BF16)
        dh = d_att[:, head(h)]
        kh = keys[:, head(h)]
        vh = keys[:, val(h)]
        s = dot(qh, kh, NT) * SCALE + bias[...]
        e = jnp.exp(s - jnp.max(s, axis=-1, keepdims=True))
        p_h = e * (1.0 / jnp.sum(e, axis=-1, keepdims=True))
        pb = p_h.astype(BF16)
        att[:, head(h)] = dot(pb, vh).astype(BF16)
        dp = dot(dh, vh, NT)
        ds = (p_h * (dp - jnp.sum(p_h * dp, axis=-1, keepdims=True))).astype(BF16)
        d_q = dot(ds, kh) * SCALE
        dq[:, head(h)] = norm_pull(q, q_gain[:, head(h)], d_q).astype(BF16)
        kt = dot(ds[:, :n], qh, TN) * SCALE
        vt = dot(pb[:, :n], dh, TN)
        for lanes, term in ((head(h), kt), (val(h), vt)):
            near_t[:, lanes] = term[: 2 * ROWS].astype(BF16)
            even_t[:, lanes] = (term[2 * ROWS :] * even).astype(BF16)
            odd_t[:, lanes] = (term[2 * ROWS :] * odd).astype(BF16)


def out_kernel(att, dq, wo, wt, pick_o, pick_t, out, gq):
    for j in range(4):
        rows = slice(j * PART, (j + 1) * PART)
        o = dot(att[...], wo[rows, 3 * W :], NT).astype(BF16)
        t = dot(att[...], wt[rows, 3 * W :], NT).astype(BF16)
        out[j] = (dot(o, pick_o[...], NT) + dot(t, pick_t[...], NT)).astype(BF16)
        gq[0, j] = dot(dq[...], wo[rows, 2 * W : 3 * W], NT)
        gq[1, j] = dot(dq[...], wt[rows, 2 * W : 3 * W], NT)


def term_kernel(flags, near_t, got_even, got_odd, own, to_mate, to_next):
    total = near_t[...].astype(F32) + got_even[...].astype(F32) + got_odd[...].astype(F32)
    own[...] = total[:ROWS]
    mate = flags[1].astype(F32)
    to_mate[...] = (total[ROWS:] * mate).astype(BF16)
    to_next[...] = (total[ROWS:] * (1.0 - mate)).astype(BF16)


def grad_kernel(own, in_a, in_b, kraw, k_gain, gq, wo, wt, pick_o, pick_t, o0, o1, o2, o3, out, res):
    total = own[...] + in_a[...].astype(F32) + in_b[...].astype(F32)
    parts = [
        norm_pull(kraw[:, head(h)], k_gain[:, head(h)], total[:, head(h)]).astype(BF16)
        for h in range(NH)
    ]
    d = jnp.concatenate(parts + [total[:, W:].astype(BF16)], axis=1)
    for j in range(4):
        rows = slice(j * PART, (j + 1) * PART)
        o = (gq[0, j] + dot(d, wo[rows, : 2 * W], NT)).astype(BF16)
        t = (gq[1, j] + dot(d, wt[rows, : 2 * W], NT)).astype(BF16)
        out[j] = (dot(o, pick_o[...], NT) + dot(t, pick_t[...], NT)).astype(BF16)
    res[...] = f32_sum(o0[...], o1[...], o2[...], o3[...]).astype(BF16)


def to_heads(blocks, me):
    def block(to):
        return lax.dynamic_index_in_dim(blocks, to & 3, 0, keepdims=False)

    return [block(me)] + [head_shift(block(me + by), by) for by in (1, 2, 3)]


def f32_sum(*terms):
    total = terms[0].astype(F32)
    for term in terms[1:]:
        total = total + term.astype(F32)
    return total


def head_shift(value, by):
    return lax.ppermute(value, "heads", [(i, (i + by) % 4) for i in range(4)])


def per_device(
    x_tiles, x_text, w_query, w_key, w_value, w_output, q_gain, k_gain, text_mask, windows, grad_out
):
    place = lax.axis_index("seq")
    me = lax.axis_index("heads")
    core, x, col = place & 1, place >> 5, place & 31
    window = lax.dynamic_slice(windows, (place, jnp.int32(0)), (1, 2))
    use_even = (window[0, 0] == x) == ((x & 1) == 0)
    use_core = (window[0, 1] == col) == (core == 0)
    q_gain = q_gain[None, :]
    k_gain = k_gain[None, :]
    blocks = [(me - by) & 3 for by in range(4)]
    flags = jnp.stack([use_even.astype(jnp.int32), use_core.astype(jnp.int32)] + blocks)

    at = jnp.arange(PART, dtype=jnp.int32)
    inner = at % BLOCK
    feature = lax.broadcasted_iota(jnp.int32, (W, PART), 0)

    def pick(which):
        natural = ((inner // 12 * 4 + at // BLOCK) * 2 + which) * 12 + inner % 12
        hit = (feature == natural[None, :]) & (inner < 48)[None, :]
        return hit.astype(BF16)

    pick_o, pick_t = pick(core), pick(1 - core)
    t = jnp.arange(HALF_TEXT, dtype=jnp.int32)
    line = t // 8 * BLOCK + 48 + t % 8
    lines = (line[:, None] == jnp.arange(16 * BLOCK, dtype=jnp.int32)[None, :]).astype(BF16)
    t = jnp.arange(TEXT, dtype=jnp.int32)
    token = place_of(t // 32 % 4, t // 2 % 4, t // 8 % 4, (t // 128) ^ core) * 2 + t % 2
    valid = jnp.sum(jnp.where(t[:, None] == token[None, :], text_mask[:, None], 0), axis=0)
    bias = jnp.concatenate(
        [jnp.zeros((4 * ROWS,), F32), jnp.where(valid == 1, 0.0, -1e30).astype(F32)]
    )[None, :]

    quarter = lax.dynamic_slice(x_tiles, (jnp.int32(0), me * W), (ROWS, W))
    mine = jnp.concatenate([w_key, w_value, w_query, w_output], axis=1)
    four = over_zh(jnp.concatenate([mine, x_text], axis=0))
    behind = jnp.where(use_even, row_even(x_tiles), row_odd(x_tiles))
    side = jnp.where(use_core, core_mate(quarter), next_chip(quarter))
    side, behind, pick_o, pick_t, flags = lax.optimization_barrier(
        (side, behind, pick_o, pick_t, flags)
    )
    corner = jnp.where(use_even, row_even(side), row_odd(side))
    beside = jnp.concatenate([side, corner])
    block = jnp.concatenate([four[:, :12].reshape(48, 1536), four[:, 12:].reshape(8, 1536)], axis=0)
    block, beside, lines, bias = lax.optimization_barrier((block, beside, lines, bias))
    parts = [beside] + [head_shift(beside, by) for by in (1, 2, 3)]
    wo = over_xy(block).reshape(16 * BLOCK, 1536)
    picked = shape((4, ROWS, PART), BF16)
    x_o, x_t, g_o, g_t, f_o, f_t = call(pick_kernel, (picked,) * 6, "v" * 5)(
        x_tiles, grad_out, behind, pick_o, pick_t
    )
    p_o, p_t = call(pick_parts_kernel, (shape((4, 2 * ROWS, PART), BF16),) * 2, "v" * 6)(
        *parts, pick_o, pick_t
    )
    wo, x_o, x_t, g_o, g_t, f_o, f_t, p_o, p_t = lax.optimization_barrier(
        (wo, x_o, x_t, g_o, g_t, f_o, f_t, p_o, p_t)
    )
    wt = core_mate(wo)

    *accs, text = call(
        first_kernel,
        (
            shape((ROWS, 3 * W), F32),
            shape((ROWS, W), F32),
            shape((ROWS, 2 * W), F32),
            shape((2 * ROWS, 2 * W), F32),
            shape((HALF_TEXT, 2 * W), F32),
            shape((4, HALF_TEXT, PART), BF16),
        ),
        "s" + "v" * 8,
    )(flags, x_o, g_o, f_o, p_o, pick_o, pick_t, lines, wo)
    att, dq, near_t, even_t, odd_t, kraw = call(
        attend_kernel,
        (
            shape((ROWS, W), BF16),
            shape((ROWS, W), BF16),
            shape((2 * ROWS, 768), BF16),
            shape((2 * ROWS, 768), BF16),
            shape((2 * ROWS, 768), BF16),
            shape((ROWS, W), F32),
        ),
        "s" + "v" * 18,
        scratch=[pltpu.VMEM((1024, 768), BF16)],
        mib=28,
    )(flags, x_t, g_t, f_t, p_t, text, pick_o, pick_t, lines, wo, wt, *accs, q_gain, k_gain, bias)

    got_even, got_odd = row_even(even_t), row_odd(odd_t)
    out, gq = call(
        out_kernel,
        (shape((4, ROWS, W), BF16), shape((2, 4, ROWS, PART), F32)),
        "v" * 6,
        flops=OUT_COST,
    )(att, dq, wo, wt, pick_o, pick_t)
    outs = to_heads(out, me)
    got_even, got_odd, outs[1], outs[2] = lax.optimization_barrier(
        (got_even, got_odd, outs[1], outs[2])
    )
    own_t, to_mate, to_next = call(
        term_kernel,
        (shape((ROWS, 768), F32), shape((ROWS, 768), BF16), shape((ROWS, 768), BF16)),
        "svvv",
        mib=8,
    )(flags, near_t, got_even, got_odd)
    mate_t, next_t = core_mate(to_mate), next_chip(to_next)
    grad, out_tiles = call(
        grad_kernel,
        (shape((4, ROWS, W), BF16), shape((ROWS, W), BF16)),
        "v" * 14,
        flops=GRAD_COST,
    )(own_t, mate_t, next_t, kraw, k_gain, gq, wo, wt, pick_o, pick_t, *outs)
    grads = lax.all_to_all(grad, "heads", 0, 0)
    return (out_tiles, f32_sum(*[grads[n] for n in range(4)]).astype(BF16))


def solution(mesh):
    in_specs = (
        P("seq", None),
        P("seq", None),
        P("seq", "heads"),
        P("seq", "heads"),
        P("seq", "heads"),
        P("seq", "heads"),
        P("heads"),
        P("heads"),
        P(),
        P(),
        P("seq", None),
    )
    out_specs = (P("seq", "heads"), P("seq", "heads"))
    return jax.shard_map(
        per_device, mesh=mesh, in_specs=in_specs, out_specs=out_specs, check_vma=False
    )
```

time: 206 us -> 191 us (0.927)
  the two profiles are of different devices: /device:TPU:155 before, /device:TPU:25 now
where the time goes in v4:
time: 191 us; the launch traced here: 188 us
  starting transfers between devices  83.3 us (44%)
  waiting for transfers between devices  40.2 us (21%)
  local copies, waits for them, and re-layouts  22.7 us (12%)
  Pallas kernels  20.6 us (11%)
  blocking collectives  14.2 us (7%)
  other arithmetic  4.32 us (2%)
  between operations  2.39 us (1%)
    ppermute x11, starting transfers between devices, seq_move(): return lax.ppermute(value, 'seq', pairs)  39.4 us
    ppermute x6, starting transfers between devices, head_shift(): return lax.ppermute(value, 'heads', [(i, (i + by) % 4) for i in range(4)])  26.1 us
    unnamed x62, local copies, waits for them, and re-layouts  18.5 us
    all_to_all x2, starting transfers between devices, give_all(): return lax.all_to_all(copies, 'seq', 0, 0, axis_index_groups=groups)  17.8 us
    ppermute x6, waiting for transfers between devices, head_shift(): return lax.ppermute(value, 'heads', [(i, (i + by) % 4) for i in range(4)])  16.6 us
    all_to_all x1, blocking collectives, per_device(): grads = lax.all_to_all(grad, 'heads', 0, 0)  14.2 us
    all_to_all x2, waiting for transfers between devices, give_all(): return lax.all_to_all(copies, 'seq', 0, 0, axis_index_groups=groups)  12.9 us
    ppermute x11, waiting for transfers between devices, seq_move(): return lax.ppermute(value, 'seq', pairs)  10.6 us
  transfers between devices with their start and end apart: 19, of which 8 were waited for; matrix products, arithmetic and copies ran while one was open for 2% of the time, Pallas kernels for 4%

profile of v4, /device:TPU:25, one launch (start us, length us, event | category | flops | bytes accessed | tf_op | source)
XLA Modules:
  0.0 187.6 jit_solution(6429863767083473127)
XLA Ops:
  0.7 0.9 constant_dynamic-slice_fusion
  1.6 2.6 %collective-permute-start = (bf16[192,384]{1,0:T(8,128)(2,1)S(1)}, bf16[192,384]{1,0:T(8,128)(2,1)S(1)}, u32[]{:S(2)}, u32[]{:S(2)}) collective-permute-start(bf16[192,384]{1,0:T(8,128)(2,1)S(1)} %constant_dynamic-slice_fusion), channel_id=1, source_target_pairs={{0,4},{4,0},{8,12},{12,8},{16,20},{20,16},{24,28},{28,24},{32,36},... | collective-permute-start | bytes 442376 | tf_op jit(solution)/shard_map/ppermute | solution.py:41
  4.2 8.4 %collective-permute-start.1 = (bf16[192,384]{1,0:T(8,128)(2,1)S(1)}, bf16[192,384]{1,0:T(8,128)(2,1)S(1)}, u32[]{:S(2)}, u32[]{:S(2)}) collective-permute-start(bf16[192,384]{1,0:T(8,128)(2,1)S(1)} %constant_dynamic-slice_fusion), channel_id=1, source_target_pairs={{4,8},{8,4},{12,16},{16,12},{20,24},{24,20},{28,32},{32,28},{36,40... | collective-permute-start | bytes 442376 | tf_op jit(solution)/shard_map/ppermute | solution.py:41
  12.6 3.1 %collective-permute-start.2 = (bf16[192,1536]{1,0:T(8,128)(2,1)}, bf16[192,1536]{1,0:T(8,128)(2,1)S(1)}, u32[]{:S(2)}, u32[]{:S(2)}) collective-permute-start(bf16[192,1536]{1,0:T(8,128)(2,1)} %refs_0_.1), channel_id=1, source_target_pairs={{0,128},{4,132},{8,136},{12,140},{16,144},{20,148},{24,152},{28,15... | collective-permute-start | bytes 1769480 | tf_op jit(solution)/shard_map/ppermute | solution.py:41
  15.7 0.7 collective-permute-start.3
  16.4 0.8 pad_maximum_fusion.2
  17.2 0.7 broadcast_in_dim.30
  17.9 10.0 %all-to-all-start = ((bf16[4,14,1536]{2,1,0:T(8,128)(2,1)}), bf16[4,14,1536]{2,1,0:T(8,128)(2,1)S(1)}, u32[]{:S(2)}, u32[]{:S(2)}) async-start(bf16[4,14,1536]{2,1,0:T(8,128)(2,1)} %broadcast_in_dim.30), calls=%async_computation | async-start | bytes 393216 | tf_op jit(solution)/shard_map/all_to_all | solution.py:69
  27.9 0.8 select_reduce_fusion
  29.0 0.5 fusion.28
  31.1 10.9 %all-to-all-done = bf16[4,14,1536]{2,1,0:T(8,128)(2,1)S(1)} async-done(((bf16[4,14,1536]{2,1,0:T(8,128)(2,1)}), bf16[4,14,1536]{2,1,0:T(8,128)(2,1)S(1)}, u32[]{:S(2)}, u32[]{:S(2)}) %all-to-all-start) | async-done | bytes 172064 | tf_op jit(solution)/shard_map/all_to_all | solution.py:69
  42.1 0.9 broadcast_select_fusion.refs_2_
  43.0 5.2 %collective-permute-start.4 = (bf16[192,384]{1,0:T(8,128)(2,1)S(1)}, bf16[192,384]{1,0:T(8,128)(2,1)S(1)}, u32[]{:S(2)}, u32[]{:S(2)}) collective-permute-start(bf16[192,384]{1,0:T(8,128)(2,1)S(1)} %broadcast_select_fusion.2), channel_id=1, source_target_pairs={{0,128},{4,132},{8,136},{12,140},{16,144},{20,148},{24,152},{28,15... | collective-permute-start | bytes 442376 | tf_op jit(solution)/shard_map/ppermute | solution.py:41
  48.2 0.7 collective-permute-start.5
  48.9 1.8 collective-permute-done.4
  50.7 0.7 pad_maximum_fusion.p0
  51.5 1.7 broadcast_in_dim.57
  53.2 7.8 %all-to-all-start.1 = ((bf16[16,56,1536]{2,1,0:T(8,128)(2,1)}), bf16[16,56,1536]{2,1,0:T(8,128)(2,1)S(1)}, u32[]{:S(2)}, u32[]{:S(2)}) async-start(bf16[16,56,1536]{2,1,0:T(8,128)(2,1)} %broadcast_in_dim.57), calls=%async_computation.1 | async-start | bytes 5505024 | tf_op jit(solution)/shard_map/all_to_all | solution.py:69
  60.9 7.4 %collective-permute-start.6 = (bf16[384,384]{1,0:T(8,128)(2,1)}, bf16[384,384]{1,0:T(8,128)(2,1)S(1)}, u32[]{:S(2)}, u32[]{:S(2)}) collective-permute-start(bf16[384,384]{1,0:T(8,128)(2,1)} %pad_maximum_fusion.p0), channel_id=1, source_target_pairs={{0,1},{1,2},{2,3},{3,0},{4,5},{5,6},{6,7},{7,4},{8,9},{9,10},{10,1... | collective-permute-start | bytes 884744 | tf_op jit(solution)/shard_map/ppermute | solution.py:302
  68.3 2.4 %collective-permute-start.7 = (bf16[384,384]{1,0:T(8,128)(2,1)}, bf16[384,384]{1,0:T(8,128)(2,1)S(1)}, u32[]{:S(2)}, u32[]{:S(2)}) collective-permute-start(bf16[384,384]{1,0:T(8,128)(2,1)} %pad_maximum_fusion.p0), channel_id=1, source_target_pairs={{0,2},{1,3},{2,0},{3,1},{4,6},{5,7},{6,4},{7,5},{8,10},{9,11},{10,... | collective-permute-start | bytes 884744 | tf_op jit(solution)/shard_map/ppermute | solution.py:302
  70.7 4.3 %collective-permute-start.8 = (bf16[384,384]{1,0:T(8,128)(2,1)}, bf16[384,384]{1,0:T(8,128)(2,1)S(1)}, u32[]{:S(2)}, u32[]{:S(2)}) collective-permute-start(bf16[384,384]{1,0:T(8,128)(2,1)} %pad_maximum_fusion.p0), channel_id=1, source_target_pairs={{0,3},{1,0},{2,1},{3,2},{4,7},{5,4},{6,5},{7,6},{8,11},{9,8},{10,9... | collective-permute-start | bytes 884744 | tf_op jit(solution)/shard_map/ppermute | solution.py:302
  75.0 1.1 copy-done.7
  76.1 1.1 copy-done.25
  77.1 1.1 copy-done.26
  78.2 1.4 shard_map.122
  79.6 0.8 copy-done.8
  80.4 0.8 copy-done.10
  81.1 0.7 copy-done.12
  81.9 0.8 copy-done.14
  82.6 0.8 copy-done.16
  83.4 0.8 copy-done.18
  84.2 4.0 %collective-permute-done.7.p2 = bf16[384,384]{1,0:T(8,128)(2,1)S(1)} collective-permute-done((bf16[384,384]{1,0:T(8,128)(2,1)}, bf16[384,384]{1,0:T(8,128)(2,1)S(1)}, u32[]{:S(2)}, u32[]{:S(2)}) %collective-permute-start.7) | collective-permute-done | bytes 294944 | tf_op jit(solution)/shard_map/ppermute | solution.py:302
  88.1 1.0 shard_map.123
  89.1 0.9 copy-done.3
  90.0 0.9 copy-done.5
  90.9 2.0 %all-to-all-done.1 = bf16[16,56,1536]{2,1,0:T(8,128)(2,1)S(1)} async-done(((bf16[16,56,1536]{2,1,0:T(8,128)(2,1)}), bf16[16,56,1536]{2,1,0:T(8,128)(2,1)S(1)}, u32[]{:S(2)}, u32[]{:S(2)}) %all-to-all-start.1) | async-done | bytes 2752544 | tf_op jit(solution)/shard_map/all_to_all | solution.py:69
  92.9 7.3 %collective-permute-start.9 = (bf16[896,1536]{1,0:T(8,128)(2,1)S(1)}, bf16[896,1536]{1,0:T(8,128)(2,1)S(1)}, u32[]{:S(2)}, u32[]{:S(2)}) collective-permute-start(bf16[896,1536]{1,0:T(8,128)(2,1)S(1)} %bitcast.21), channel_id=1, source_target_pairs={{0,4},{4,0},{8,12},{12,8},{16,20},{20,16},{24,28},{28,24},{32,36},... | collective-permute-start | bytes 8257544 | tf_op jit(solution)/shard_map/ppermute | solution.py:41
  100.2 1.1 copy-done.6
  101.4 1.0 copy-done.15
  102.4 1.0 copy-done.17
  103.4 1.0 copy-done.19
  104.4 3.2 %shard_map.124 = (f32[192,1152]{1,0:T(8,128)S(1)}, f32[192,384]{1,0:T(8,128)S(1)}, f32[192,768]{1,0:T(8,128)S(1)}, f32[384,768]{1,0:T(8,128)S(1)}, f32[128,768]{...) custom-call(s32[6]{0:T(128)S(1)} %stack.35.flags, bf16[4,192,224]{2,1,0:T(8,128)(2,1)S(1)} %copy-done.15, ...), custom_call_target="tpu_custom_call" | custom-call | flops 1000000000 | bytes 8000000 | tf_op jit(solution)/shard_map/pallas_call | solution.py:365
  107.7 8.9 %shard_map.125 = (bf16[192,384]{1,0:T(8,128)(2,1)S(1)}, bf16[192,384]{1,0:T(8,128)(2,1)S(1)}, bf16[384,768]{1,0:T(8,128)(2,1)S(1)}, bf16[384,768]{1,0:T(8,128)(2...) custom-call(s32[6]{0:T(128)S(1)} %stack.35.flags, bf16[4,192,224]{2,1,0:T(8,128)(2,1)S(1)} %copy-done.9, ...), custom_call_target="tpu_custom_call" | custom-call | flops 1000000000 | bytes 8000000 | tf_op jit(solution)/shard_map/pallas_call | solution.py:377
  116.6 0.7 copy-done.20
  117.3 0.7 copy-done.23
  118.0 0.8 copy-done.27
  118.8 1.9 %collective-permute-start.10 = (bf16[384,768]{1,0:T(8,128)(2,1)}, bf16[384,768]{1,0:T(8,128)(2,1)}, u32[]{:S(2)}, u32[]{:S(2)}) collective-permute-start(bf16[384,768]{1,0:T(8,128)(2,1)} %get-tuple-element.84), channel_id=1, source_target_pairs={{0,128},{4,132},{8,136},{12,140},{16,144},{20,148},{24,152},{28,15... | collective-permute-start | bytes 1769480 | tf_op jit(solution)/shard_map/ppermute | solution.py:41
  120.7 1.5 collective-permute-start.11
  122.2 1.8 copy-done.2
  124.0 0.9 copy-done.24
  124.9 2.0 %shard_map.126 = (bf16[4,192,384]{2,1,0:T(8,128)(2,1)S(1)}, f32[2,4,192,224]{3,2,1,0:T(8,128)S(1)}) custom-call(bf16[192,384]{1,0:T(8,128)(2,1)S(1)} %get-tuple-element.86.att, bf16[192,384]{1,0:T(8,128)(2,1)S(1)} %copy-done.24, bf16[896,1536]{1,0:T(8,128)(2,1)S(1)} %bitcast.24, bf16[896,1536]{1,0:T(8,128)(2,1)S(1)} %copy-done.2, ...), custom_call_target="tpu_custom_call" | custom-call | flops 1000000000 | bytes 8000000 | tf_op jit(solution)/shard_map/pallas_call | solution.py:393
  127.0 6.5 %collective-permute-start.12 = (bf16[192,384]{1,0:T(8,128)(2,1)S(1)}, bf16[192,384]{1,0:T(8,128)(2,1)S(1)}, u32[]{:S(2)}, u32[]{:S(2)}) collective-permute-start(bf16[192,384]{1,0:T(8,128)(2,1)S(1)} %get-tuple-element.103), channel_id=1, source_target_pairs={{0,1},{1,2},{2,3},{3,0},{4,5},{5,6},{6,7},{7,4},{8,9},{9,10},{10,1... | collective-permute-start | bytes 442376 | tf_op jit(solution)/shard_map/ppermute | solution.py:302
  133.5 2.4 %collective-permute-start.13 = (bf16[192,384]{1,0:T(8,128)(2,1)S(1)}, bf16[192,384]{1,0:T(8,128)(2,1)S(1)}, u32[]{:S(2)}, u32[]{:S(2)}) collective-permute-start(bf16[192,384]{1,0:T(8,128)(2,1)S(1)} %get-tuple-element.102), channel_id=1, source_target_pairs={{0,2},{1,3},{2,0},{3,1},{4,6},{5,7},{6,4},{7,5},{8,10},{9,11},{10,... | collective-permute-start | bytes 442376 | tf_op jit(solution)/shard_map/ppermute | solution.py:302
  135.9 1.2 collective-permute-done.12.o1
  137.1 7.7 %collective-permute-done.13.o2 = bf16[192,384]{1,0:T(8,128)(2,1)S(1)} collective-permute-done((bf16[192,384]{1,0:T(8,128)(2,1)S(1)}, bf16[192,384]{1,0:T(8,128)(2,1)S(1)}, u32[]{:S(2)}, u32[]{:S(2)}) %collective-permute-start.13) | collective-permute-done | bytes 147488 | tf_op jit(solution)/shard_map/ppermute | solution.py:302
  144.8 1.5 shard_map.127
  146.3 2.9 %collective-permute-start.14 = (bf16[192,768]{1,0:T(8,128)(2,1)S(1)}, bf16[192,768]{1,0:T(8,128)(2,1)S(1)}, u32[]{:S(2)}, u32[]{:S(2)}) collective-permute-start(bf16[192,768]{1,0:T(8,128)(2,1)S(1)} %get-tuple-element.92), channel_id=1, source_target_pairs={{0,4},{4,0},{8,12},{12,8},{16,20},{20,16},{24,28},{28,24},{32,36},... | collective-permute-start | bytes 884744 | tf_op jit(solution)/shard_map/ppermute | solution.py:41
  149.2 5.2 %collective-permute-start.15 = (bf16[192,768]{1,0:T(8,128)(2,1)S(1)}, bf16[192,768]{1,0:T(8,128)(2,1)S(1)}, u32[]{:S(2)}, u32[]{:S(2)}) collective-permute-start(bf16[192,768]{1,0:T(8,128)(2,1)S(1)} %get-tuple-element.93), channel_id=1, source_target_pairs={{4,8},{8,4},{12,16},{16,12},{20,24},{24,20},{28,32},{32,28},{36,40... | collective-permute-start | bytes 884744 | tf_op jit(solution)/shard_map/ppermute | solution.py:41
  154.5 3.1 %collective-permute-start.16 = (bf16[192,384]{1,0:T(8,128)(2,1)S(1)}, bf16[192,384]{1,0:T(8,128)(2,1)S(1)}, u32[]{:S(2)}, u32[]{:S(2)}) collective-permute-start(bf16[192,384]{1,0:T(8,128)(2,1)S(1)} %get-tuple-element.100), channel_id=1, source_target_pairs={{0,3},{1,0},{2,1},{3,2},{4,7},{5,4},{6,5},{7,6},{8,11},{9,8},{10,9... | collective-permute-start | bytes 442376 | tf_op jit(solution)/shard_map/ppermute | solution.py:302
  157.6 3.8 %collective-permute-done.16.o3 = bf16[192,384]{1,0:T(8,128)(2,1)S(1)} collective-permute-done((bf16[192,384]{1,0:T(8,128)(2,1)S(1)}, bf16[192,384]{1,0:T(8,128)(2,1)S(1)}, u32[]{:S(2)}, u32[]{:S(2)}) %collective-permute-start.16) | collective-permute-done | bytes 147488 | tf_op jit(solution)/shard_map/ppermute | solution.py:302
  161.4 8.8 %collective-permute-done.15.in_b = bf16[192,768]{1,0:T(8,128)(2,1)S(1)} collective-permute-done((bf16[192,768]{1,0:T(8,128)(2,1)S(1)}, bf16[192,768]{1,0:T(8,128)(2,1)S(1)}, u32[]{:S(2)}, u32[]{:S(2)}) %collective-permute-start.15) | collective-permute-done | bytes 294944 | tf_op jit(solution)/shard_map/ppermute | solution.py:41
  170.2 2.6 %shard_map.128 = (bf16[4,192,384]{2,1,0:T(8,128)(2,1)S(1)}, bf16[192,384]{1,0:T(8,128)(2,1)}) custom-call(f32[192,768]{1,0:T(8,128)S(1)} %get-tuple-element.91.own, bf16[192,768]{1,0:T(8,128)(2,1)S(1)} %collective-permute-done.14.in_a, bf16[192,768]{1,0:T(8,128)(2,1)S(1)} %collective-permute-done.15.in_b, f32[192,384]{1,0:T(8,128)S(1)} %copy-done.21, ...), custom_call_target="tpu_custom_call" | custom-call | flops 1000000000 | bytes 8000000 | tf_op jit(solution)/shard_map/pallas_call | solution.py:410
  172.7 14.2 %all_to_all.15 = bf16[4,192,384]{2,1,0:T(8,128)(2,1)S(1)} all-to-all(bf16[4,192,384]{2,1,0:T(8,128)(2,1)S(1)} %get-tuple-element.99), channel_id=1, replica_groups=mesh['seq'=128,'heads'=4] {'heads'}, dimensions={0} | all-to-all | bytes 1179648 | tf_op jit(solution)/shard_map/all_to_all | solution.py:416
  186.9 0.7 fusion.5
  (72 shorter events, 0.8 us)
Async XLA Ops:
  0.6 28.1 %copy-start = (s32[128,2]{0,1:T(2,128)S(1)}, s32[128,2]{0,1:T(2,128)}, u32[]{:S(2)}) copy-start(s32[128,2]{0,1:T(2,128)} %param.20) | copy-start | bytes 3076
  1.6 29.5 %collective-permute-start = (bf16[192,384]{1,0:T(8,128)(2,1)S(1)}, bf16[192,384]{1,0:T(8,128)(2,1)S(1)}, u32[]{:S(2)}, u32[]{:S(2)}) collective-permute-start(bf16[192,384]{1,0:T(8,128)(2,1)S(1)} %constant_dynamic-slice_fusion), channel_id=1, source_target_pairs={{0,4},{4,0},{8,12},{12,8},{16,20},{20,16},{24,28},{28,24},{32,36},... | collective-permute-start | bytes 442376 | tf_op jit(solution)/shard_map/ppermute | solution.py:41
  4.2 26.9 %collective-permute-start.1 = (bf16[192,384]{1,0:T(8,128)(2,1)S(1)}, bf16[192,384]{1,0:T(8,128)(2,1)S(1)}, u32[]{:S(2)}, u32[]{:S(2)}) collective-permute-start(bf16[192,384]{1,0:T(8,128)(2,1)S(1)} %constant_dynamic-slice_fusion), channel_id=1, source_target_pairs={{4,8},{8,4},{12,16},{16,12},{20,24},{24,20},{28,32},{32,28},{36,40... | collective-permute-start | bytes 442376 | tf_op jit(solution)/shard_map/ppermute | solution.py:41
  12.6 29.6 %collective-permute-start.2 = (bf16[192,1536]{1,0:T(8,128)(2,1)}, bf16[192,1536]{1,0:T(8,128)(2,1)S(1)}, u32[]{:S(2)}, u32[]{:S(2)}) collective-permute-start(bf16[192,1536]{1,0:T(8,128)(2,1)} %refs_0_.1), channel_id=1, source_target_pairs={{0,128},{4,132},{8,136},{12,140},{16,144},{20,148},{24,152},{28,15... | collective-permute-start | bytes 1769480 | tf_op jit(solution)/shard_map/ppermute | solution.py:41
  15.7 26.4 %collective-permute-start.3 = (bf16[192,1536]{1,0:T(8,128)(2,1)}, bf16[192,1536]{1,0:T(8,128)(2,1)S(1)}, u32[]{:S(2)}, u32[]{:S(2)}) collective-permute-start(bf16[192,1536]{1,0:T(8,128)(2,1)} %refs_0_.1), channel_id=1, source_target_pairs={{128,256},{132,260},{136,264},{140,268},{144,272},{148,276},{152,2... | collective-permute-start | bytes 1769480 | tf_op jit(solution)/shard_map/ppermute | solution.py:41
  17.9 24.1 %all-to-all-start = ((bf16[4,14,1536]{2,1,0:T(8,128)(2,1)}), bf16[4,14,1536]{2,1,0:T(8,128)(2,1)S(1)}, u32[]{:S(2)}, u32[]{:S(2)}) async-start(bf16[4,14,1536]{2,1,0:T(8,128)(2,1)} %broadcast_in_dim.30), calls=%async_computation | async-start | bytes 393216 | tf_op jit(solution)/shard_map/all_to_all | solution.py:69
  43.0 7.7 %collective-permute-start.4 = (bf16[192,384]{1,0:T(8,128)(2,1)S(1)}, bf16[192,384]{1,0:T(8,128)(2,1)S(1)}, u32[]{:S(2)}, u32[]{:S(2)}) collective-permute-start(bf16[192,384]{1,0:T(8,128)(2,1)S(1)} %broadcast_select_fusion.2), channel_id=1, source_target_pairs={{0,128},{4,132},{8,136},{12,140},{16,144},{20,148},{24,152},{28,15... | collective-permute-start | bytes 442376 | tf_op jit(solution)/shard_map/ppermute | solution.py:41
  48.2 2.5 %collective-permute-start.5 = (bf16[192,384]{1,0:T(8,128)(2,1)S(1)}, bf16[192,384]{1,0:T(8,128)(2,1)S(1)}, u32[]{:S(2)}, u32[]{:S(2)}) collective-permute-start(bf16[192,384]{1,0:T(8,128)(2,1)S(1)} %broadcast_select_fusion.2), channel_id=1, source_target_pairs={{128,256},{132,260},{136,264},{140,268},{144,272},{148,276},{152,2... | collective-permute-start | bytes 442376 | tf_op jit(solution)/shard_map/ppermute | solution.py:41
  53.2 39.8 %all-to-all-start.1 = ((bf16[16,56,1536]{2,1,0:T(8,128)(2,1)}), bf16[16,56,1536]{2,1,0:T(8,128)(2,1)S(1)}, u32[]{:S(2)}, u32[]{:S(2)}) async-start(bf16[16,56,1536]{2,1,0:T(8,128)(2,1)} %broadcast_in_dim.57), calls=%async_computation.1 | async-start | bytes 5505024 | tf_op jit(solution)/shard_map/all_to_all | solution.py:69
  60.9 23.3 %collective-permute-start.6 = (bf16[384,384]{1,0:T(8,128)(2,1)}, bf16[384,384]{1,0:T(8,128)(2,1)S(1)}, u32[]{:S(2)}, u32[]{:S(2)}) collective-permute-start(bf16[384,384]{1,0:T(8,128)(2,1)} %pad_maximum_fusion.p0), channel_id=1, source_target_pairs={{0,1},{1,2},{2,3},{3,0},{4,5},{5,6},{6,7},{7,4},{8,9},{9,10},{10,1... | collective-permute-start | bytes 884744 | tf_op jit(solution)/shard_map/ppermute | solution.py:302
  68.3 19.8 %collective-permute-start.7 = (bf16[384,384]{1,0:T(8,128)(2,1)}, bf16[384,384]{1,0:T(8,128)(2,1)S(1)}, u32[]{:S(2)}, u32[]{:S(2)}) collective-permute-start(bf16[384,384]{1,0:T(8,128)(2,1)} %pad_maximum_fusion.p0), channel_id=1, source_target_pairs={{0,2},{1,3},{2,0},{3,1},{4,6},{5,7},{6,4},{7,5},{8,10},{9,11},{10,... | collective-permute-start | bytes 884744 | tf_op jit(solution)/shard_map/ppermute | solution.py:302
  70.7 17.4 %collective-permute-start.8 = (bf16[384,384]{1,0:T(8,128)(2,1)}, bf16[384,384]{1,0:T(8,128)(2,1)S(1)}, u32[]{:S(2)}, u32[]{:S(2)}) collective-permute-start(bf16[384,384]{1,0:T(8,128)(2,1)} %pad_maximum_fusion.p0), channel_id=1, source_target_pairs={{0,3},{1,0},{2,1},{3,2},{4,7},{5,4},{6,5},{7,6},{8,11},{9,8},{10,9... | collective-permute-start | bytes 884744 | tf_op jit(solution)/shard_map/ppermute | solution.py:302
  75.0 1.1 copy-start.7
  76.1 1.1 copy-start.25
  77.1 1.1 copy-start.26
  78.2 9.9 %copy-start.22 = (bf16[384,384]{1,0:T(8,128)(2,1)S(1)}, bf16[384,384]{1,0:T(8,128)(2,1)}, u32[]{:S(2)}) copy-start(bf16[384,384]{1,0:T(8,128)(2,1)} %pad_maximum_fusion.p0) | copy-start | bytes 884740
  79.6 0.8 copy-start.8
  80.4 0.8 copy-start.10
  81.1 0.7 copy-start.12
  81.9 0.8 copy-start.14
  82.6 0.8 copy-start.16
  83.4 0.8 copy-start.18
  84.2 16.0 %copy-start.29 = (f32[384]{0:T(512)S(1)}, f32[384]{0:T(512)}, u32[]{:S(2)}) copy-start(f32[384]{0:T(512)} %param.18) | copy-start | bytes 4612
  84.2 16.1 %copy-start.30 = (f32[384]{0:T(512)S(1)}, f32[384]{0:T(512)}, u32[]{:S(2)}) copy-start(f32[384]{0:T(512)} %param.17) | copy-start | bytes 4612
  89.1 0.9 copy-start.3
  90.0 0.9 copy-start.5
  92.9 14.7 %copy-start.4 = (bf16[4,384,224]{2,1,0:T(8,128)(2,1)S(1)}, bf16[4,384,224]{2,1,0:T(8,128)(2,1)}, u32[]{:S(2)}) copy-start(bf16[4,384,224]{2,1,0:T(8,128)(2,1)} %copy-done.3) | copy-start | bytes 2064388
  92.9 14.7 %collective-permute-start.9 = (bf16[896,1536]{1,0:T(8,128)(2,1)S(1)}, bf16[896,1536]{1,0:T(8,128)(2,1)S(1)}, u32[]{:S(2)}, u32[]{:S(2)}) collective-permute-start(bf16[896,1536]{1,0:T(8,128)(2,1)S(1)} %bitcast.21), channel_id=1, source_target_pairs={{0,4},{4,0},{8,12},{12,8},{16,20},{20,16},{24,28},{28,24},{32,36},... | collective-permute-start | bytes 8257544 | tf_op jit(solution)/shard_map/ppermute | solution.py:41
  100.2 1.1 copy-start.6
  101.4 1.0 copy-start.15
  102.4 1.0 copy-start.17
  103.4 1.0 copy-start.19
  104.4 3.3 %copy-start.9 = (bf16[4,192,224]{2,1,0:T(8,128)(2,1)S(1)}, bf16[4,192,224]{2,1,0:T(8,128)(2,1)}, u32[]{:S(2)}) copy-start(bf16[4,192,224]{2,1,0:T(8,128)(2,1)} %copy-done.8) | copy-start | bytes 1032196
  104.4 3.3 %copy-start.11 = (bf16[4,192,224]{2,1,0:T(8,128)(2,1)S(1)}, bf16[4,192,224]{2,1,0:T(8,128)(2,1)}, u32[]{:S(2)}) copy-start(bf16[4,192,224]{2,1,0:T(8,128)(2,1)} %copy-done.10) | copy-start | bytes 1032196
  104.4 3.3 %copy-start.13 = (bf16[4,192,224]{2,1,0:T(8,128)(2,1)S(1)}, bf16[4,192,224]{2,1,0:T(8,128)(2,1)}, u32[]{:S(2)}) copy-start(bf16[4,192,224]{2,1,0:T(8,128)(2,1)} %copy-done.12) | copy-start | bytes 1032196
  107.6 9.0 %copy-start.1 = (bf16[896,1536]{1,0:T(8,128)(2,1)}, bf16[896,1536]{1,0:T(8,128)(2,1)S(1)}, u32[]{:S(2)}) copy-start(bf16[896,1536]{1,0:T(8,128)(2,1)S(1)} %collective-permute-done.9.wt) | copy-start | bytes 8257540
  116.6 0.7 copy-start.20
  117.3 0.7 copy-start.23
  118.0 0.8 copy-start.27
  118.8 26.0 %collective-permute-start.10 = (bf16[384,768]{1,0:T(8,128)(2,1)}, bf16[384,768]{1,0:T(8,128)(2,1)}, u32[]{:S(2)}, u32[]{:S(2)}) collective-permute-start(bf16[384,768]{1,0:T(8,128)(2,1)} %get-tuple-element.84), channel_id=1, source_target_pairs={{0,128},{4,132},{8,136},{12,140},{16,144},{20,148},{24,152},{28,15... | collective-permute-start | bytes 1769480 | tf_op jit(solution)/shard_map/ppermute | solution.py:41
  120.7 24.1 %collective-permute-start.11 = (bf16[384,768]{1,0:T(8,128)(2,1)}, bf16[384,768]{1,0:T(8,128)(2,1)}, u32[]{:S(2)}, u32[]{:S(2)}) collective-permute-start(bf16[384,768]{1,0:T(8,128)(2,1)} %get-tuple-element.85), channel_id=1, source_target_pairs={{128,256},{132,260},{136,264},{140,268},{144,272},{148,276},{152,2... | collective-permute-start | bytes 1769480 | tf_op jit(solution)/shard_map/ppermute | solution.py:41
  122.2 1.8 copy-start.2
  124.0 0.9 copy-start.24
  124.9 19.9 %copy-start.28 = (bf16[384,768]{1,0:T(8,128)(2,1)S(1)}, bf16[384,768]{1,0:T(8,128)(2,1)}, u32[]{:S(2)}) copy-start(bf16[384,768]{1,0:T(8,128)(2,1)} %copy-done.27) | copy-start | bytes 1769476
  126.9 43.3 %copy-start.21 = (f32[192,384]{1,0:T(8,128)S(1)}, f32[192,384]{1,0:T(8,128)}, u32[]{:S(2)}) copy-start(f32[192,384]{1,0:T(8,128)} %copy-done.20) | copy-start | bytes 884740
  127.0 10.1 %collective-permute-start.12 = (bf16[192,384]{1,0:T(8,128)(2,1)S(1)}, bf16[192,384]{1,0:T(8,128)(2,1)S(1)}, u32[]{:S(2)}, u32[]{:S(2)}) collective-permute-start(bf16[192,384]{1,0:T(8,128)(2,1)S(1)} %get-tuple-element.103), channel_id=1, source_target_pairs={{0,1},{1,2},{2,3},{3,0},{4,5},{5,6},{6,7},{7,4},{8,9},{9,10},{10,1... | collective-permute-start | bytes 442376 | tf_op jit(solution)/shard_map/ppermute | solution.py:302
  133.5 11.3 %collective-permute-start.13 = (bf16[192,384]{1,0:T(8,128)(2,1)S(1)}, bf16[192,384]{1,0:T(8,128)(2,1)S(1)}, u32[]{:S(2)}, u32[]{:S(2)}) collective-permute-start(bf16[192,384]{1,0:T(8,128)(2,1)S(1)} %get-tuple-element.102), channel_id=1, source_target_pairs={{0,2},{1,3},{2,0},{3,1},{4,6},{5,7},{6,4},{7,5},{8,10},{9,11},{10,... | collective-permute-start | bytes 442376 | tf_op jit(solution)/shard_map/ppermute | solution.py:302
  146.3 15.1 %collective-permute-start.14 = (bf16[192,768]{1,0:T(8,128)(2,1)S(1)}, bf16[192,768]{1,0:T(8,128)(2,1)S(1)}, u32[]{:S(2)}, u32[]{:S(2)}) collective-permute-start(bf16[192,768]{1,0:T(8,128)(2,1)S(1)} %get-tuple-element.92), channel_id=1, source_target_pairs={{0,4},{4,0},{8,12},{12,8},{16,20},{20,16},{24,28},{28,24},{32,36},... | collective-permute-start | bytes 884744 | tf_op jit(solution)/shard_map/ppermute | solution.py:41
  149.2 21.0 %collective-permute-start.15 = (bf16[192,768]{1,0:T(8,128)(2,1)S(1)}, bf16[192,768]{1,0:T(8,128)(2,1)S(1)}, u32[]{:S(2)}, u32[]{:S(2)}) collective-permute-start(bf16[192,768]{1,0:T(8,128)(2,1)S(1)} %get-tuple-element.93), channel_id=1, source_target_pairs={{4,8},{8,4},{12,16},{16,12},{20,24},{24,20},{28,32},{32,28},{36,40... | collective-permute-start | bytes 884744 | tf_op jit(solution)/shard_map/ppermute | solution.py:41
  154.5 6.9 %collective-permute-start.16 = (bf16[192,384]{1,0:T(8,128)(2,1)S(1)}, bf16[192,384]{1,0:T(8,128)(2,1)S(1)}, u32[]{:S(2)}, u32[]{:S(2)}) collective-permute-start(bf16[192,384]{1,0:T(8,128)(2,1)S(1)} %get-tuple-element.100), channel_id=1, source_target_pairs={{0,3},{1,0},{2,1},{3,2},{4,7},{5,4},{6,5},{7,6},{8,11},{9,8},{10,9... | collective-permute-start | bytes 442376 | tf_op jit(solution)/shard_map/ppermute | solution.py:302

commit v5 on v4

--- a/solution.py
+++ b/solution.py
@@ -15,6 +15,7 @@
 EPS = 1e-6
 SCALE = HD**-0.5
 OUT_COST = 10**9
+TERM_COST = 10**11
 GRAD_COST = 10**9
 BLOCK = 56
 PART = 4 * BLOCK
@@ -251,14 +252,12 @@
             odd_t[:, lanes] = (term[2 * ROWS :] * odd).astype(BF16)
 
 
-def out_kernel(att, dq, wo, wt, pick_o, pick_t, out, gq):
+def out_kernel(att, wo, wt, pick_o, pick_t, out):
     for j in range(4):
         rows = slice(j * PART, (j + 1) * PART)
-        o = dot(att[...], wo[rows, 3 * W :], NT).astype(BF16)
-        t = dot(att[...], wt[rows, 3 * W :], NT).astype(BF16)
+        o = dot(att[...], wo[rows, LAST], NT).astype(BF16)
+        t = dot(att[...], wt[rows, LAST], NT).astype(BF16)
         out[j] = (dot(o, pick_o[...], NT) + dot(t, pick_t[...], NT)).astype(BF16)
-        gq[0, j] = dot(dq[...], wo[rows, 2 * W : 3 * W], NT)
-        gq[1, j] = dot(dq[...], wt[rows, 2 * W : 3 * W], NT)
 
 
 def term_kernel(flags, near_t, got_even, got_odd, own, to_mate, to_next):
@@ -269,26 +268,22 @@
     to_next[...] = (total[ROWS:] * (1.0 - mate)).astype(BF16)
 
 
-def grad_kernel(own, in_a, in_b, kraw, k_gain, gq, wo, wt, pick_o, pick_t, o0, o1, o2, o3, out, res):
+def grad_kernel(own, in_a, in_b, kraw, k_gain, dq, wo, wt, pick_o, pick_t, out):
     total = own[...] + in_a[...].astype(F32) + in_b[...].astype(F32)
     parts = [
         norm_pull(kraw[:, head(h)], k_gain[:, head(h)], total[:, head(h)]).astype(BF16)
         for h in range(NH)
     ]
-    d = jnp.concatenate(parts + [total[:, W:].astype(BF16)], axis=1)
+    d = jnp.concatenate(parts + [total[:, W:].astype(BF16), dq[...]], axis=1)
     for j in range(4):
         rows = slice(j * PART, (j + 1) * PART)
-        o = (gq[0, j] + dot(d, wo[rows, : 2 * W], NT)).astype(BF16)
-        t = (gq[1, j] + dot(d, wt[rows, : 2 * W], NT)).astype(BF16)
+        o = dot(d, wo[rows, KVQ], NT).astype(BF16)
+        t = dot(d, wt[rows, KVQ], NT).astype(BF16)
         out[j] = (dot(o, pick_o[...], NT) + dot(t, pick_t[...], NT)).astype(BF16)
-    res[...] = f32_sum(o0[...], o1[...], o2[...], o3[...]).astype(BF16)
-
-
-def to_heads(blocks, me):
-    def block(to):
-        return lax.dynamic_index_in_dim(blocks, to & 3, 0, keepdims=False)
-
-    return [block(me)] + [head_shift(block(me + by), by) for by in (1, 2, 3)]
+
+
+def head_total(parts):
+    return f32_sum(*[parts[n] for n in range(4)]).astype(BF16)
 
 
 def f32_sum(*terms):
@@ -344,7 +339,9 @@
     side, behind, pick_o, pick_t, flags = lax.optimization_barrier(
         (side, behind, pick_o, pick_t, flags)
     )
-    corner = jnp.where(use_even, row_even(side), row_odd(side))
+    c_even, c_odd = row_even(side), row_odd(side)
+    four, c_even, c_odd = lax.optimization_barrier((four, c_even, c_odd))
+    corner = jnp.where(use_even, c_even, c_odd)
     beside = jnp.concatenate([side, corner])
     block = jnp.concatenate([four[:, :12].reshape(48, 1536), four[:, 12:].reshape(8, 1536)], axis=0)
     block, beside, lines, bias = lax.optimization_barrier((block, beside, lines, bias))
@@ -390,31 +387,23 @@
     )(flags, x_t, g_t, f_t, p_t, text, pick_o, pick_t, lines, wo, wt, *accs, q_gain, k_gain, bias)
 
     got_even, got_odd = row_even(even_t), row_odd(odd_t)
-    out, gq = call(
-        out_kernel,
-        (shape((4, ROWS, W), BF16), shape((2, 4, ROWS, PART), F32)),
-        "v" * 6,
-        flops=OUT_COST,
-    )(att, dq, wo, wt, pick_o, pick_t)
-    outs = to_heads(out, me)
-    got_even, got_odd, outs[1], outs[2] = lax.optimization_barrier(
-        (got_even, got_odd, outs[1], outs[2])
-    )
+    out = call(out_kernel, shape((4, ROWS, W), BF16), "v" * 5, flops=OUT_COST)(
+        att, wo, wt, pick_o, pick_t
+    )
+    outs = lax.all_to_all(out, "heads", 0, 0)
     own_t, to_mate, to_next = call(
         term_kernel,
         (shape((ROWS, 768), F32), shape((ROWS, 768), BF16), shape((ROWS, 768), BF16)),
         "svvv",
         mib=8,
+        flops=TERM_COST,
     )(flags, near_t, got_even, got_odd)
     mate_t, next_t = core_mate(to_mate), next_chip(to_next)
-    grad, out_tiles = call(
-        grad_kernel,
-        (shape((4, ROWS, W), BF16), shape((ROWS, W), BF16)),
-        "v" * 14,
-        flops=GRAD_COST,
-    )(own_t, mate_t, next_t, kraw, k_gain, gq, wo, wt, pick_o, pick_t, *outs)
+    grad = call(grad_kernel, shape((4, ROWS, W), BF16), "v" * 10, flops=GRAD_COST)(
+        own_t, mate_t, next_t, kraw, k_gain, dq, wo, wt, pick_o, pick_t
+    )
     grads = lax.all_to_all(grad, "heads", 0, 0)
-    return (out_tiles, f32_sum(*[grads[n] for n in range(4)]).astype(BF16))
+    return (head_total(outs), head_total(grads))
 
 
 def solution(mesh):

time: 191 us -> 176 us (0.921)
  the two profiles are of different devices: /device:TPU:25 before, /device:TPU:29 now
where the time goes in v5:
time: 176 us; the launch traced here: 175 us
  starting transfers between devices  77.2 us (44%)
  waiting for transfers between devices  47.2 us (27%)
  local copies, waits for them, and re-layouts  22 us (12%)
  Pallas kernels  20 us (11%)
  other arithmetic  6.19 us (4%)
  between operations  2.39 us (1%)
    ppermute x11, starting transfers between devices, seq_move(): return lax.ppermute(value, 'seq', pairs)  41 us
    ppermute x11, waiting for transfers between devices, seq_move(): return lax.ppermute(value, 'seq', pairs)  26.2 us
    unnamed x62, local copies, waits for them, and re-layouts  17.9 us
    all_to_all x2, starting transfers between devices, give_all(): return lax.all_to_all(copies, 'seq', 0, 0, axis_index_groups=groups)  16.4 us
    ppermute x3, starting transfers between devices, head_shift(): return lax.ppermute(value, 'heads', [(i, (i + by) % 4) for i in range(4)])  11.9 us
    ppermute x3, waiting for transfers between devices, head_shift(): return lax.ppermute(value, 'heads', [(i, (i + by) % 4) for i in range(4)])  9.83 us
    pallas_call x1, Pallas kernels, per_device(): call(attend_kernel, (shape((ROWS, W), BF16), shape((ROWS, W), BF16), shap...  8.95 us
    all_to_all x1, waiting for transfers between devices, per_device(): grads = lax.all_to_all(grad, 'heads', 0, 0)  7.94 us
  transfers between devices with their start and end apart: 18, of which 7 were waited for; matrix products, arithmetic and copies ran while one was open for 3% of the time, Pallas kernels for 6%

profile of v5, /device:TPU:29, one launch (start us, length us, event | category | flops | bytes accessed | tf_op | source)
XLA Modules:
  0.0 175.1 jit_solution(14000249919147094236)
XLA Ops:
  0.7 0.9 constant_dynamic-slice_fusion
  1.6 9.0 %collective-permute-start.1 = (bf16[192,384]{1,0:T(8,128)(2,1)S(1)}, bf16[192,384]{1,0:T(8,128)(2,1)S(1)}, u32[]{:S(2)}, u32[]{:S(2)}) collective-permute-start(bf16[192,384]{1,0:T(8,128)(2,1)S(1)} %constant_dynamic-slice_fusion), channel_id=1, source_target_pairs={{4,8},{8,4},{12,16},{16,12},{20,24},{24,20},{28,32},{32,28},{36,40... | collective-permute-start | bytes 442376 | tf_op jit(solution)/shard_map/ppermute | solution.py:42
  10.6 1.9 %collective-permute-start = (bf16[192,384]{1,0:T(8,128)(2,1)S(1)}, bf16[192,384]{1,0:T(8,128)(2,1)S(1)}, u32[]{:S(2)}, u32[]{:S(2)}) collective-permute-start(bf16[192,384]{1,0:T(8,128)(2,1)S(1)} %constant_dynamic-slice_fusion), channel_id=1, source_target_pairs={{0,4},{4,0},{8,12},{12,8},{16,20},{20,16},{24,28},{28,24},{32,36},... | collective-permute-start | bytes 442376 | tf_op jit(solution)/shard_map/ppermute | solution.py:42
  12.6 2.8 %collective-permute-start.2 = (bf16[192,1536]{1,0:T(8,128)(2,1)}, bf16[192,1536]{1,0:T(8,128)(2,1)S(1)}, u32[]{:S(2)}, u32[]{:S(2)}) collective-permute-start(bf16[192,1536]{1,0:T(8,128)(2,1)} %refs_0_.1), channel_id=1, source_target_pairs={{0,128},{4,132},{8,136},{12,140},{16,144},{20,148},{24,152},{28,15... | collective-permute-start | bytes 1769480 | tf_op jit(solution)/shard_map/ppermute | solution.py:42
  15.4 1.9 %collective-permute-start.3 = (bf16[192,1536]{1,0:T(8,128)(2,1)}, bf16[192,1536]{1,0:T(8,128)(2,1)S(1)}, u32[]{:S(2)}, u32[]{:S(2)}) collective-permute-start(bf16[192,1536]{1,0:T(8,128)(2,1)} %refs_0_.1), channel_id=1, source_target_pairs={{128,256},{132,260},{136,264},{140,268},{144,272},{148,276},{152,2... | collective-permute-start | bytes 1769480 | tf_op jit(solution)/shard_map/ppermute | solution.py:42
  17.3 0.8 pad_maximum_fusion.2
  18.1 0.7 broadcast_in_dim.30
  18.8 10.0 %all-to-all-start = ((bf16[4,14,1536]{2,1,0:T(8,128)(2,1)}), bf16[4,14,1536]{2,1,0:T(8,128)(2,1)S(1)}, u32[]{:S(2)}, u32[]{:S(2)}) async-start(bf16[4,14,1536]{2,1,0:T(8,128)(2,1)} %broadcast_in_dim.30), calls=%async_computation | async-start | bytes 393216 | tf_op jit(solution)/shard_map/all_to_all | solution.py:70
  28.9 0.8 select_reduce_fusion
  29.7 0.1 fusion.4
  29.9 0.5 fusion.29
  31.9 0.9 broadcast_select_fusion.refs_2_
  32.8 3.4 %collective-permute-start.5 = (bf16[192,384]{1,0:T(8,128)(2,1)S(1)}, bf16[192,384]{1,0:T(8,128)(2,1)S(1)}, u32[]{:S(2)}, u32[]{:S(2)}) collective-permute-start(bf16[192,384]{1,0:T(8,128)(2,1)S(1)} %broadcast_select_fusion.2), channel_id=1, source_target_pairs={{128,256},{132,260},{136,264},{140,268},{144,272},{148,276},{152,2... | collective-permute-start | bytes 442376 | tf_op jit(solution)/shard_map/ppermute | solution.py:42
  36.2 1.9 %collective-permute-start.4 = (bf16[192,384]{1,0:T(8,128)(2,1)S(1)}, bf16[192,384]{1,0:T(8,128)(2,1)S(1)}, u32[]{:S(2)}, u32[]{:S(2)}) collective-permute-start(bf16[192,384]{1,0:T(8,128)(2,1)S(1)} %broadcast_select_fusion.2), channel_id=1, source_target_pairs={{0,128},{4,132},{8,136},{12,140},{16,144},{20,148},{24,152},{28,15... | collective-permute-start | bytes 442376 | tf_op jit(solution)/shard_map/ppermute | solution.py:42
  38.1 0.1 fusion.lines
  38.2 3.3 %all-to-all-done = bf16[4,14,1536]{2,1,0:T(8,128)(2,1)S(1)} async-done(((bf16[4,14,1536]{2,1,0:T(8,128)(2,1)}), bf16[4,14,1536]{2,1,0:T(8,128)(2,1)S(1)}, u32[]{:S(2)}, u32[]{:S(2)}) %all-to-all-start) | async-done | bytes 172064 | tf_op jit(solution)/shard_map/all_to_all | solution.py:70
  41.5 0.9 collective-permute-done.4
  42.4 0.7 pad_maximum_fusion.p0
  43.2 1.7 broadcast_in_dim.57
  44.9 6.4 %all-to-all-start.1 = ((bf16[16,56,1536]{2,1,0:T(8,128)(2,1)}), bf16[16,56,1536]{2,1,0:T(8,128)(2,1)S(1)}, u32[]{:S(2)}, u32[]{:S(2)}) async-start(bf16[16,56,1536]{2,1,0:T(8,128)(2,1)} %broadcast_in_dim.57), calls=%async_computation.1 | async-start | bytes 5505024 | tf_op jit(solution)/shard_map/all_to_all | solution.py:70
  51.3 4.8 %collective-permute-start.8 = (bf16[384,384]{1,0:T(8,128)(2,1)}, bf16[384,384]{1,0:T(8,128)(2,1)S(1)}, u32[]{:S(2)}, u32[]{:S(2)}) collective-permute-start(bf16[384,384]{1,0:T(8,128)(2,1)} %pad_maximum_fusion.p0), channel_id=1, source_target_pairs={{0,3},{1,0},{2,1},{3,2},{4,7},{5,4},{6,5},{7,6},{8,11},{9,8},{10,9... | collective-permute-start | bytes 884744 | tf_op jit(solution)/shard_map/ppermute | solution.py:297
  56.1 4.6 %collective-permute-start.7 = (bf16[384,384]{1,0:T(8,128)(2,1)}, bf16[384,384]{1,0:T(8,128)(2,1)S(1)}, u32[]{:S(2)}, u32[]{:S(2)}) collective-permute-start(bf16[384,384]{1,0:T(8,128)(2,1)} %pad_maximum_fusion.p0), channel_id=1, source_target_pairs={{0,2},{1,3},{2,0},{3,1},{4,6},{5,7},{6,4},{7,5},{8,10},{9,11},{10,... | collective-permute-start | bytes 884744 | tf_op jit(solution)/shard_map/ppermute | solution.py:297
  60.7 2.6 %collective-permute-start.6 = (bf16[384,384]{1,0:T(8,128)(2,1)}, bf16[384,384]{1,0:T(8,128)(2,1)S(1)}, u32[]{:S(2)}, u32[]{:S(2)}) collective-permute-start(bf16[384,384]{1,0:T(8,128)(2,1)} %pad_maximum_fusion.p0), channel_id=1, source_target_pairs={{0,1},{1,2},{2,3},{3,0},{4,5},{5,6},{6,7},{7,4},{8,9},{9,10},{10,1... | collective-permute-start | bytes 884744 | tf_op jit(solution)/shard_map/ppermute | solution.py:297
  63.3 1.1 copy-done.9
  64.3 1.1 copy-done.25
  65.4 1.1 copy-done.26
  66.5 1.4 shard_map.122
  67.9 0.7 copy-done.10
  68.6 0.8 copy-done.12
  69.4 0.7 copy-done.14
  70.1 0.8 copy-done.16
  70.9 0.8 copy-done.18
  71.6 0.7 copy-done.20
  72.4 9.8 %collective-permute-done.7.p2 = bf16[384,384]{1,0:T(8,128)(2,1)S(1)} collective-permute-done((bf16[384,384]{1,0:T(8,128)(2,1)}, bf16[384,384]{1,0:T(8,128)(2,1)S(1)}, u32[]{:S(2)}, u32[]{:S(2)}) %collective-permute-start.7) | collective-permute-done | bytes 294944 | tf_op jit(solution)/shard_map/ppermute | solution.py:297
  82.2 1.0 shard_map.123
  83.2 0.9 copy-done.5
  84.1 0.9 copy-done.7
  85.0 5.8 %collective-permute-start.9 = (bf16[896,1536]{1,0:T(8,128)(2,1)S(1)}, bf16[896,1536]{1,0:T(8,128)(2,1)S(1)}, u32[]{:S(2)}, u32[]{:S(2)}) collective-permute-start(bf16[896,1536]{1,0:T(8,128)(2,1)S(1)} %bitcast.15), channel_id=1, source_target_pairs={{0,4},{4,0},{8,12},{12,8},{16,20},{20,16},{24,28},{28,24},{32,36},... | collective-permute-start | bytes 8257544 | tf_op jit(solution)/shard_map/ppermute | solution.py:42
  90.9 1.1 copy-done.8
  92.0 1.0 copy-done.17
  93.0 1.0 copy-done.19
  94.0 1.0 copy-done.21
  95.0 3.3 %shard_map.124 = (f32[192,1152]{1,0:T(8,128)S(1)}, f32[192,384]{1,0:T(8,128)S(1)}, f32[192,768]{1,0:T(8,128)S(1)}, f32[384,768]{1,0:T(8,128)S(1)}, f32[128,768]{...) custom-call(s32[6]{0:T(128)S(1)} %stack.35.flags, bf16[4,192,224]{2,1,0:T(8,128)(2,1)S(1)} %copy-done.17, ...), custom_call_target="tpu_custom_call" | custom-call | flops 1000000000 | bytes 8000000 | tf_op jit(solution)/shard_map/pallas_call | solution.py:362
  98.4 8.9 %shard_map.125 = (bf16[192,384]{1,0:T(8,128)(2,1)S(1)}, bf16[192,384]{1,0:T(8,128)(2,1)S(1)}, bf16[384,768]{1,0:T(8,128)(2,1)S(1)}, bf16[384,768]{1,0:T(8,128)(2...) custom-call(s32[6]{0:T(128)S(1)} %stack.35.flags, bf16[4,192,224]{2,1,0:T(8,128)(2,1)S(1)} %copy-done.11, ...), custom_call_target="tpu_custom_call" | custom-call | flops 1000000000 | bytes 8000000 | tf_op jit(solution)/shard_map/pallas_call | solution.py:374
  107.3 0.7 copy-done.22
  108.0 0.8 copy-done.27
  108.8 2.8 %collective-permute-start.10 = (bf16[384,768]{1,0:T(8,128)(2,1)}, bf16[384,768]{1,0:T(8,128)(2,1)}, u32[]{:S(2)}, u32[]{:S(2)}) collective-permute-start(bf16[384,768]{1,0:T(8,128)(2,1)} %get-tuple-element.83), channel_id=1, source_target_pairs={{0,128},{4,132},{8,136},{12,140},{16,144},{20,148},{24,152},{28,15... | collective-permute-start | bytes 1769480 | tf_op jit(solution)/shard_map/ppermute | solution.py:42
  111.6 1.9 %collective-permute-start.11 = (bf16[384,768]{1,0:T(8,128)(2,1)}, bf16[384,768]{1,0:T(8,128)(2,1)}, u32[]{:S(2)}, u32[]{:S(2)}) collective-permute-start(bf16[384,768]{1,0:T(8,128)(2,1)} %get-tuple-element.84), channel_id=1, source_target_pairs={{128,256},{132,260},{136,264},{140,268},{144,272},{148,276},{152,2... | collective-permute-start | bytes 1769480 | tf_op jit(solution)/shard_map/ppermute | solution.py:42
  113.6 1.5 shard_map.126
  115.1 0.8 copy-done.3
  115.9 4.5 %all-to-all-start.2 = ((bf16[4,192,384]{2,1,0:T(8,128)(2,1)}), bf16[4,192,384]{2,1,0:T(8,128)(2,1)}, u32[]{:S(2)}, u32[]{:S(2)}) async-start(bf16[4,192,384]{2,1,0:T(8,128)(2,1)} %copy-done.3), calls=%async_computation.2 | async-start | bytes 1179648 | tf_op jit(solution)/shard_map/all_to_all | solution.py:393
  120.4 5.6 %collective-permute-done.10.got_even = bf16[384,768]{1,0:T(8,128)(2,1)} collective-permute-done((bf16[384,768]{1,0:T(8,128)(2,1)}, bf16[384,768]{1,0:T(8,128)(2,1)}, u32[]{:S(2)}, u32[]{:S(2)}) %collective-permute-start.10) | collective-permute-done | bytes 589856 | tf_op jit(solution)/shard_map/ppermute | solution.py:42
  126.0 2.5 %collective-permute-done.11.got_odd = bf16[384,768]{1,0:T(8,128)(2,1)} collective-permute-done((bf16[384,768]{1,0:T(8,128)(2,1)}, bf16[384,768]{1,0:T(8,128)(2,1)}, u32[]{:S(2)}, u32[]{:S(2)}) %collective-permute-start.11) | collective-permute-done | bytes 589856 | tf_op jit(solution)/shard_map/ppermute | solution.py:42
  128.5 1.1 copy-done.28
  129.6 1.7 shard_map.127
  131.2 3.0 %collective-permute-start.12 = (bf16[192,768]{1,0:T(8,128)(2,1)S(1)}, bf16[192,768]{1,0:T(8,128)(2,1)S(1)}, u32[]{:S(2)}, u32[]{:S(2)}) collective-permute-start(bf16[192,768]{1,0:T(8,128)(2,1)S(1)} %get-tuple-element.86), channel_id=1, source_target_pairs={{0,4},{4,0},{8,12},{12,8},{16,20},{20,16},{24,28},{28,24},{32,36},... | collective-permute-start | bytes 884744 | tf_op jit(solution)/shard_map/ppermute | solution.py:42
  134.2 6.4 %collective-permute-start.13 = (bf16[192,768]{1,0:T(8,128)(2,1)S(1)}, bf16[192,768]{1,0:T(8,128)(2,1)S(1)}, u32[]{:S(2)}, u32[]{:S(2)}) collective-permute-start(bf16[192,768]{1,0:T(8,128)(2,1)S(1)} %get-tuple-element.87), channel_id=1, source_target_pairs={{4,8},{8,4},{12,16},{16,12},{20,24},{24,20},{28,32},{32,28},{36,40... | collective-permute-start | bytes 884744 | tf_op jit(solution)/shard_map/ppermute | solution.py:42
  140.7 17.2 %collective-permute-done.13.in_b = bf16[192,768]{1,0:T(8,128)(2,1)S(1)} collective-permute-done((bf16[192,768]{1,0:T(8,128)(2,1)S(1)}, bf16[192,768]{1,0:T(8,128)(2,1)S(1)}, u32[]{:S(2)}, u32[]{:S(2)}) %collective-permute-start.13) | collective-permute-done | bytes 294944 | tf_op jit(solution)/shard_map/ppermute | solution.py:42
  157.9 2.3 %shard_map.128 = bf16[4,192,384]{2,1,0:T(8,128)(2,1)S(1)} custom-call(f32[192,768]{1,0:T(8,128)S(1)} %get-tuple-element.85.own, bf16[192,768]{1,0:T(8,128)(2,1)S(1)} %collective-permute-done.12.in_a, bf16[192,768]{1,0:T(8,128)(2,1)S(1)} %collective-permute-done.13.in_b, f32[192,384]{1,0:T(8,128)S(1)} %copy-done.23, f32[1,384]{1,0:T(1,128)S(1)} %broadcast_in_dim.59.k_gain, ...), custom_call_target="tpu_custom_call" | custom-call | flops 1000000000 | bytes 8000000 | tf_op jit(solution)/shard_map/pallas_call | solution.py:402
  160.2 0.8 copy-done.4
  161.1 3.5 %all-to-all-start.3 = ((bf16[4,192,384]{2,1,0:T(8,128)(2,1)}), bf16[4,192,384]{2,1,0:T(8,128)(2,1)S(1)}, u32[]{:S(2)}, u32[]{:S(2)}) async-start(bf16[4,192,384]{2,1,0:T(8,128)(2,1)} %copy-done.4), calls=%async_computation.3 | async-start | bytes 1179648 | tf_op jit(solution)/shard_map/all_to_all | solution.py:405
  164.5 1.9 %fusion.5 = bf16[192,384]{1,0:T(8,128)(2,1)} fusion(bf16[4,192,384]{2,1,0:T(8,128)(2,1)} %all-to-all-done.2), kind=kLoop, calls=%fused_computation.15 | loop fusion | flops 589824 | bytes 737280 | tf_op jit(solution)/shard_map/add | solution.py:292
  166.4 7.9 %all-to-all-done.3 = bf16[4,192,384]{2,1,0:T(8,128)(2,1)S(1)} async-done(((bf16[4,192,384]{2,1,0:T(8,128)(2,1)}), bf16[4,192,384]{2,1,0:T(8,128)(2,1)S(1)}, u32[]{:S(2)}, u32[]{:S(2)}) %all-to-all-start.3) | async-done | bytes 589856 | tf_op jit(solution)/shard_map/all_to_all | solution.py:405
  174.3 0.7 fusion.6
  (69 shorter events, 0.5 us)
Async XLA Ops:
  0.6 29.2 %copy-start = (s32[128,2]{0,1:T(2,128)S(1)}, s32[128,2]{0,1:T(2,128)}, u32[]{:S(2)}) copy-start(s32[128,2]{0,1:T(2,128)} %param.20) | copy-start | bytes 3076
  1.6 30.3 %collective-permute-start.1 = (bf16[192,384]{1,0:T(8,128)(2,1)S(1)}, bf16[192,384]{1,0:T(8,128)(2,1)S(1)}, u32[]{:S(2)}, u32[]{:S(2)}) collective-permute-start(bf16[192,384]{1,0:T(8,128)(2,1)S(1)} %constant_dynamic-slice_fusion), channel_id=1, source_target_pairs={{4,8},{8,4},{12,16},{16,12},{20,24},{24,20},{28,32},{32,28},{36,40... | collective-permute-start | bytes 442376 | tf_op jit(solution)/shard_map/ppermute | solution.py:42
  10.6 21.2 %collective-permute-start = (bf16[192,384]{1,0:T(8,128)(2,1)S(1)}, bf16[192,384]{1,0:T(8,128)(2,1)S(1)}, u32[]{:S(2)}, u32[]{:S(2)}) collective-permute-start(bf16[192,384]{1,0:T(8,128)(2,1)S(1)} %constant_dynamic-slice_fusion), channel_id=1, source_target_pairs={{0,4},{4,0},{8,12},{12,8},{16,20},{20,16},{24,28},{28,24},{32,36},... | collective-permute-start | bytes 442376 | tf_op jit(solution)/shard_map/ppermute | solution.py:42
  12.6 19.4 %collective-permute-start.2 = (bf16[192,1536]{1,0:T(8,128)(2,1)}, bf16[192,1536]{1,0:T(8,128)(2,1)S(1)}, u32[]{:S(2)}, u32[]{:S(2)}) collective-permute-start(bf16[192,1536]{1,0:T(8,128)(2,1)} %refs_0_.1), channel_id=1, source_target_pairs={{0,128},{4,132},{8,136},{12,140},{16,144},{20,148},{24,152},{28,15... | collective-permute-start | bytes 1769480 | tf_op jit(solution)/shard_map/ppermute | solution.py:42
  15.4 16.5 %collective-permute-start.3 = (bf16[192,1536]{1,0:T(8,128)(2,1)}, bf16[192,1536]{1,0:T(8,128)(2,1)S(1)}, u32[]{:S(2)}, u32[]{:S(2)}) collective-permute-start(bf16[192,1536]{1,0:T(8,128)(2,1)} %refs_0_.1), channel_id=1, source_target_pairs={{128,256},{132,260},{136,264},{140,268},{144,272},{148,276},{152,2... | collective-permute-start | bytes 1769480 | tf_op jit(solution)/shard_map/ppermute | solution.py:42
  18.8 22.7 %all-to-all-start = ((bf16[4,14,1536]{2,1,0:T(8,128)(2,1)}), bf16[4,14,1536]{2,1,0:T(8,128)(2,1)S(1)}, u32[]{:S(2)}, u32[]{:S(2)}) async-start(bf16[4,14,1536]{2,1,0:T(8,128)(2,1)} %broadcast_in_dim.30), calls=%async_computation | async-start | bytes 393216 | tf_op jit(solution)/shard_map/all_to_all | solution.py:70
  32.8 8.7 %collective-permute-start.5 = (bf16[192,384]{1,0:T(8,128)(2,1)S(1)}, bf16[192,384]{1,0:T(8,128)(2,1)S(1)}, u32[]{:S(2)}, u32[]{:S(2)}) collective-permute-start(bf16[192,384]{1,0:T(8,128)(2,1)S(1)} %broadcast_select_fusion.2), channel_id=1, source_target_pairs={{128,256},{132,260},{136,264},{140,268},{144,272},{148,276},{152,2... | collective-permute-start | bytes 442376 | tf_op jit(solution)/shard_map/ppermute | solution.py:42
  36.2 6.2 %collective-permute-start.4 = (bf16[192,384]{1,0:T(8,128)(2,1)S(1)}, bf16[192,384]{1,0:T(8,128)(2,1)S(1)}, u32[]{:S(2)}, u32[]{:S(2)}) collective-permute-start(bf16[192,384]{1,0:T(8,128)(2,1)S(1)} %broadcast_select_fusion.2), channel_id=1, source_target_pairs={{0,128},{4,132},{8,136},{12,140},{16,144},{20,148},{24,152},{28,15... | collective-permute-start | bytes 442376 | tf_op jit(solution)/shard_map/ppermute | solution.py:42
  44.9 40.1 %all-to-all-start.1 = ((bf16[16,56,1536]{2,1,0:T(8,128)(2,1)}), bf16[16,56,1536]{2,1,0:T(8,128)(2,1)S(1)}, u32[]{:S(2)}, u32[]{:S(2)}) async-start(bf16[16,56,1536]{2,1,0:T(8,128)(2,1)} %broadcast_in_dim.57), calls=%async_computation.1 | async-start | bytes 5505024 | tf_op jit(solution)/shard_map/all_to_all | solution.py:70
  51.3 21.1 %collective-permute-start.8 = (bf16[384,384]{1,0:T(8,128)(2,1)}, bf16[384,384]{1,0:T(8,128)(2,1)S(1)}, u32[]{:S(2)}, u32[]{:S(2)}) collective-permute-start(bf16[384,384]{1,0:T(8,128)(2,1)} %pad_maximum_fusion.p0), channel_id=1, source_target_pairs={{0,3},{1,0},{2,1},{3,2},{4,7},{5,4},{6,5},{7,6},{8,11},{9,8},{10,9... | collective-permute-start | bytes 884744 | tf_op jit(solution)/shard_map/ppermute | solution.py:297
  56.1 26.1 %collective-permute-start.7 = (bf16[384,384]{1,0:T(8,128)(2,1)}, bf16[384,384]{1,0:T(8,128)(2,1)S(1)}, u32[]{:S(2)}, u32[]{:S(2)}) collective-permute-start(bf16[384,384]{1,0:T(8,128)(2,1)} %pad_maximum_fusion.p0), channel_id=1, source_target_pairs={{0,2},{1,3},{2,0},{3,1},{4,6},{5,7},{6,4},{7,5},{8,10},{9,11},{10,... | collective-permute-start | bytes 884744 | tf_op jit(solution)/shard_map/ppermute | solution.py:297
  60.7 21.6 %collective-permute-start.6 = (bf16[384,384]{1,0:T(8,128)(2,1)}, bf16[384,384]{1,0:T(8,128)(2,1)S(1)}, u32[]{:S(2)}, u32[]{:S(2)}) collective-permute-start(bf16[384,384]{1,0:T(8,128)(2,1)} %pad_maximum_fusion.p0), channel_id=1, source_target_pairs={{0,1},{1,2},{2,3},{3,0},{4,5},{5,6},{6,7},{7,4},{8,9},{9,10},{10,1... | collective-permute-start | bytes 884744 | tf_op jit(solution)/shard_map/ppermute | solution.py:297
  63.3 1.1 copy-start.9
  64.3 1.1 copy-start.25
  65.4 1.1 copy-start.26
  66.5 15.8 %copy-start.24 = (bf16[384,384]{1,0:T(8,128)(2,1)S(1)}, bf16[384,384]{1,0:T(8,128)(2,1)}, u32[]{:S(2)}) copy-start(bf16[384,384]{1,0:T(8,128)(2,1)} %pad_maximum_fusion.p0) | copy-start | bytes 884740
  67.9 0.8 copy-start.10
  68.6 0.8 copy-start.12
  69.4 0.8 copy-start.14
  70.1 0.8 copy-start.16
  70.9 0.8 copy-start.18
  71.6 0.7 copy-start.20
  72.4 18.5 %copy-start.29 = (f32[384]{0:T(512)S(1)}, f32[384]{0:T(512)}, u32[]{:S(2)}) copy-start(f32[384]{0:T(512)} %param.18) | copy-start | bytes 4612
  72.4 18.5 %copy-start.30 = (f32[384]{0:T(512)S(1)}, f32[384]{0:T(512)}, u32[]{:S(2)}) copy-start(f32[384]{0:T(512)} %param.17) | copy-start | bytes 4612
  83.2 0.9 copy-start.5
  84.1 0.9 copy-start.7
  85.0 13.3 %copy-start.6 = (bf16[4,384,224]{2,1,0:T(8,128)(2,1)S(1)}, bf16[4,384,224]{2,1,0:T(8,128)(2,1)}, u32[]{:S(2)}) copy-start(bf16[4,384,224]{2,1,0:T(8,128)(2,1)} %copy-done.5) | copy-start | bytes 2064388
  85.0 13.3 %collective-permute-start.9 = (bf16[896,1536]{1,0:T(8,128)(2,1)S(1)}, bf16[896,1536]{1,0:T(8,128)(2,1)S(1)}, u32[]{:S(2)}, u32[]{:S(2)}) collective-permute-start(bf16[896,1536]{1,0:T(8,128)(2,1)S(1)} %bitcast.15), channel_id=1, source_target_pairs={{0,4},{4,0},{8,12},{12,8},{16,20},{20,16},{24,28},{28,24},{32,36},... | collective-permute-start | bytes 8257544 | tf_op jit(solution)/shard_map/ppermute | solution.py:42
  90.9 1.1 copy-start.8
  92.0 1.0 copy-start.17
  93.0 1.0 copy-start.19
  94.0 1.0 copy-start.21
  95.0 3.3 %copy-start.11 = (bf16[4,192,224]{2,1,0:T(8,128)(2,1)S(1)}, bf16[4,192,224]{2,1,0:T(8,128)(2,1)}, u32[]{:S(2)}) copy-start(bf16[4,192,224]{2,1,0:T(8,128)(2,1)} %copy-done.10) | copy-start | bytes 1032196
  95.0 3.3 %copy-start.13 = (bf16[4,192,224]{2,1,0:T(8,128)(2,1)S(1)}, bf16[4,192,224]{2,1,0:T(8,128)(2,1)}, u32[]{:S(2)}) copy-start(bf16[4,192,224]{2,1,0:T(8,128)(2,1)} %copy-done.12) | copy-start | bytes 1032196
  95.0 3.3 %copy-start.15 = (bf16[4,192,224]{2,1,0:T(8,128)(2,1)S(1)}, bf16[4,192,224]{2,1,0:T(8,128)(2,1)}, u32[]{:S(2)}) copy-start(bf16[4,192,224]{2,1,0:T(8,128)(2,1)} %copy-done.14) | copy-start | bytes 1032196
  98.3 15.3 %copy-start.1 = (bf16[896,1536]{1,0:T(8,128)(2,1)}, bf16[896,1536]{1,0:T(8,128)(2,1)S(1)}, u32[]{:S(2)}) copy-start(bf16[896,1536]{1,0:T(8,128)(2,1)S(1)} %collective-permute-done.9.wt) | copy-start | bytes 8257540
  107.3 0.7 copy-start.22
  108.0 0.8 copy-start.27
  108.8 17.2 %collective-permute-start.10 = (bf16[384,768]{1,0:T(8,128)(2,1)}, bf16[384,768]{1,0:T(8,128)(2,1)}, u32[]{:S(2)}, u32[]{:S(2)}) collective-permute-start(bf16[384,768]{1,0:T(8,128)(2,1)} %get-tuple-element.83), channel_id=1, source_target_pairs={{0,128},{4,132},{8,136},{12,140},{16,144},{20,148},{24,152},{28,15... | collective-permute-start | bytes 1769480 | tf_op jit(solution)/shard_map/ppermute | solution.py:42
  111.6 16.8 %collective-permute-start.11 = (bf16[384,768]{1,0:T(8,128)(2,1)}, bf16[384,768]{1,0:T(8,128)(2,1)}, u32[]{:S(2)}, u32[]{:S(2)}) collective-permute-start(bf16[384,768]{1,0:T(8,128)(2,1)} %get-tuple-element.84), channel_id=1, source_target_pairs={{128,256},{132,260},{136,264},{140,268},{144,272},{148,276},{152,2... | collective-permute-start | bytes 1769480 | tf_op jit(solution)/shard_map/ppermute | solution.py:42
  115.1 0.8 copy-start.3
  115.9 45.2 %all-to-all-start.2 = ((bf16[4,192,384]{2,1,0:T(8,128)(2,1)}), bf16[4,192,384]{2,1,0:T(8,128)(2,1)}, u32[]{:S(2)}, u32[]{:S(2)}) async-start(bf16[4,192,384]{2,1,0:T(8,128)(2,1)} %copy-done.3), calls=%async_computation.2 | async-start | bytes 1179648 | tf_op jit(solution)/shard_map/all_to_all | solution.py:393
  128.5 1.1 copy-start.28
  129.6 28.3 %copy-start.2 = (bf16[896,1536]{1,0:T(8,128)(2,1)S(1)}, bf16[896,1536]{1,0:T(8,128)(2,1)}, u32[]{:S(2)}) copy-start(bf16[896,1536]{1,0:T(8,128)(2,1)} %copy-done.1) | copy-start | bytes 8257540
  129.6 28.3 %copy-start.23 = (f32[192,384]{1,0:T(8,128)S(1)}, f32[192,384]{1,0:T(8,128)}, u32[]{:S(2)}) copy-start(f32[192,384]{1,0:T(8,128)} %copy-done.22) | copy-start | bytes 884740
  131.2 9.4 %collective-permute-start.12 = (bf16[192,768]{1,0:T(8,128)(2,1)S(1)}, bf16[192,768]{1,0:T(8,128)(2,1)S(1)}, u32[]{:S(2)}, u32[]{:S(2)}) collective-permute-start(bf16[192,768]{1,0:T(8,128)(2,1)S(1)} %get-tuple-element.86), channel_id=1, source_target_pairs={{0,4},{4,0},{8,12},{12,8},{16,20},{20,16},{24,28},{28,24},{32,36},... | collective-permute-start | bytes 884744 | tf_op jit(solution)/shard_map/ppermute | solution.py:42
  134.2 23.6 %collective-permute-start.13 = (bf16[192,768]{1,0:T(8,128)(2,1)S(1)}, bf16[192,768]{1,0:T(8,128)(2,1)S(1)}, u32[]{:S(2)}, u32[]{:S(2)}) collective-permute-start(bf16[192,768]{1,0:T(8,128)(2,1)S(1)} %get-tuple-element.87), channel_id=1, source_target_pairs={{4,8},{8,4},{12,16},{16,12},{20,24},{24,20},{28,32},{32,28},{36,40... | collective-permute-start | bytes 884744 | tf_op jit(solution)/shard_map/ppermute | solution.py:42
  160.2 0.8 copy-start.4
  161.1 13.3 %all-to-all-start.3 = ((bf16[4,192,384]{2,1,0:T(8,128)(2,1)}), bf16[4,192,384]{2,1,0:T(8,128)(2,1)S(1)}, u32[]{:S(2)}, u32[]{:S(2)}) async-start(bf16[4,192,384]{2,1,0:T(8,128)(2,1)} %copy-done.4), calls=%async_computation.3 | async-start | bytes 1179648 | tf_op jit(solution)/shard_map/all_to_all | solution.py:405

commit v6 on v5

--- a/solution.py
+++ b/solution.py
@@ -15,7 +15,7 @@
 EPS = 1e-6
 SCALE = HD**-0.5
 OUT_COST = 10**9
-TERM_COST = 10**11
+TURN_COST = 10**11
 GRAD_COST = 10**9
 BLOCK = 56
 PART = 4 * BLOCK
@@ -129,19 +129,19 @@
 KV = slice(0, 2 * W)
 LAST = slice(3 * W, 4 * W)
 HALF_TEXT = TEXT // 2
-
-
-def pick_rows(rows, pick, out):
-    for j in range(4):
-        out[j] = dot(rows[:, j * W : (j + 1) * W], pick[...]).astype(BF16)
-
-
-def pick_kernel(*refs):
-    n = (len(refs) - 2) // 3
-    pick_o, pick_t = refs[n], refs[n + 1]
-    for i in range(n):
-        pick_rows(refs[i], pick_o, refs[n + 2 + 2 * i])
-        pick_rows(refs[i], pick_t, refs[n + 3 + 2 * i])
+OWN = slice(0, ROWS)
+GIVEN = slice(ROWS, 2 * ROWS)
+KRAW = slice(2 * ROWS, 3 * ROWS)
+D_Q = slice(3 * ROWS, 4 * ROWS)
+BEHIND = slice(2 * ROWS, 3 * ROWS)
+
+
+def pick_kernel(x, g, f, pick_o, pick_t, out_o, out_t):
+    for n, rows in enumerate((x, g, f)):
+        at = slice(n * ROWS, (n + 1) * ROWS)
+        for j in range(4):
+            out_o[j, at] = dot(rows[:, j * W : (j + 1) * W], pick_o[...]).astype(BF16)
+            out_t[j, at] = dot(rows[:, j * W : (j + 1) * W], pick_t[...]).astype(BF16)
 
 
 def pick_parts_kernel(p0, p1, p2, p3, pick_o, pick_t, out_o, out_t):
@@ -150,14 +150,14 @@
         out_t[n] = dot(part[...], pick_t[...]).astype(BF16)
 
 
-def project(picked, w, cols, order=(0, 1, 2, 3)):
+def project(picked, w, cols, order=(0, 1, 2, 3), at=slice(None)):
     acc = None
     for n, j in enumerate(order):
         if isinstance(j, int):
             rows = w[j * PART : (j + 1) * PART, cols]
         else:
             rows = w[pl.ds(pl.multiple_of(j * PART, PART), PART), cols]
-        term = dot(picked[n], rows)
+        term = dot(picked[n][at] if isinstance(picked, list) else picked[n, at], rows)
         acc = term if acc is None else acc + term
     return acc
 
@@ -171,22 +171,21 @@
 
 
 def first_kernel(
-    flags, x, g, f, p, pick_o, pick_t, lines, w, acc_x, acc_g, acc_f, acc_p, acc_t, text
+    flags, r, p, pick_o, pick_t, lines, w, acc_x, acc_g, acc_f, acc_p, acc_t, text
 ):
-    acc_x[...] = project(x, w, KVQ)
-    acc_g[...] = project(g, w, LAST)
-    acc_f[...] = project(f, w, KV)
+    acc_x[...] = project(r, w, KVQ, at=OWN)
+    acc_g[...] = project(r, w, LAST, at=GIVEN)
+    acc_f[...] = project(r, w, KV, at=BEHIND)
     acc_p[...] = project(p, w, KV, part_order(flags))
     t = dot(lines[...], w[...]).astype(BF16)
     acc_t[...] = project(picked_value(t, pick_o), w, KV)
-    pick_rows(t, pick_t, text)
+    for j, rows in enumerate(picked_value(t, pick_t)):
+        text[j] = rows
 
 
 def attend_kernel(
     flags,
-    x,
-    g,
-    f,
+    r,
     p,
     text,
     pick_o,
@@ -203,22 +202,23 @@
     k_gain,
     bias,
     att,
-    dq,
-    near_t,
+    keep,
     even_t,
     odd_t,
-    kraw,
     keys,
 ):
     n = 4 * ROWS
-    mine = acc_x[...] + project(x, wt, KVQ)
-    d_att = (acc_g[...] + project(g, wt, LAST)).astype(BF16)
-    behind = acc_f[...] + project(f, wt, KV)
+    mine = acc_x[...] + project(r, wt, KVQ, at=OWN)
+    d_att = (acc_g[...] + project(r, wt, LAST, at=GIVEN)).astype(BF16)
+    behind = acc_f[...] + project(r, wt, KV, at=BEHIND)
     beside = acc_p[...] + project(p, wt, KV, part_order(flags))
     words = acc_t[...] + project(text, wt, KV)
     t = dot(lines[...], wt[...]).astype(BF16)
     more = project(picked_value(t, pick_o), wo, KV) + project(picked_value(t, pick_t), wt, KV)
-    kraw[...] = mine[:, :W]
+    high = mine[:, :W].astype(BF16)
+    keep[KRAW, :W] = high
+    keep[KRAW, W:] = (mine[:, :W] - high.astype(F32)).astype(BF16)
+    keep[D_Q, W:] = jnp.zeros((ROWS, W), BF16)
     low = 0
     for values in (mine, beside[:ROWS], behind, beside[ROWS:], words, more):
         high = low + values.shape[0]
@@ -243,11 +243,11 @@
         dp = dot(dh, vh, NT)
         ds = (p_h * (dp - jnp.sum(p_h * dp, axis=-1, keepdims=True))).astype(BF16)
         d_q = dot(ds, kh) * SCALE
-        dq[:, head(h)] = norm_pull(q, q_gain[:, head(h)], d_q).astype(BF16)
+        keep[D_Q, head(h)] = norm_pull(q, q_gain[:, head(h)], d_q).astype(BF16)
         kt = dot(ds[:, :n], qh, TN) * SCALE
         vt = dot(pb[:, :n], dh, TN)
         for lanes, term in ((head(h), kt), (val(h), vt)):
-            near_t[:, lanes] = term[: 2 * ROWS].astype(BF16)
+            keep[: 2 * ROWS, lanes] = term[: 2 * ROWS].astype(BF16)
             even_t[:, lanes] = (term[2 * ROWS :] * even).astype(BF16)
             odd_t[:, lanes] = (term[2 * ROWS :] * odd).astype(BF16)
 
@@ -260,21 +260,22 @@
         out[j] = (dot(o, pick_o[...], NT) + dot(t, pick_t[...], NT)).astype(BF16)
 
 
-def term_kernel(flags, near_t, got_even, got_odd, own, to_mate, to_next):
-    total = near_t[...].astype(F32) + got_even[...].astype(F32) + got_odd[...].astype(F32)
+def turn_kernel(flags, keep, got_even, got_odd, own, to_next, to_mate):
+    total = keep[: 2 * ROWS, :].astype(F32) + got_even[...].astype(F32) + got_odd[...].astype(F32)
     own[...] = total[:ROWS]
     mate = flags[1].astype(F32)
+    to_next[...] = (total[ROWS:] * (1.0 - mate)).astype(BF16)
     to_mate[...] = (total[ROWS:] * mate).astype(BF16)
-    to_next[...] = (total[ROWS:] * (1.0 - mate)).astype(BF16)
-
-
-def grad_kernel(own, in_a, in_b, kraw, k_gain, dq, wo, wt, pick_o, pick_t, out):
-    total = own[...] + in_a[...].astype(F32) + in_b[...].astype(F32)
+
+
+def grad_kernel(own, from_next, from_mate, keep, k_gain, wo, wt, pick_o, pick_t, out):
+    total = own[...] + from_next[...].astype(F32) + from_mate[...].astype(F32)
+    kraw = keep[KRAW, :W].astype(F32) + keep[KRAW, W:].astype(F32)
     parts = [
         norm_pull(kraw[:, head(h)], k_gain[:, head(h)], total[:, head(h)]).astype(BF16)
         for h in range(NH)
     ]
-    d = jnp.concatenate(parts + [total[:, W:].astype(BF16), dq[...]], axis=1)
+    d = jnp.concatenate(parts + [total[:, W:].astype(BF16), keep[D_Q, :W]], axis=1)
     for j in range(4):
         rows = slice(j * PART, (j + 1) * PART)
         o = dot(d, wo[rows, KVQ], NT).astype(BF16)
@@ -336,26 +337,23 @@
     four = over_zh(jnp.concatenate([mine, x_text], axis=0))
     behind = jnp.where(use_even, row_even(x_tiles), row_odd(x_tiles))
     side = jnp.where(use_core, core_mate(quarter), next_chip(quarter))
-    side, behind, pick_o, pick_t, flags = lax.optimization_barrier(
-        (side, behind, pick_o, pick_t, flags)
-    )
+    side, behind = lax.optimization_barrier((side, behind))
     c_even, c_odd = row_even(side), row_odd(side)
     four, c_even, c_odd = lax.optimization_barrier((four, c_even, c_odd))
     corner = jnp.where(use_even, c_even, c_odd)
     beside = jnp.concatenate([side, corner])
     block = jnp.concatenate([four[:, :12].reshape(48, 1536), four[:, 12:].reshape(8, 1536)], axis=0)
-    block, beside, lines, bias = lax.optimization_barrier((block, beside, lines, bias))
+    block, beside = lax.optimization_barrier((block, beside))
     parts = [beside] + [head_shift(beside, by) for by in (1, 2, 3)]
     wo = over_xy(block).reshape(16 * BLOCK, 1536)
-    picked = shape((4, ROWS, PART), BF16)
-    x_o, x_t, g_o, g_t, f_o, f_t = call(pick_kernel, (picked,) * 6, "v" * 5)(
+    r_o, r_t = call(pick_kernel, (shape((4, 3 * ROWS, PART), BF16),) * 2, "v" * 5)(
         x_tiles, grad_out, behind, pick_o, pick_t
     )
     p_o, p_t = call(pick_parts_kernel, (shape((4, 2 * ROWS, PART), BF16),) * 2, "v" * 6)(
         *parts, pick_o, pick_t
     )
-    wo, x_o, x_t, g_o, g_t, f_o, f_t, p_o, p_t = lax.optimization_barrier(
-        (wo, x_o, x_t, g_o, g_t, f_o, f_t, p_o, p_t)
+    wo, r_o, r_t, p_o, p_t, lines, bias, flags = lax.optimization_barrier(
+        (wo, r_o, r_t, p_o, p_t, lines, bias, flags)
     )
     wt = core_mate(wo)
 
@@ -369,38 +367,35 @@
             shape((HALF_TEXT, 2 * W), F32),
             shape((4, HALF_TEXT, PART), BF16),
         ),
-        "s" + "v" * 8,
-    )(flags, x_o, g_o, f_o, p_o, pick_o, pick_t, lines, wo)
-    att, dq, near_t, even_t, odd_t, kraw = call(
+        "s" + "v" * 6,
+    )(flags, r_o, p_o, pick_o, pick_t, lines, wo)
+    att, keep, *terms = call(
         attend_kernel,
         (
             shape((ROWS, W), BF16),
-            shape((ROWS, W), BF16),
-            shape((2 * ROWS, 768), BF16),
-            shape((2 * ROWS, 768), BF16),
-            shape((2 * ROWS, 768), BF16),
-            shape((ROWS, W), F32),
+            shape((4 * ROWS, 2 * W), BF16),
+            *[shape((2 * ROWS, 2 * W), BF16)] * 2,
         ),
-        "s" + "v" * 18,
+        "s" + "v" * 16,
         scratch=[pltpu.VMEM((1024, 768), BF16)],
         mib=28,
-    )(flags, x_t, g_t, f_t, p_t, text, pick_o, pick_t, lines, wo, wt, *accs, q_gain, k_gain, bias)
-
-    got_even, got_odd = row_even(even_t), row_odd(odd_t)
+    )(flags, r_t, p_t, text, pick_o, pick_t, lines, wo, wt, *accs, q_gain, k_gain, bias)
+
     out = call(out_kernel, shape((4, ROWS, W), BF16), "v" * 5, flops=OUT_COST)(
         att, wo, wt, pick_o, pick_t
     )
     outs = lax.all_to_all(out, "heads", 0, 0)
-    own_t, to_mate, to_next = call(
-        term_kernel,
-        (shape((ROWS, 768), F32), shape((ROWS, 768), BF16), shape((ROWS, 768), BF16)),
+
+    even_t, odd_t = terms
+    own, to_next, to_mate = call(
+        turn_kernel,
+        (shape((ROWS, 2 * W), F32), *[shape((ROWS, 2 * W), BF16)] * 2),
         "svvv",
         mib=8,
-        flops=TERM_COST,
-    )(flags, near_t, got_even, got_odd)
-    mate_t, next_t = core_mate(to_mate), next_chip(to_next)
-    grad = call(grad_kernel, shape((4, ROWS, W), BF16), "v" * 10, flops=GRAD_COST)(
-        own_t, mate_t, next_t, kraw, k_gain, dq, wo, wt, pick_o, pick_t
+        flops=TURN_COST,
+    )(flags, keep, row_even(even_t), row_odd(odd_t))
+    grad = call(grad_kernel, shape((4, ROWS, W), BF16), "v" * 9, flops=GRAD_COST)(
+        own, next_chip(to_next), core_mate(to_mate), keep, k_gain, wo, wt, pick_o, pick_t
     )
     grads = lax.all_to_all(grad, "heads", 0, 0)
     return (head_total(outs), head_total(grads))

time: 176 us -> 172 us (0.977)
  the two profiles are of different devices: /device:TPU:29 before, /device:TPU:25 now
where the time goes in v6:
time: 172 us; the launch traced here: 169 us
  starting transfers between devices  79.1 us (46%)
  waiting for transfers between devices  43.4 us (25%)
  Pallas kernels  21 us (12%)
  local copies, waits for them, and re-layouts  17.5 us (10%)
  other arithmetic  5.54 us (3%)
  between operations  2.36 us (1%)
    ppermute x11, starting transfers between devices, seq_move(): return lax.ppermute(value, 'seq', pairs)  42.1 us
    ppermute x11, waiting for transfers between devices, seq_move(): return lax.ppermute(value, 'seq', pairs)  21.4 us
    all_to_all x2, starting transfers between devices, give_all(): return lax.all_to_all(copies, 'seq', 0, 0, axis_index_groups=groups)  16.5 us
    unnamed x44, local copies, waits for them, and re-layouts  13.4 us
    ppermute x3, starting transfers between devices, head_shift(): return lax.ppermute(value, 'heads', [(i, (i + by) % 4) for i in range(4)])  12.8 us
    ppermute x3, waiting for transfers between devices, head_shift(): return lax.ppermute(value, 'heads', [(i, (i + by) % 4) for i in range(4)])  12.2 us
    pallas_call x1, Pallas kernels, per_device(): call(attend_kernel, (shape((ROWS, W), BF16), shape((4 * ROWS, 2 * W), BF1...  8.95 us
    all_to_all x1, waiting for transfers between devices, per_device(): grads = lax.all_to_all(grad, 'heads', 0, 0)  7.94 us
  transfers between devices with their start and end apart: 18, of which 6 were waited for; matrix products, arithmetic and copies ran while one was open for 3% of the time, Pallas kernels for 7%

profile of v6, /device:TPU:25, one launch (start us, length us, event | category | flops | bytes accessed | tf_op | source)
XLA Modules:
  0.0 168.8 jit_solution(15658802537577869725)
XLA Ops:
  0.6 0.0 copy-start
  0.7 0.9 constant_dynamic-slice_fusion
  1.6 9.0 %collective-permute-start.1 = (bf16[192,384]{1,0:T(8,128)(2,1)S(1)}, bf16[192,384]{1,0:T(8,128)(2,1)S(1)}, u32[]{:S(2)}, u32[]{:S(2)}) collective-permute-start(bf16[192,384]{1,0:T(8,128)(2,1)S(1)} %constant_dynamic-slice_fusion), channel_id=1, source_target_pairs={{4,8},{8,4},{12,16},{16,12},{20,24},{24,20},{28,32},{32,28},{36,40... | collective-permute-start | bytes 442376 | tf_op jit(solution)/shard_map/ppermute | solution.py:42
  10.6 1.9 %collective-permute-start = (bf16[192,384]{1,0:T(8,128)(2,1)S(1)}, bf16[192,384]{1,0:T(8,128)(2,1)S(1)}, u32[]{:S(2)}, u32[]{:S(2)}) collective-permute-start(bf16[192,384]{1,0:T(8,128)(2,1)S(1)} %constant_dynamic-slice_fusion), channel_id=1, source_target_pairs={{0,4},{4,0},{8,12},{12,8},{16,20},{20,16},{24,28},{28,24},{32,36},... | collective-permute-start | bytes 442376 | tf_op jit(solution)/shard_map/ppermute | solution.py:42
  12.6 3.1 %collective-permute-start.2 = (bf16[192,1536]{1,0:T(8,128)(2,1)}, bf16[192,1536]{1,0:T(8,128)(2,1)S(1)}, u32[]{:S(2)}, u32[]{:S(2)}) collective-permute-start(bf16[192,1536]{1,0:T(8,128)(2,1)} %x.3), channel_id=1, source_target_pairs={{0,128},{4,132},{8,136},{12,140},{16,144},{20,148},{24,152},{28,15... | collective-permute-start | bytes 1769480 | tf_op jit(solution)/shard_map/ppermute | solution.py:42
  15.7 0.7 collective-permute-start.3
  16.4 0.8 pad_maximum_fusion.2
  17.2 0.7 broadcast_in_dim.30
  17.9 10.0 %all-to-all-start = ((bf16[4,14,1536]{2,1,0:T(8,128)(2,1)}), bf16[4,14,1536]{2,1,0:T(8,128)(2,1)S(1)}, u32[]{:S(2)}, u32[]{:S(2)}) async-start(bf16[4,14,1536]{2,1,0:T(8,128)(2,1)} %broadcast_in_dim.30), calls=%async_computation | async-start | bytes 393216 | tf_op jit(solution)/shard_map/all_to_all | solution.py:70
  27.9 0.1 constant_dynamic-slice_fusion.1
  28.0 0.5 fusion.29
  29.8 0.0 collective-permute-done.1
  29.8 0.0 collective-permute-done
  29.8 0.0 collective-permute-done.2
  29.9 0.0 collective-permute-done.3
  29.9 0.9 broadcast_select_fusion.f
  30.8 0.7 collective-permute-start.5
  31.4 7.3 %collective-permute-start.4 = (bf16[192,384]{1,0:T(8,128)(2,1)S(1)}, bf16[192,384]{1,0:T(8,128)(2,1)S(1)}, u32[]{:S(2)}, u32[]{:S(2)}) collective-permute-start(bf16[192,384]{1,0:T(8,128)(2,1)S(1)} %broadcast_select_fusion.2), channel_id=1, source_target_pairs={{0,128},{4,132},{8,136},{12,140},{16,144},{20,148},{24,152},{28,15... | collective-permute-start | bytes 442376 | tf_op jit(solution)/shard_map/ppermute | solution.py:42
  38.7 1.9 %all-to-all-done = bf16[4,14,1536]{2,1,0:T(8,128)(2,1)S(1)} async-done(((bf16[4,14,1536]{2,1,0:T(8,128)(2,1)}), bf16[4,14,1536]{2,1,0:T(8,128)(2,1)S(1)}, u32[]{:S(2)}, u32[]{:S(2)}) %all-to-all-start) | async-done | bytes 172064 | tf_op jit(solution)/shard_map/all_to_all | solution.py:70
  40.6 0.9 collective-permute-done.4
  41.5 0.8 pad_maximum_fusion.p0
  42.4 1.7 %broadcast_in_dim.31 = bf16[16,56,1536]{2,1,0:T(8,128)(2,1)} broadcast(bf16[56,1536]{1,0:T(8,128)(2,1)S(1)} %pad_maximum_fusion.1), dimensions={1,2} | broadcast | bytes 2924544 | tf_op jit(solution)/shard_map/broadcast_in_dim | solution.py:69
  44.1 6.5 %all-to-all-start.1 = ((bf16[16,56,1536]{2,1,0:T(8,128)(2,1)}), bf16[16,56,1536]{2,1,0:T(8,128)(2,1)S(1)}, u32[]{:S(2)}, u32[]{:S(2)}) async-start(bf16[16,56,1536]{2,1,0:T(8,128)(2,1)} %broadcast_in_dim.31), calls=%async_computation.1 | async-start | bytes 5505024 | tf_op jit(solution)/shard_map/all_to_all | solution.py:70
  50.7 0.1 select_reduce_fusion
  50.8 0.1 stack.35.flags
  51.0 0.2 fusion.4
  51.1 5.6 %collective-permute-start.8 = (bf16[384,384]{1,0:T(8,128)(2,1)}, bf16[384,384]{1,0:T(8,128)(2,1)S(1)}, u32[]{:S(2)}, u32[]{:S(2)}) collective-permute-start(bf16[384,384]{1,0:T(8,128)(2,1)} %pad_maximum_fusion.p0), channel_id=1, source_target_pairs={{0,3},{1,0},{2,1},{3,2},{4,7},{5,4},{6,5},{7,6},{8,11},{9,8},{10,9... | collective-permute-start | bytes 884744 | tf_op jit(solution)/shard_map/ppermute | solution.py:298
  56.8 4.6 %collective-permute-start.7 = (bf16[384,384]{1,0:T(8,128)(2,1)}, bf16[384,384]{1,0:T(8,128)(2,1)S(1)}, u32[]{:S(2)}, u32[]{:S(2)}) collective-permute-start(bf16[384,384]{1,0:T(8,128)(2,1)} %pad_maximum_fusion.p0), channel_id=1, source_target_pairs={{0,2},{1,3},{2,0},{3,1},{4,6},{5,7},{6,4},{7,5},{8,10},{9,11},{10,... | collective-permute-start | bytes 884744 | tf_op jit(solution)/shard_map/ppermute | solution.py:298
  61.3 2.6 %collective-permute-start.6 = (bf16[384,384]{1,0:T(8,128)(2,1)}, bf16[384,384]{1,0:T(8,128)(2,1)S(1)}, u32[]{:S(2)}, u32[]{:S(2)}) collective-permute-start(bf16[384,384]{1,0:T(8,128)(2,1)} %pad_maximum_fusion.p0), channel_id=1, source_target_pairs={{0,1},{1,2},{2,3},{3,0},{4,5},{5,6},{6,7},{7,4},{8,9},{9,10},{10,1... | collective-permute-start | bytes 884744 | tf_op jit(solution)/shard_map/ppermute | solution.py:298
  63.9 0.1 fusion.lines
  64.1 1.1 copy-done.16
  65.1 1.1 copy-done.17
  66.2 1.1 copy-done.18
  67.2 1.4 shard_map.122
  68.6 1.0 copy-done.8
  69.6 1.1 copy-done.10
  70.7 0.0 collective-permute-done.8.p3
  70.7 12.2 %collective-permute-done.7.p2 = bf16[384,384]{1,0:T(8,128)(2,1)S(1)} collective-permute-done((bf16[384,384]{1,0:T(8,128)(2,1)}, bf16[384,384]{1,0:T(8,128)(2,1)S(1)}, u32[]{:S(2)}, u32[]{:S(2)}) %collective-permute-start.7) | collective-permute-done | bytes 294944 | tf_op jit(solution)/shard_map/ppermute | solution.py:298
  82.9 1.9 %shard_map.123 = (bf16[4,384,224]{2,1,0:T(8,128)(2,1)S(1)}, bf16[4,384,224]{2,1,0:T(8,128)(2,1)S(1)}) custom-call(bf16[384,384]{1,0:T(8,128)(2,1)} %pad_maximum_fusion.p0, bf16[384,384]{1,0:T(8,128)(2,1)S(1)} %collective-permute-done.6.p1, bf16[384,384]{1,0:T(8,128)(2,1)S(1)} %collective-permute-done.7.p2, bf16[384,384]{1,0:T(8,128)(2,1)S(1)} %collective-permute-done.8.p3, ...), custom_call_target="tpu_custom_call" | custom-call | flops 1000000000 | bytes 8000000 | tf_op jit(solution)/shard_map/pallas_call | solution.py:352
  84.9 0.9 copy-done.12
  85.7 0.9 copy-done.14
  86.6 5.7 %collective-permute-start.9 = (bf16[896,1536]{1,0:T(8,128)(2,1)S(1)}, bf16[896,1536]{1,0:T(8,128)(2,1)S(1)}, u32[]{:S(2)}, u32[]{:S(2)}) collective-permute-start(bf16[896,1536]{1,0:T(8,128)(2,1)S(1)} %bitcast.15), channel_id=1, source_target_pairs={{0,4},{4,0},{8,12},{12,8},{16,20},{20,16},{24,28},{28,24},{32,36},... | collective-permute-start | bytes 8257544 | tf_op jit(solution)/shard_map/ppermute | solution.py:42
  92.4 1.3 copy-done.11
  93.7 1.1 copy-done.15
  94.8 3.3 %shard_map.124 = (f32[192,1152]{1,0:T(8,128)S(1)}, f32[192,384]{1,0:T(8,128)S(1)}, f32[192,768]{1,0:T(8,128)S(1)}, f32[384,768]{1,0:T(8,128)S(1)}, f32[128,768]{...) custom-call(s32[6]{0:T(128)S(1)} %stack.35.flags, bf16[4,576,224]{2,1,0:T(8,128)(2,1)S(1)} %copy-done.11, ...), custom_call_target="tpu_custom_call" | custom-call | flops 1000000000 | bytes 8000000 | tf_op jit(solution)/shard_map/pallas_call | solution.py:360
  98.1 9.0 %shard_map.125 = (bf16[192,384]{1,0:T(8,128)(2,1)S(1)}, bf16[768,768]{1,0:T(8,128)(2,1)S(1)}, bf16[384,768]{1,0:T(8,128)(2,1)}, bf16[384,768]{1,0:T(8,128)(2,1)}) custom-call(s32[6]{0:T(128)S(1)} %stack.35.flags, bf16[4,576,224]{2,1,0:T(8,128)(2,1)S(1)} %copy-done.9, bf16[4,384,224]{2,1,0:T(8,128)(2,1)S(1)} %copy-done.13, ...), custom_call_target="tpu_custom_call" | custom-call | flops 1000000000 | bytes 8000000 | tf_op jit(solution)/shard_map/pallas_call | solution.py:372
  107.1 1.0 copy-done.5
  108.1 3.1 %collective-permute-start.10 = (bf16[384,768]{1,0:T(8,128)(2,1)}, bf16[384,768]{1,0:T(8,128)(2,1)}, u32[]{:S(2)}, u32[]{:S(2)}) collective-permute-start(bf16[384,768]{1,0:T(8,128)(2,1)} %get-tuple-element.61), channel_id=1, source_target_pairs={{0,128},{4,132},{8,136},{12,140},{16,144},{20,148},{24,152},{28,15... | collective-permute-start | bytes 1769480 | tf_op jit(solution)/shard_map/ppermute | solution.py:42
  111.2 1.5 collective-permute-start.11
  112.7 1.5 shard_map.126
  114.2 0.8 copy-done.3
  115.0 4.2 %all-to-all-start.2 = ((bf16[4,192,384]{2,1,0:T(8,128)(2,1)}), bf16[4,192,384]{2,1,0:T(8,128)(2,1)}, u32[]{:S(2)}, u32[]{:S(2)}) async-start(bf16[4,192,384]{2,1,0:T(8,128)(2,1)} %copy-done.3), calls=%async_computation.2 | async-start | bytes 1179648 | tf_op jit(solution)/shard_map/all_to_all | solution.py:387
  119.2 6.1 %collective-permute-done.10.got_even = bf16[384,768]{1,0:T(8,128)(2,1)} collective-permute-done((bf16[384,768]{1,0:T(8,128)(2,1)}, bf16[384,768]{1,0:T(8,128)(2,1)}, u32[]{:S(2)}, u32[]{:S(2)}) %collective-permute-start.10) | collective-permute-done | bytes 589856 | tf_op jit(solution)/shard_map/ppermute | solution.py:42
  125.3 1.3 copy-done.6
  126.5 1.7 shard_map.127
  128.2 7.2 %collective-permute-start.12 = (bf16[192,768]{1,0:T(8,128)(2,1)S(1)}, bf16[192,768]{1,0:T(8,128)(2,1)S(1)}, u32[]{:S(2)}, u32[]{:S(2)}) collective-permute-start(bf16[192,768]{1,0:T(8,128)(2,1)S(1)} %get-tuple-element.64), channel_id=1, source_target_pairs={{4,8},{8,4},{12,16},{16,12},{20,24},{24,20},{28,32},{32,28},{36,40... | collective-permute-start | bytes 884744 | tf_op jit(solution)/shard_map/ppermute | solution.py:42
  135.4 1.9 %collective-permute-start.13 = (bf16[192,768]{1,0:T(8,128)(2,1)S(1)}, bf16[192,768]{1,0:T(8,128)(2,1)S(1)}, u32[]{:S(2)}, u32[]{:S(2)}) collective-permute-start(bf16[192,768]{1,0:T(8,128)(2,1)S(1)} %get-tuple-element.65), channel_id=1, source_target_pairs={{0,4},{4,0},{8,12},{12,8},{16,20},{20,16},{24,28},{28,24},{32,36},... | collective-permute-start | bytes 884744 | tf_op jit(solution)/shard_map/ppermute | solution.py:42
  137.3 14.3 %collective-permute-done.12.from_next = bf16[192,768]{1,0:T(8,128)(2,1)S(1)} collective-permute-done((bf16[192,768]{1,0:T(8,128)(2,1)S(1)}, bf16[192,768]{1,0:T(8,128)(2,1)S(1)}, u32[]{:S(2)}, u32[]{:S(2)}) %collective-permute-start.12) | collective-permute-done | bytes 294944 | tf_op jit(solution)/shard_map/ppermute | solution.py:42
  151.7 2.3 %shard_map.128 = bf16[4,192,384]{2,1,0:T(8,128)(2,1)S(1)} custom-call(f32[192,768]{1,0:T(8,128)S(1)} %get-tuple-element.63.own, bf16[192,768]{1,0:T(8,128)(2,1)S(1)} %collective-permute-done.12.from_next, bf16[192,768]{1,0:T(8,128)(2,1)S(1)} %collective-permute-done.13.from_mate, bf16[768,768]{1,0:T(8,128)(2,1)S(1)} %copy-done.7, ...), custom_call_target="tpu_custom_call" | custom-call | flops 1000000000 | bytes 8000000 | tf_op jit(solution)/shard_map/pallas_call | solution.py:397
  154.0 0.8 copy-done.4
  154.8 3.5 %all-to-all-start.3 = ((bf16[4,192,384]{2,1,0:T(8,128)(2,1)}), bf16[4,192,384]{2,1,0:T(8,128)(2,1)S(1)}, u32[]{:S(2)}, u32[]{:S(2)}) async-start(bf16[4,192,384]{2,1,0:T(8,128)(2,1)} %copy-done.4), calls=%async_computation.3 | async-start | bytes 1179648 | tf_op jit(solution)/shard_map/all_to_all | solution.py:400
  158.3 1.9 %fusion.5 = bf16[192,384]{1,0:T(8,128)(2,1)} fusion(bf16[4,192,384]{2,1,0:T(8,128)(2,1)} %all-to-all-done.2), kind=kLoop, calls=%fused_computation.15 | loop fusion | flops 589824 | bytes 737280 | tf_op jit(solution)/shard_map/add | solution.py:293
  160.2 7.9 %all-to-all-done.3 = bf16[4,192,384]{2,1,0:T(8,128)(2,1)S(1)} async-done(((bf16[4,192,384]{2,1,0:T(8,128)(2,1)}), bf16[4,192,384]{2,1,0:T(8,128)(2,1)S(1)}, u32[]{:S(2)}, u32[]{:S(2)}) %all-to-all-start.3) | async-done | bytes 589856 | tf_op jit(solution)/shard_map/all_to_all | solution.py:400
  168.1 0.7 fusion.6
  (51 shorter events, 0.3 us)
Async XLA Ops:
  0.6 27.3 %copy-start = (s32[128,2]{0,1:T(2,128)S(1)}, s32[128,2]{0,1:T(2,128)}, u32[]{:S(2)}) copy-start(s32[128,2]{0,1:T(2,128)} %param.20) | copy-start | bytes 3076
  1.6 28.2 %collective-permute-start.1 = (bf16[192,384]{1,0:T(8,128)(2,1)S(1)}, bf16[192,384]{1,0:T(8,128)(2,1)S(1)}, u32[]{:S(2)}, u32[]{:S(2)}) collective-permute-start(bf16[192,384]{1,0:T(8,128)(2,1)S(1)} %constant_dynamic-slice_fusion), channel_id=1, source_target_pairs={{4,8},{8,4},{12,16},{16,12},{20,24},{24,20},{28,32},{32,28},{36,40... | collective-permute-start | bytes 442376 | tf_op jit(solution)/shard_map/ppermute | solution.py:42
  10.6 19.2 %collective-permute-start = (bf16[192,384]{1,0:T(8,128)(2,1)S(1)}, bf16[192,384]{1,0:T(8,128)(2,1)S(1)}, u32[]{:S(2)}, u32[]{:S(2)}) collective-permute-start(bf16[192,384]{1,0:T(8,128)(2,1)S(1)} %constant_dynamic-slice_fusion), channel_id=1, source_target_pairs={{0,4},{4,0},{8,12},{12,8},{16,20},{20,16},{24,28},{28,24},{32,36},... | collective-permute-start | bytes 442376 | tf_op jit(solution)/shard_map/ppermute | solution.py:42
  12.6 17.3 %collective-permute-start.2 = (bf16[192,1536]{1,0:T(8,128)(2,1)}, bf16[192,1536]{1,0:T(8,128)(2,1)S(1)}, u32[]{:S(2)}, u32[]{:S(2)}) collective-permute-start(bf16[192,1536]{1,0:T(8,128)(2,1)} %x.3), channel_id=1, source_target_pairs={{0,128},{4,132},{8,136},{12,140},{16,144},{20,148},{24,152},{28,15... | collective-permute-start | bytes 1769480 | tf_op jit(solution)/shard_map/ppermute | solution.py:42
  15.7 14.2 %collective-permute-start.3 = (bf16[192,1536]{1,0:T(8,128)(2,1)}, bf16[192,1536]{1,0:T(8,128)(2,1)S(1)}, u32[]{:S(2)}, u32[]{:S(2)}) collective-permute-start(bf16[192,1536]{1,0:T(8,128)(2,1)} %x.3), channel_id=1, source_target_pairs={{128,256},{132,260},{136,264},{140,268},{144,272},{148,276},{152,2... | collective-permute-start | bytes 1769480 | tf_op jit(solution)/shard_map/ppermute | solution.py:42
  17.9 22.7 %all-to-all-start = ((bf16[4,14,1536]{2,1,0:T(8,128)(2,1)}), bf16[4,14,1536]{2,1,0:T(8,128)(2,1)S(1)}, u32[]{:S(2)}, u32[]{:S(2)}) async-start(bf16[4,14,1536]{2,1,0:T(8,128)(2,1)} %broadcast_in_dim.30), calls=%async_computation | async-start | bytes 393216 | tf_op jit(solution)/shard_map/all_to_all | solution.py:70
  30.8 9.8 %collective-permute-start.5 = (bf16[192,384]{1,0:T(8,128)(2,1)S(1)}, bf16[192,384]{1,0:T(8,128)(2,1)S(1)}, u32[]{:S(2)}, u32[]{:S(2)}) collective-permute-start(bf16[192,384]{1,0:T(8,128)(2,1)S(1)} %broadcast_select_fusion.2), channel_id=1, source_target_pairs={{128,256},{132,260},{136,264},{140,268},{144,272},{148,276},{152,2... | collective-permute-start | bytes 442376 | tf_op jit(solution)/shard_map/ppermute | solution.py:42
  31.4 10.1 %collective-permute-start.4 = (bf16[192,384]{1,0:T(8,128)(2,1)S(1)}, bf16[192,384]{1,0:T(8,128)(2,1)S(1)}, u32[]{:S(2)}, u32[]{:S(2)}) collective-permute-start(bf16[192,384]{1,0:T(8,128)(2,1)S(1)} %broadcast_select_fusion.2), channel_id=1, source_target_pairs={{0,128},{4,132},{8,136},{12,140},{16,144},{20,148},{24,152},{28,15... | collective-permute-start | bytes 442376 | tf_op jit(solution)/shard_map/ppermute | solution.py:42
  44.1 6.6 %copy-start.21 = (s32[256]{0:T(256)S(1)}, s32[256]{0:T(256)}, u32[]{:S(2)}) copy-start(s32[256]{0:T(256)} %param.19) | copy-start | bytes 3076
  44.1 42.5 %all-to-all-start.1 = ((bf16[16,56,1536]{2,1,0:T(8,128)(2,1)}), bf16[16,56,1536]{2,1,0:T(8,128)(2,1)S(1)}, u32[]{:S(2)}, u32[]{:S(2)}) async-start(bf16[16,56,1536]{2,1,0:T(8,128)(2,1)} %broadcast_in_dim.31), calls=%async_computation.1 | async-start | bytes 5505024 | tf_op jit(solution)/shard_map/all_to_all | solution.py:70
  51.1 19.6 %collective-permute-start.8 = (bf16[384,384]{1,0:T(8,128)(2,1)}, bf16[384,384]{1,0:T(8,128)(2,1)S(1)}, u32[]{:S(2)}, u32[]{:S(2)}) collective-permute-start(bf16[384,384]{1,0:T(8,128)(2,1)} %pad_maximum_fusion.p0), channel_id=1, source_target_pairs={{0,3},{1,0},{2,1},{3,2},{4,7},{5,4},{6,5},{7,6},{8,11},{9,8},{10,9... | collective-permute-start | bytes 884744 | tf_op jit(solution)/shard_map/ppermute | solution.py:298
  56.8 26.1 %collective-permute-start.7 = (bf16[384,384]{1,0:T(8,128)(2,1)}, bf16[384,384]{1,0:T(8,128)(2,1)S(1)}, u32[]{:S(2)}, u32[]{:S(2)}) collective-permute-start(bf16[384,384]{1,0:T(8,128)(2,1)} %pad_maximum_fusion.p0), channel_id=1, source_target_pairs={{0,2},{1,3},{2,0},{3,1},{4,6},{5,7},{6,4},{7,5},{8,10},{9,11},{10,... | collective-permute-start | bytes 884744 | tf_op jit(solution)/shard_map/ppermute | solution.py:298
  61.3 21.6 %collective-permute-start.6 = (bf16[384,384]{1,0:T(8,128)(2,1)}, bf16[384,384]{1,0:T(8,128)(2,1)S(1)}, u32[]{:S(2)}, u32[]{:S(2)}) collective-permute-start(bf16[384,384]{1,0:T(8,128)(2,1)} %pad_maximum_fusion.p0), channel_id=1, source_target_pairs={{0,1},{1,2},{2,3},{3,0},{4,5},{5,6},{6,7},{7,4},{8,9},{9,10},{10,1... | collective-permute-start | bytes 884744 | tf_op jit(solution)/shard_map/ppermute | solution.py:298
  64.0 1.1 copy-start.16
  65.1 1.1 copy-start.17
  66.2 1.1 copy-start.18
  68.6 1.0 copy-start.8
  69.6 1.1 copy-start.10
  70.7 21.7 %copy-start.19 = (f32[384]{0:T(512)S(1)}, f32[384]{0:T(512)}, u32[]{:S(2)}) copy-start(f32[384]{0:T(512)} %param.18) | copy-start | bytes 4612
  70.7 21.7 %copy-start.20 = (f32[384]{0:T(512)S(1)}, f32[384]{0:T(512)}, u32[]{:S(2)}) copy-start(f32[384]{0:T(512)} %param.17) | copy-start | bytes 4612
  84.8 0.9 copy-start.12
  85.7 0.9 copy-start.14
  86.6 11.5 %collective-permute-start.9 = (bf16[896,1536]{1,0:T(8,128)(2,1)S(1)}, bf16[896,1536]{1,0:T(8,128)(2,1)S(1)}, u32[]{:S(2)}, u32[]{:S(2)}) collective-permute-start(bf16[896,1536]{1,0:T(8,128)(2,1)S(1)} %bitcast.15), channel_id=1, source_target_pairs={{0,4},{4,0},{8,12},{12,8},{16,20},{20,16},{24,28},{28,24},{32,36},... | collective-permute-start | bytes 8257544 | tf_op jit(solution)/shard_map/ppermute | solution.py:42
  92.4 1.3 copy-start.11
  93.7 1.1 copy-start.15
  94.8 3.3 %copy-start.9 = (bf16[4,576,224]{2,1,0:T(8,128)(2,1)S(1)}, bf16[4,576,224]{2,1,0:T(8,128)(2,1)}, u32[]{:S(2)}) copy-start(bf16[4,576,224]{2,1,0:T(8,128)(2,1)} %copy-done.8) | copy-start | bytes 3096580
  94.8 3.3 %copy-start.13 = (bf16[4,384,224]{2,1,0:T(8,128)(2,1)S(1)}, bf16[4,384,224]{2,1,0:T(8,128)(2,1)}, u32[]{:S(2)}) copy-start(bf16[4,384,224]{2,1,0:T(8,128)(2,1)} %copy-done.12) | copy-start | bytes 2064388
  98.1 14.6 %copy-start.1 = (bf16[896,1536]{1,0:T(8,128)(2,1)}, bf16[896,1536]{1,0:T(8,128)(2,1)S(1)}, u32[]{:S(2)}) copy-start(bf16[896,1536]{1,0:T(8,128)(2,1)S(1)} %collective-permute-done.9.wt) | copy-start | bytes 8257540
  107.1 1.0 copy-start.5
  108.1 17.2 %collective-permute-start.10 = (bf16[384,768]{1,0:T(8,128)(2,1)}, bf16[384,768]{1,0:T(8,128)(2,1)}, u32[]{:S(2)}, u32[]{:S(2)}) collective-permute-start(bf16[384,768]{1,0:T(8,128)(2,1)} %get-tuple-element.61), channel_id=1, source_target_pairs={{0,128},{4,132},{8,136},{12,140},{16,144},{20,148},{24,152},{28,15... | collective-permute-start | bytes 1769480 | tf_op jit(solution)/shard_map/ppermute | solution.py:42
  111.2 14.1 %collective-permute-start.11 = (bf16[384,768]{1,0:T(8,128)(2,1)}, bf16[384,768]{1,0:T(8,128)(2,1)}, u32[]{:S(2)}, u32[]{:S(2)}) collective-permute-start(bf16[384,768]{1,0:T(8,128)(2,1)} %get-tuple-element.62), channel_id=1, source_target_pairs={{128,256},{132,260},{136,264},{140,268},{144,272},{148,276},{152,2... | collective-permute-start | bytes 1769480 | tf_op jit(solution)/shard_map/ppermute | solution.py:42
  114.2 0.8 copy-start.3
  115.0 39.8 %all-to-all-start.2 = ((bf16[4,192,384]{2,1,0:T(8,128)(2,1)}), bf16[4,192,384]{2,1,0:T(8,128)(2,1)}, u32[]{:S(2)}, u32[]{:S(2)}) async-start(bf16[4,192,384]{2,1,0:T(8,128)(2,1)} %copy-done.3), calls=%async_computation.2 | async-start | bytes 1179648 | tf_op jit(solution)/shard_map/all_to_all | solution.py:387
  125.3 1.3 copy-start.6
  126.5 25.1 %copy-start.2 = (bf16[896,1536]{1,0:T(8,128)(2,1)S(1)}, bf16[896,1536]{1,0:T(8,128)(2,1)}, u32[]{:S(2)}) copy-start(bf16[896,1536]{1,0:T(8,128)(2,1)} %copy-done.1) | copy-start | bytes 8257540
  126.5 25.1 %copy-start.7 = (bf16[768,768]{1,0:T(8,128)(2,1)S(1)}, bf16[768,768]{1,0:T(8,128)(2,1)}, u32[]{:S(2)}) copy-start(bf16[768,768]{1,0:T(8,128)(2,1)} %copy-done.5) | copy-start | bytes 3538948
  128.2 23.5 %collective-permute-start.12 = (bf16[192,768]{1,0:T(8,128)(2,1)S(1)}, bf16[192,768]{1,0:T(8,128)(2,1)S(1)}, u32[]{:S(2)}, u32[]{:S(2)}) collective-permute-start(bf16[192,768]{1,0:T(8,128)(2,1)S(1)} %get-tuple-element.64), channel_id=1, source_target_pairs={{4,8},{8,4},{12,16},{16,12},{20,24},{24,20},{28,32},{32,28},{36,40... | collective-permute-start | bytes 884744 | tf_op jit(solution)/shard_map/ppermute | solution.py:42
  135.4 16.3 %collective-permute-start.13 = (bf16[192,768]{1,0:T(8,128)(2,1)S(1)}, bf16[192,768]{1,0:T(8,128)(2,1)S(1)}, u32[]{:S(2)}, u32[]{:S(2)}) collective-permute-start(bf16[192,768]{1,0:T(8,128)(2,1)S(1)} %get-tuple-element.65), channel_id=1, source_target_pairs={{0,4},{4,0},{8,12},{12,8},{16,20},{20,16},{24,28},{28,24},{32,36},... | collective-permute-start | bytes 884744 | tf_op jit(solution)/shard_map/ppermute | solution.py:42
  154.0 0.8 copy-start.4
  154.8 13.3 %all-to-all-start.3 = ((bf16[4,192,384]{2,1,0:T(8,128)(2,1)}), bf16[4,192,384]{2,1,0:T(8,128)(2,1)S(1)}, u32[]{:S(2)}, u32[]{:S(2)}) async-start(bf16[4,192,384]{2,1,0:T(8,128)(2,1)} %copy-done.4), calls=%async_computation.3 | async-start | bytes 1179648 | tf_op jit(solution)/shard_map/all_to_all | solution.py:400

commit v7 on v6

--- a/solution.py
+++ b/solution.py
@@ -305,12 +305,12 @@
     me = lax.axis_index("heads")
     core, x, col = place & 1, place >> 5, place & 31
     window = lax.dynamic_slice(windows, (place, jnp.int32(0)), (1, 2))
-    use_even = (window[0, 0] == x) == ((x & 1) == 0)
-    use_core = (window[0, 1] == col) == (core == 0)
+    use_even = (window[:, :1] == x) == ((x & 1) == 0)
+    use_core = (window[:, 1:] == col) == (core == 0)
     q_gain = q_gain[None, :]
     k_gain = k_gain[None, :]
     blocks = [(me - by) & 3 for by in range(4)]
-    flags = jnp.stack([use_even.astype(jnp.int32), use_core.astype(jnp.int32)] + blocks)
+    flags = jnp.stack([use_even[0, 0].astype(jnp.int32), use_core[0, 0].astype(jnp.int32)] + blocks)
 
     at = jnp.arange(PART, dtype=jnp.int32)
     inner = at % BLOCK
@@ -343,7 +343,6 @@
     corner = jnp.where(use_even, c_even, c_odd)
     beside = jnp.concatenate([side, corner])
     block = jnp.concatenate([four[:, :12].reshape(48, 1536), four[:, 12:].reshape(8, 1536)], axis=0)
-    block, beside = lax.optimization_barrier((block, beside))
     parts = [beside] + [head_shift(beside, by) for by in (1, 2, 3)]
     wo = over_xy(block).reshape(16 * BLOCK, 1536)
     r_o, r_t = call(pick_kernel, (shape((4, 3 * ROWS, PART), BF16),) * 2, "v" * 5)(

time: 172 us -> 172 us (level)
    unnamed x44 -> x46, local copies, waits for them, and re-layouts: 13.4 us -> 14.1 us
  transfers between devices with their start and end apart: 18 -> 18, of which waited for: 6 -> 6; matrix products, arithmetic and copies ran while one was open for 3% -> 4% of each run, Pallas kernels for 7% -> 7%
where the time goes in v7:
time: 172 us; the launch traced here: 169 us
  starting transfers between devices  79.3 us (46%)
  waiting for transfers between devices  43 us (25%)
  Pallas kernels  19.9 us (12%)
  local copies, waits for them, and re-layouts  18.2 us (11%)
  other arithmetic  5.75 us (3%)
  between operations  2.36 us (1%)
    ppermute x11, starting transfers between devices, seq_move(): return lax.ppermute(value, 'seq', pairs)  42.3 us
    ppermute x11, waiting for transfers between devices, seq_move(): return lax.ppermute(value, 'seq', pairs)  21.2 us
    all_to_all x2, starting transfers between devices, give_all(): return lax.all_to_all(copies, 'seq', 0, 0, axis_index_groups=groups)  16.5 us
    unnamed x46, local copies, waits for them, and re-layouts  14.1 us
    ppermute x3, starting transfers between devices, head_shift(): return lax.ppermute(value, 'heads', [(i, (i + by) % 4) for i in range(4)])  12.8 us
    ppermute x3, waiting for transfers between devices, head_shift(): return lax.ppermute(value, 'heads', [(i, (i + by) % 4) for i in range(4)])  12 us
    pallas_call x1, Pallas kernels, per_device(): call(attend_kernel, (shape((ROWS, W), BF16), shape((4 * ROWS, 2 * W), BF1...  8.86 us
    all_to_all x1, waiting for transfers between devices, per_device(): grads = lax.all_to_all(grad, 'heads', 0, 0)  7.94 us
  transfers between devices with their start and end apart: 18, of which 6 were waited for; matrix products, arithmetic and copies ran while one was open for 4% of the time, Pallas kernels for 7%

profile of v7, /device:TPU:25, one launch (start us, length us, event | category | flops | bytes accessed | tf_op | source)
XLA Modules:
  0.0 168.5 jit_solution(14265272113744316614)
XLA Ops:
  0.6 0.0 copy-start
  0.7 0.9 constant_dynamic-slice_fusion
  1.6 9.0 %collective-permute-start.1 = (bf16[192,384]{1,0:T(8,128)(2,1)S(1)}, bf16[192,384]{1,0:T(8,128)(2,1)S(1)}, u32[]{:S(2)}, u32[]{:S(2)}) collective-permute-start(bf16[192,384]{1,0:T(8,128)(2,1)S(1)} %constant_dynamic-slice_fusion), channel_id=1, source_target_pairs={{4,8},{8,4},{12,16},{16,12},{20,24},{24,20},{28,32},{32,28},{36,40... | collective-permute-start | bytes 442376 | tf_op jit(solution)/shard_map/ppermute | solution.py:42
  10.6 1.9 %collective-permute-start = (bf16[192,384]{1,0:T(8,128)(2,1)S(1)}, bf16[192,384]{1,0:T(8,128)(2,1)S(1)}, u32[]{:S(2)}, u32[]{:S(2)}) collective-permute-start(bf16[192,384]{1,0:T(8,128)(2,1)S(1)} %constant_dynamic-slice_fusion), channel_id=1, source_target_pairs={{0,4},{4,0},{8,12},{12,8},{16,20},{20,16},{24,28},{28,24},{32,36},... | collective-permute-start | bytes 442376 | tf_op jit(solution)/shard_map/ppermute | solution.py:42
  12.6 3.1 %collective-permute-start.2 = (bf16[192,1536]{1,0:T(8,128)(2,1)}, bf16[192,1536]{1,0:T(8,128)(2,1)S(1)}, u32[]{:S(2)}, u32[]{:S(2)}) collective-permute-start(bf16[192,1536]{1,0:T(8,128)(2,1)} %x.3), channel_id=1, source_target_pairs={{0,128},{4,132},{8,136},{12,140},{16,144},{20,148},{24,152},{28,15... | collective-permute-start | bytes 1769480 | tf_op jit(solution)/shard_map/ppermute | solution.py:42
  15.7 0.7 collective-permute-start.3
  16.4 0.8 pad_maximum_fusion.2
  17.2 0.7 broadcast_in_dim.76
  17.9 10.0 %all-to-all-start = ((bf16[4,14,1536]{2,1,0:T(8,128)(2,1)}), bf16[4,14,1536]{2,1,0:T(8,128)(2,1)S(1)}, u32[]{:S(2)}, u32[]{:S(2)}) async-start(bf16[4,14,1536]{2,1,0:T(8,128)(2,1)} %broadcast_in_dim.76), calls=%async_computation | async-start | bytes 393216 | tf_op jit(solution)/shard_map/all_to_all | solution.py:70
  27.9 0.1 constant_dynamic-slice_fusion.1
  28.0 0.5 fusion.29
  29.8 0.0 collective-permute-done
  29.9 0.0 collective-permute-done.3
  29.9 0.9 broadcast_select_fusion.f
  30.8 0.7 collective-permute-start.5
  31.4 7.3 %collective-permute-start.4 = (bf16[192,384]{1,0:T(8,128)(2,1)S(1)}, bf16[192,384]{1,0:T(8,128)(2,1)S(1)}, u32[]{:S(2)}, u32[]{:S(2)}) collective-permute-start(bf16[192,384]{1,0:T(8,128)(2,1)S(1)} %broadcast_select_fusion.2), channel_id=1, source_target_pairs={{0,128},{4,132},{8,136},{12,140},{16,144},{20,148},{24,152},{28,15... | collective-permute-start | bytes 442376 | tf_op jit(solution)/shard_map/ppermute | solution.py:42
  38.7 1.9 %all-to-all-done = bf16[4,14,1536]{2,1,0:T(8,128)(2,1)S(1)} async-done(((bf16[4,14,1536]{2,1,0:T(8,128)(2,1)}), bf16[4,14,1536]{2,1,0:T(8,128)(2,1)S(1)}, u32[]{:S(2)}, u32[]{:S(2)}) %all-to-all-start) | async-done | bytes 172064 | tf_op jit(solution)/shard_map/all_to_all | solution.py:70
  40.6 0.9 collective-permute-done.4
  41.6 0.6 copy-done.19
  42.3 1.7 %broadcast_in_dim.81 = bf16[16,56,1536]{2,1,0:T(8,128)(2,1)} broadcast(bf16[56,1536]{1,0:T(8,128)(2,1)S(1)} %pad_maximum_fusion.1), dimensions={1,2} | broadcast | bytes 2924544 | tf_op jit(solution)/shard_map/broadcast_in_dim | solution.py:69
  43.9 6.5 %all-to-all-start.1 = ((bf16[16,56,1536]{2,1,0:T(8,128)(2,1)}), bf16[16,56,1536]{2,1,0:T(8,128)(2,1)S(1)}, u32[]{:S(2)}, u32[]{:S(2)}) async-start(bf16[16,56,1536]{2,1,0:T(8,128)(2,1)} %broadcast_in_dim.81), calls=%async_computation.1 | async-start | bytes 5505024 | tf_op jit(solution)/shard_map/all_to_all | solution.py:70
  50.5 0.1 select_reduce_fusion
  50.6 0.1 stack.35.flags
  50.8 0.2 fusion.4
  51.0 0.9 broadcast_select_fusion.1
  51.9 5.6 %collective-permute-start.8 = (bf16[384,384]{1,0:T(8,128)(2,1)S(1)}, bf16[384,384]{1,0:T(8,128)(2,1)S(1)}, u32[]{:S(2)}, u32[]{:S(2)}) collective-permute-start(bf16[384,384]{1,0:T(8,128)(2,1)S(1)} %pad_maximum_fusion.p0), channel_id=1, source_target_pairs={{0,3},{1,0},{2,1},{3,2},{4,7},{5,4},{6,5},{7,6},{8,11},{9,8},{10,9... | collective-permute-start | bytes 884744 | tf_op jit(solution)/shard_map/ppermute | solution.py:298
  57.6 4.6 %collective-permute-start.7 = (bf16[384,384]{1,0:T(8,128)(2,1)S(1)}, bf16[384,384]{1,0:T(8,128)(2,1)S(1)}, u32[]{:S(2)}, u32[]{:S(2)}) collective-permute-start(bf16[384,384]{1,0:T(8,128)(2,1)S(1)} %pad_maximum_fusion.p0), channel_id=1, source_target_pairs={{0,2},{1,3},{2,0},{3,1},{4,6},{5,7},{6,4},{7,5},{8,10},{9,11},{10,... | collective-permute-start | bytes 884744 | tf_op jit(solution)/shard_map/ppermute | solution.py:298
  62.2 2.6 %collective-permute-start.6 = (bf16[384,384]{1,0:T(8,128)(2,1)S(1)}, bf16[384,384]{1,0:T(8,128)(2,1)S(1)}, u32[]{:S(2)}, u32[]{:S(2)}) collective-permute-start(bf16[384,384]{1,0:T(8,128)(2,1)S(1)} %pad_maximum_fusion.p0), channel_id=1, source_target_pairs={{0,1},{1,2},{2,3},{3,0},{4,5},{5,6},{6,7},{7,4},{8,9},{9,10},{10,1... | collective-permute-start | bytes 884744 | tf_op jit(solution)/shard_map/ppermute | solution.py:298
  64.8 0.1 fusion.lines
  64.9 1.1 copy-done.16
  65.9 1.1 copy-done.17
  67.0 1.1 copy-done.18
  68.1 1.4 shard_map.122
  69.5 1.0 copy-done.8
  70.5 1.1 copy-done.10
  71.5 12.0 %collective-permute-done.7.p2 = bf16[384,384]{1,0:T(8,128)(2,1)S(1)} collective-permute-done((bf16[384,384]{1,0:T(8,128)(2,1)S(1)}, bf16[384,384]{1,0:T(8,128)(2,1)S(1)}, u32[]{:S(2)}, u32[]{:S(2)}) %collective-permute-start.7) | collective-permute-done | bytes 294944 | tf_op jit(solution)/shard_map/ppermute | solution.py:298
  83.5 0.0 collective-permute-done.6.p1
  83.5 1.0 shard_map.123
  84.5 0.9 copy-done.12
  85.4 0.9 copy-done.14
  86.3 0.0 all-to-all-done.1
  86.3 5.7 %collective-permute-start.9 = (bf16[896,1536]{1,0:T(8,128)(2,1)S(1)}, bf16[896,1536]{1,0:T(8,128)(2,1)S(1)}, u32[]{:S(2)}, u32[]{:S(2)}) collective-permute-start(bf16[896,1536]{1,0:T(8,128)(2,1)S(1)} %bitcast.19), channel_id=1, source_target_pairs={{0,4},{4,0},{8,12},{12,8},{16,20},{20,16},{24,28},{28,24},{32,36},... | collective-permute-start | bytes 8257544 | tf_op jit(solution)/shard_map/ppermute | solution.py:42
  92.1 1.3 copy-done.11
  93.3 1.1 copy-done.15
  94.5 3.3 %shard_map.124 = (f32[192,1152]{1,0:T(8,128)S(1)}, f32[192,384]{1,0:T(8,128)S(1)}, f32[192,768]{1,0:T(8,128)S(1)}, f32[384,768]{1,0:T(8,128)S(1)}, f32[128,768]{...) custom-call(s32[6]{0:T(128)S(1)} %stack.35.flags, bf16[4,576,224]{2,1,0:T(8,128)(2,1)S(1)} %copy-done.11, ...), custom_call_target="tpu_custom_call" | custom-call | flops 1000000000 | bytes 8000000 | tf_op jit(solution)/shard_map/pallas_call | solution.py:359
  97.8 8.9 %shard_map.125 = (bf16[192,384]{1,0:T(8,128)(2,1)S(1)}, bf16[768,768]{1,0:T(8,128)(2,1)S(1)}, bf16[384,768]{1,0:T(8,128)(2,1)}, bf16[384,768]{1,0:T(8,128)(2,1)}) custom-call(s32[6]{0:T(128)S(1)} %stack.35.flags, bf16[4,576,224]{2,1,0:T(8,128)(2,1)S(1)} %copy-done.9, bf16[4,384,224]{2,1,0:T(8,128)(2,1)S(1)} %copy-done.13, ...), custom_call_target="tpu_custom_call" | custom-call | flops 1000000000 | bytes 8000000 | tf_op jit(solution)/shard_map/pallas_call | solution.py:371
  106.6 1.0 copy-done.5
  107.7 3.1 %collective-permute-start.10 = (bf16[384,768]{1,0:T(8,128)(2,1)}, bf16[384,768]{1,0:T(8,128)(2,1)}, u32[]{:S(2)}, u32[]{:S(2)}) collective-permute-start(bf16[384,768]{1,0:T(8,128)(2,1)} %get-tuple-element.57), channel_id=1, source_target_pairs={{0,128},{4,132},{8,136},{12,140},{16,144},{20,148},{24,152},{28,15... | collective-permute-start | bytes 1769480 | tf_op jit(solution)/shard_map/ppermute | solution.py:42
  110.7 1.5 collective-permute-start.11
  112.2 1.5 shard_map.126
  113.7 0.8 copy-done.3
  114.6 4.2 %all-to-all-start.2 = ((bf16[4,192,384]{2,1,0:T(8,128)(2,1)}), bf16[4,192,384]{2,1,0:T(8,128)(2,1)}, u32[]{:S(2)}, u32[]{:S(2)}) async-start(bf16[4,192,384]{2,1,0:T(8,128)(2,1)} %copy-done.3), calls=%async_computation.2 | async-start | bytes 1179648 | tf_op jit(solution)/shard_map/all_to_all | solution.py:386
  118.7 6.0 %collective-permute-done.10.got_even = bf16[384,768]{1,0:T(8,128)(2,1)} collective-permute-done((bf16[384,768]{1,0:T(8,128)(2,1)}, bf16[384,768]{1,0:T(8,128)(2,1)}, u32[]{:S(2)}, u32[]{:S(2)}) %collective-permute-start.10) | collective-permute-done | bytes 589856 | tf_op jit(solution)/shard_map/ppermute | solution.py:42
  124.8 1.3 copy-done.6
  126.1 1.7 shard_map.127
  127.7 7.4 %collective-permute-start.12 = (bf16[192,768]{1,0:T(8,128)(2,1)S(1)}, bf16[192,768]{1,0:T(8,128)(2,1)S(1)}, u32[]{:S(2)}, u32[]{:S(2)}) collective-permute-start(bf16[192,768]{1,0:T(8,128)(2,1)S(1)} %get-tuple-element.60), channel_id=1, source_target_pairs={{4,8},{8,4},{12,16},{16,12},{20,24},{24,20},{28,32},{32,28},{36,40... | collective-permute-start | bytes 884744 | tf_op jit(solution)/shard_map/ppermute | solution.py:42
  135.2 1.9 %collective-permute-start.13 = (bf16[192,768]{1,0:T(8,128)(2,1)S(1)}, bf16[192,768]{1,0:T(8,128)(2,1)S(1)}, u32[]{:S(2)}, u32[]{:S(2)}) collective-permute-start(bf16[192,768]{1,0:T(8,128)(2,1)S(1)} %get-tuple-element.61), channel_id=1, source_target_pairs={{0,4},{4,0},{8,12},{12,8},{16,20},{20,16},{24,28},{28,24},{32,36},... | collective-permute-start | bytes 884744 | tf_op jit(solution)/shard_map/ppermute | solution.py:42
  137.1 14.2 %collective-permute-done.12.from_next = bf16[192,768]{1,0:T(8,128)(2,1)S(1)} collective-permute-done((bf16[192,768]{1,0:T(8,128)(2,1)S(1)}, bf16[192,768]{1,0:T(8,128)(2,1)S(1)}, u32[]{:S(2)}, u32[]{:S(2)}) %collective-permute-start.12) | collective-permute-done | bytes 294944 | tf_op jit(solution)/shard_map/ppermute | solution.py:42
  151.3 2.3 %shard_map.128 = bf16[4,192,384]{2,1,0:T(8,128)(2,1)S(1)} custom-call(f32[192,768]{1,0:T(8,128)S(1)} %get-tuple-element.59.own, bf16[192,768]{1,0:T(8,128)(2,1)S(1)} %collective-permute-done.12.from_next, bf16[192,768]{1,0:T(8,128)(2,1)S(1)} %collective-permute-done.13.from_mate, bf16[768,768]{1,0:T(8,128)(2,1)S(1)} %copy-done.7, ...), custom_call_target="tpu_custom_call" | custom-call | flops 1000000000 | bytes 8000000 | tf_op jit(solution)/shard_map/pallas_call | solution.py:396
  153.7 0.8 copy-done.4
  154.5 3.5 %all-to-all-start.3 = ((bf16[4,192,384]{2,1,0:T(8,128)(2,1)}), bf16[4,192,384]{2,1,0:T(8,128)(2,1)S(1)}, u32[]{:S(2)}, u32[]{:S(2)}) async-start(bf16[4,192,384]{2,1,0:T(8,128)(2,1)} %copy-done.4), calls=%async_computation.3 | async-start | bytes 1179648 | tf_op jit(solution)/shard_map/all_to_all | solution.py:399
  158.0 1.9 %fusion.5 = bf16[192,384]{1,0:T(8,128)(2,1)} fusion(bf16[4,192,384]{2,1,0:T(8,128)(2,1)} %all-to-all-done.2), kind=kLoop, calls=%fused_computation.15 | loop fusion | flops 589824 | bytes 737280 | tf_op jit(solution)/shard_map/add | solution.py:293
  159.8 7.9 %all-to-all-done.3 = bf16[4,192,384]{2,1,0:T(8,128)(2,1)S(1)} async-done(((bf16[4,192,384]{2,1,0:T(8,128)(2,1)}), bf16[4,192,384]{2,1,0:T(8,128)(2,1)S(1)}, u32[]{:S(2)}, u32[]{:S(2)}) %all-to-all-start.3) | async-done | bytes 589856 | tf_op jit(solution)/shard_map/all_to_all | solution.py:399
  167.8 0.7 fusion.6
  (53 shorter events, 0.3 us)
Async XLA Ops:
  0.6 27.3 %copy-start = (s32[128,2]{0,1:T(2,128)S(1)}, s32[128,2]{0,1:T(2,128)}, u32[]{:S(2)}) copy-start(s32[128,2]{0,1:T(2,128)} %param.20) | copy-start | bytes 3076
  1.6 28.2 %collective-permute-start.1 = (bf16[192,384]{1,0:T(8,128)(2,1)S(1)}, bf16[192,384]{1,0:T(8,128)(2,1)S(1)}, u32[]{:S(2)}, u32[]{:S(2)}) collective-permute-start(bf16[192,384]{1,0:T(8,128)(2,1)S(1)} %constant_dynamic-slice_fusion), channel_id=1, source_target_pairs={{4,8},{8,4},{12,16},{16,12},{20,24},{24,20},{28,32},{32,28},{36,40... | collective-permute-start | bytes 442376 | tf_op jit(solution)/shard_map/ppermute | solution.py:42
  10.6 19.2 %collective-permute-start = (bf16[192,384]{1,0:T(8,128)(2,1)S(1)}, bf16[192,384]{1,0:T(8,128)(2,1)S(1)}, u32[]{:S(2)}, u32[]{:S(2)}) collective-permute-start(bf16[192,384]{1,0:T(8,128)(2,1)S(1)} %constant_dynamic-slice_fusion), channel_id=1, source_target_pairs={{0,4},{4,0},{8,12},{12,8},{16,20},{20,16},{24,28},{28,24},{32,36},... | collective-permute-start | bytes 442376 | tf_op jit(solution)/shard_map/ppermute | solution.py:42
  12.6 17.3 %collective-permute-start.2 = (bf16[192,1536]{1,0:T(8,128)(2,1)}, bf16[192,1536]{1,0:T(8,128)(2,1)S(1)}, u32[]{:S(2)}, u32[]{:S(2)}) collective-permute-start(bf16[192,1536]{1,0:T(8,128)(2,1)} %x.3), channel_id=1, source_target_pairs={{0,128},{4,132},{8,136},{12,140},{16,144},{20,148},{24,152},{28,15... | collective-permute-start | bytes 1769480 | tf_op jit(solution)/shard_map/ppermute | solution.py:42
  15.7 14.2 %collective-permute-start.3 = (bf16[192,1536]{1,0:T(8,128)(2,1)}, bf16[192,1536]{1,0:T(8,128)(2,1)S(1)}, u32[]{:S(2)}, u32[]{:S(2)}) collective-permute-start(bf16[192,1536]{1,0:T(8,128)(2,1)} %x.3), channel_id=1, source_target_pairs={{128,256},{132,260},{136,264},{140,268},{144,272},{148,276},{152,2... | collective-permute-start | bytes 1769480 | tf_op jit(solution)/shard_map/ppermute | solution.py:42
  17.9 22.7 %all-to-all-start = ((bf16[4,14,1536]{2,1,0:T(8,128)(2,1)}), bf16[4,14,1536]{2,1,0:T(8,128)(2,1)S(1)}, u32[]{:S(2)}, u32[]{:S(2)}) async-start(bf16[4,14,1536]{2,1,0:T(8,128)(2,1)} %broadcast_in_dim.76), calls=%async_computation | async-start | bytes 393216 | tf_op jit(solution)/shard_map/all_to_all | solution.py:70
  30.8 9.8 %collective-permute-start.5 = (bf16[192,384]{1,0:T(8,128)(2,1)S(1)}, bf16[192,384]{1,0:T(8,128)(2,1)S(1)}, u32[]{:S(2)}, u32[]{:S(2)}) collective-permute-start(bf16[192,384]{1,0:T(8,128)(2,1)S(1)} %broadcast_select_fusion.2), channel_id=1, source_target_pairs={{128,256},{132,260},{136,264},{140,268},{144,272},{148,276},{152,2... | collective-permute-start | bytes 442376 | tf_op jit(solution)/shard_map/ppermute | solution.py:42
  31.4 10.1 %collective-permute-start.4 = (bf16[192,384]{1,0:T(8,128)(2,1)S(1)}, bf16[192,384]{1,0:T(8,128)(2,1)S(1)}, u32[]{:S(2)}, u32[]{:S(2)}) collective-permute-start(bf16[192,384]{1,0:T(8,128)(2,1)S(1)} %broadcast_select_fusion.2), channel_id=1, source_target_pairs={{0,128},{4,132},{8,136},{12,140},{16,144},{20,148},{24,152},{28,15... | collective-permute-start | bytes 442376 | tf_op jit(solution)/shard_map/ppermute | solution.py:42
  41.5 0.7 copy-start.19
  43.9 6.6 %copy-start.22 = (s32[256]{0:T(256)S(1)}, s32[256]{0:T(256)}, u32[]{:S(2)}) copy-start(s32[256]{0:T(256)} %param.19) | copy-start | bytes 3076
  43.9 42.4 %all-to-all-start.1 = ((bf16[16,56,1536]{2,1,0:T(8,128)(2,1)}), bf16[16,56,1536]{2,1,0:T(8,128)(2,1)S(1)}, u32[]{:S(2)}, u32[]{:S(2)}) async-start(bf16[16,56,1536]{2,1,0:T(8,128)(2,1)} %broadcast_in_dim.81), calls=%async_computation.1 | async-start | bytes 5505024 | tf_op jit(solution)/shard_map/all_to_all | solution.py:70
  51.9 19.6 %collective-permute-start.8 = (bf16[384,384]{1,0:T(8,128)(2,1)S(1)}, bf16[384,384]{1,0:T(8,128)(2,1)S(1)}, u32[]{:S(2)}, u32[]{:S(2)}) collective-permute-start(bf16[384,384]{1,0:T(8,128)(2,1)S(1)} %pad_maximum_fusion.p0), channel_id=1, source_target_pairs={{0,3},{1,0},{2,1},{3,2},{4,7},{5,4},{6,5},{7,6},{8,11},{9,8},{10,9... | collective-permute-start | bytes 884744 | tf_op jit(solution)/shard_map/ppermute | solution.py:298
  57.6 25.9 %collective-permute-start.7 = (bf16[384,384]{1,0:T(8,128)(2,1)S(1)}, bf16[384,384]{1,0:T(8,128)(2,1)S(1)}, u32[]{:S(2)}, u32[]{:S(2)}) collective-permute-start(bf16[384,384]{1,0:T(8,128)(2,1)S(1)} %pad_maximum_fusion.p0), channel_id=1, source_target_pairs={{0,2},{1,3},{2,0},{3,1},{4,6},{5,7},{6,4},{7,5},{8,10},{9,11},{10,... | collective-permute-start | bytes 884744 | tf_op jit(solution)/shard_map/ppermute | solution.py:298
  62.2 21.3 %collective-permute-start.6 = (bf16[384,384]{1,0:T(8,128)(2,1)S(1)}, bf16[384,384]{1,0:T(8,128)(2,1)S(1)}, u32[]{:S(2)}, u32[]{:S(2)}) collective-permute-start(bf16[384,384]{1,0:T(8,128)(2,1)S(1)} %pad_maximum_fusion.p0), channel_id=1, source_target_pairs={{0,1},{1,2},{2,3},{3,0},{4,5},{5,6},{6,7},{7,4},{8,9},{9,10},{10,1... | collective-permute-start | bytes 884744 | tf_op jit(solution)/shard_map/ppermute | solution.py:298
  64.9 1.1 copy-start.16
  65.9 1.1 copy-start.17
  67.0 1.1 copy-start.18
  69.5 1.0 copy-start.8
  70.5 1.1 copy-start.10
  71.5 20.5 %copy-start.20 = (f32[384]{0:T(512)S(1)}, f32[384]{0:T(512)}, u32[]{:S(2)}) copy-start(f32[384]{0:T(512)} %param.18) | copy-start | bytes 4612
  71.5 20.5 %copy-start.21 = (f32[384]{0:T(512)S(1)}, f32[384]{0:T(512)}, u32[]{:S(2)}) copy-start(f32[384]{0:T(512)} %param.17) | copy-start | bytes 4612
  84.5 0.9 copy-start.12
  85.4 0.9 copy-start.14
  86.3 11.4 %collective-permute-start.9 = (bf16[896,1536]{1,0:T(8,128)(2,1)S(1)}, bf16[896,1536]{1,0:T(8,128)(2,1)S(1)}, u32[]{:S(2)}, u32[]{:S(2)}) collective-permute-start(bf16[896,1536]{1,0:T(8,128)(2,1)S(1)} %bitcast.19), channel_id=1, source_target_pairs={{0,4},{4,0},{8,12},{12,8},{16,20},{20,16},{24,28},{28,24},{32,36},... | collective-permute-start | bytes 8257544 | tf_op jit(solution)/shard_map/ppermute | solution.py:42
  92.1 1.3 copy-start.11
  93.3 1.1 copy-start.15
  94.5 3.3 %copy-start.9 = (bf16[4,576,224]{2,1,0:T(8,128)(2,1)S(1)}, bf16[4,576,224]{2,1,0:T(8,128)(2,1)}, u32[]{:S(2)}) copy-start(bf16[4,576,224]{2,1,0:T(8,128)(2,1)} %copy-done.8) | copy-start | bytes 3096580
  94.5 3.3 %copy-start.13 = (bf16[4,384,224]{2,1,0:T(8,128)(2,1)S(1)}, bf16[4,384,224]{2,1,0:T(8,128)(2,1)}, u32[]{:S(2)}) copy-start(bf16[4,384,224]{2,1,0:T(8,128)(2,1)} %copy-done.12) | copy-start | bytes 2064388
  97.7 14.5 %copy-start.1 = (bf16[896,1536]{1,0:T(8,128)(2,1)}, bf16[896,1536]{1,0:T(8,128)(2,1)S(1)}, u32[]{:S(2)}) copy-start(bf16[896,1536]{1,0:T(8,128)(2,1)S(1)} %collective-permute-done.9.wt) | copy-start | bytes 8257540
  106.6 1.0 copy-start.5
  107.7 17.1 %collective-permute-start.10 = (bf16[384,768]{1,0:T(8,128)(2,1)}, bf16[384,768]{1,0:T(8,128)(2,1)}, u32[]{:S(2)}, u32[]{:S(2)}) collective-permute-start(bf16[384,768]{1,0:T(8,128)(2,1)} %get-tuple-element.57), channel_id=1, source_target_pairs={{0,128},{4,132},{8,136},{12,140},{16,144},{20,148},{24,152},{28,15... | collective-permute-start | bytes 1769480 | tf_op jit(solution)/shard_map/ppermute | solution.py:42
  110.7 14.0 %collective-permute-start.11 = (bf16[384,768]{1,0:T(8,128)(2,1)}, bf16[384,768]{1,0:T(8,128)(2,1)}, u32[]{:S(2)}, u32[]{:S(2)}) collective-permute-start(bf16[384,768]{1,0:T(8,128)(2,1)} %get-tuple-element.58), channel_id=1, source_target_pairs={{128,256},{132,260},{136,264},{140,268},{144,272},{148,276},{152,2... | collective-permute-start | bytes 1769480 | tf_op jit(solution)/shard_map/ppermute | solution.py:42
  113.7 0.9 copy-start.3
  114.6 39.9 %all-to-all-start.2 = ((bf16[4,192,384]{2,1,0:T(8,128)(2,1)}), bf16[4,192,384]{2,1,0:T(8,128)(2,1)}, u32[]{:S(2)}, u32[]{:S(2)}) async-start(bf16[4,192,384]{2,1,0:T(8,128)(2,1)} %copy-done.3), calls=%async_computation.2 | async-start | bytes 1179648 | tf_op jit(solution)/shard_map/all_to_all | solution.py:386
  124.8 1.3 copy-start.6
  126.1 25.3 %copy-start.2 = (bf16[896,1536]{1,0:T(8,128)(2,1)S(1)}, bf16[896,1536]{1,0:T(8,128)(2,1)}, u32[]{:S(2)}) copy-start(bf16[896,1536]{1,0:T(8,128)(2,1)} %copy-done.1) | copy-start | bytes 8257540
  126.1 25.3 %copy-start.7 = (bf16[768,768]{1,0:T(8,128)(2,1)S(1)}, bf16[768,768]{1,0:T(8,128)(2,1)}, u32[]{:S(2)}) copy-start(bf16[768,768]{1,0:T(8,128)(2,1)} %copy-done.5) | copy-start | bytes 3538948
  127.7 23.6 %collective-permute-start.12 = (bf16[192,768]{1,0:T(8,128)(2,1)S(1)}, bf16[192,768]{1,0:T(8,128)(2,1)S(1)}, u32[]{:S(2)}, u32[]{:S(2)}) collective-permute-start(bf16[192,768]{1,0:T(8,128)(2,1)S(1)} %get-tuple-element.60), channel_id=1, source_target_pairs={{4,8},{8,4},{12,16},{16,12},{20,24},{24,20},{28,32},{32,28},{36,40... | collective-permute-start | bytes 884744 | tf_op jit(solution)/shard_map/ppermute | solution.py:42
  135.2 16.2 %collective-permute-start.13 = (bf16[192,768]{1,0:T(8,128)(2,1)S(1)}, bf16[192,768]{1,0:T(8,128)(2,1)S(1)}, u32[]{:S(2)}, u32[]{:S(2)}) collective-permute-start(bf16[192,768]{1,0:T(8,128)(2,1)S(1)} %get-tuple-element.61), channel_id=1, source_target_pairs={{0,4},{4,0},{8,12},{12,8},{16,20},{20,16},{24,28},{28,24},{32,36},... | collective-permute-start | bytes 884744 | tf_op jit(solution)/shard_map/ppermute | solution.py:42
  153.7 0.8 copy-start.4
  154.5 13.3 %all-to-all-start.3 = ((bf16[4,192,384]{2,1,0:T(8,128)(2,1)}), bf16[4,192,384]{2,1,0:T(8,128)(2,1)S(1)}, u32[]{:S(2)}, u32[]{:S(2)}) async-start(bf16[4,192,384]{2,1,0:T(8,128)(2,1)} %copy-done.4), calls=%async_computation.3 | async-start | bytes 1179648 | tf_op jit(solution)/shard_map/all_to_all | solution.py:399

commit v8 on v7

--- a/solution.py
+++ b/solution.py
@@ -162,6 +162,11 @@
     return acc
 
 
+def text_rows(lines, w):
+    parts = [dot(lines[...], w[j * PART : (j + 1) * PART, :]) for j in range(4)]
+    return jnp.concatenate(parts, axis=0).astype(BF16)
+
+
 def picked_value(rows, pick):
     return [dot(rows[:, j * W : (j + 1) * W], pick[...]).astype(BF16) for j in range(4)]
 
@@ -177,7 +182,7 @@
     acc_g[...] = project(r, w, LAST, at=GIVEN)
     acc_f[...] = project(r, w, KV, at=BEHIND)
     acc_p[...] = project(p, w, KV, part_order(flags))
-    t = dot(lines[...], w[...]).astype(BF16)
+    t = text_rows(lines, w)
     acc_t[...] = project(picked_value(t, pick_o), w, KV)
     for j, rows in enumerate(picked_value(t, pick_t)):
         text[j] = rows
@@ -213,7 +218,7 @@
     behind = acc_f[...] + project(r, wt, KV, at=BEHIND)
     beside = acc_p[...] + project(p, wt, KV, part_order(flags))
     words = acc_t[...] + project(text, wt, KV)
-    t = dot(lines[...], wt[...]).astype(BF16)
+    t = text_rows(lines, wt)
     more = project(picked_value(t, pick_o), wo, KV) + project(picked_value(t, pick_t), wt, KV)
     high = mine[:, :W].astype(BF16)
     keep[KRAW, :W] = high
@@ -322,9 +327,9 @@
         return hit.astype(BF16)
 
     pick_o, pick_t = pick(core), pick(1 - core)
-    t = jnp.arange(HALF_TEXT, dtype=jnp.int32)
+    t = jnp.arange(HALF_TEXT // 4, dtype=jnp.int32)
     line = t // 8 * BLOCK + 48 + t % 8
-    lines = (line[:, None] == jnp.arange(16 * BLOCK, dtype=jnp.int32)[None, :]).astype(BF16)
+    lines = (line[:, None] == jnp.arange(PART, dtype=jnp.int32)[None, :]).astype(BF16)
     t = jnp.arange(TEXT, dtype=jnp.int32)
     token = place_of(t // 32 % 4, t // 2 % 4, t // 8 % 4, (t // 128) ^ core) * 2 + t % 2
     valid = jnp.sum(jnp.where(t[:, None] == token[None, :], text_mask[:, None], 0), axis=0)

time: 172 us -> 171 us (level)
  no operation moved by 1% of the time
where the time goes in v8:
time: 171 us; the launch traced here: 168 us
  starting transfers between devices  78.4 us (46%)
  waiting for transfers between devices  44 us (26%)
  Pallas kernels  19.9 us (12%)
  local copies, waits for them, and re-layouts  18.2 us (11%)
  other arithmetic  5.72 us (3%)
  between operations  2.35 us (1%)
    ppermute x11, starting transfers between devices, seq_move(): return lax.ppermute(value, 'seq', pairs)  41.4 us
    ppermute x11, waiting for transfers between devices, seq_move(): return lax.ppermute(value, 'seq', pairs)  22.1 us
    all_to_all x2, starting transfers between devices, give_all(): return lax.all_to_all(copies, 'seq', 0, 0, axis_index_groups=groups)  16.5 us
    unnamed x46, local copies, waits for them, and re-layouts  14.1 us
    ppermute x3, starting transfers between devices, head_shift(): return lax.ppermute(value, 'heads', [(i, (i + by) % 4) for i in range(4)])  12.8 us
    ppermute x3, waiting for transfers between devices, head_shift(): return lax.ppermute(value, 'heads', [(i, (i + by) % 4) for i in range(4)])  12 us
    pallas_call x1, Pallas kernels, per_device(): call(attend_kernel, (shape((ROWS, W), BF16), shape((4 * ROWS, 2 * W), BF1...  8.82 us
    all_to_all x1, waiting for transfers between devices, per_device(): grads = lax.all_to_all(grad, 'heads', 0, 0)  7.94 us
  transfers between devices with their start and end apart: 18, of which 6 were waited for; matrix products, arithmetic and copies ran while one was open for 4% of the time, Pallas kernels for 7%

profile of v8, /device:TPU:25, one launch (start us, length us, event | category | flops | bytes accessed | tf_op | source)
XLA Modules:
  0.0 168.5 jit_solution(11562560811757640273)
XLA Ops:
  0.6 0.0 copy-start
  0.7 0.9 constant_dynamic-slice_fusion
  1.6 9.0 %collective-permute-start.1 = (bf16[192,384]{1,0:T(8,128)(2,1)S(1)}, bf16[192,384]{1,0:T(8,128)(2,1)S(1)}, u32[]{:S(2)}, u32[]{:S(2)}) collective-permute-start(bf16[192,384]{1,0:T(8,128)(2,1)S(1)} %constant_dynamic-slice_fusion), channel_id=1, source_target_pairs={{4,8},{8,4},{12,16},{16,12},{20,24},{24,20},{28,32},{32,28},{36,40... | collective-permute-start | bytes 442376 | tf_op jit(solution)/shard_map/ppermute | solution.py:42
  10.6 1.9 %collective-permute-start = (bf16[192,384]{1,0:T(8,128)(2,1)S(1)}, bf16[192,384]{1,0:T(8,128)(2,1)S(1)}, u32[]{:S(2)}, u32[]{:S(2)}) collective-permute-start(bf16[192,384]{1,0:T(8,128)(2,1)S(1)} %constant_dynamic-slice_fusion), channel_id=1, source_target_pairs={{0,4},{4,0},{8,12},{12,8},{16,20},{20,16},{24,28},{28,24},{32,36},... | collective-permute-start | bytes 442376 | tf_op jit(solution)/shard_map/ppermute | solution.py:42
  12.6 3.1 %collective-permute-start.2 = (bf16[192,1536]{1,0:T(8,128)(2,1)}, bf16[192,1536]{1,0:T(8,128)(2,1)S(1)}, u32[]{:S(2)}, u32[]{:S(2)}) collective-permute-start(bf16[192,1536]{1,0:T(8,128)(2,1)} %x.3), channel_id=1, source_target_pairs={{0,128},{4,132},{8,136},{12,140},{16,144},{20,148},{24,152},{28,15... | collective-permute-start | bytes 1769480 | tf_op jit(solution)/shard_map/ppermute | solution.py:42
  15.7 0.7 collective-permute-start.3
  16.4 0.8 pad_maximum_fusion.2
  17.2 0.7 broadcast_in_dim.76
  17.9 10.0 %all-to-all-start = ((bf16[4,14,1536]{2,1,0:T(8,128)(2,1)}), bf16[4,14,1536]{2,1,0:T(8,128)(2,1)S(1)}, u32[]{:S(2)}, u32[]{:S(2)}) async-start(bf16[4,14,1536]{2,1,0:T(8,128)(2,1)} %broadcast_in_dim.76), calls=%async_computation | async-start | bytes 393216 | tf_op jit(solution)/shard_map/all_to_all | solution.py:70
  27.9 0.1 constant_dynamic-slice_fusion.1
  28.0 0.5 fusion.29
  29.9 0.9 broadcast_select_fusion.f
  30.8 0.7 collective-permute-start.5
  31.4 7.3 %collective-permute-start.4 = (bf16[192,384]{1,0:T(8,128)(2,1)S(1)}, bf16[192,384]{1,0:T(8,128)(2,1)S(1)}, u32[]{:S(2)}, u32[]{:S(2)}) collective-permute-start(bf16[192,384]{1,0:T(8,128)(2,1)S(1)} %broadcast_select_fusion.2), channel_id=1, source_target_pairs={{0,128},{4,132},{8,136},{12,140},{16,144},{20,148},{24,152},{28,15... | collective-permute-start | bytes 442376 | tf_op jit(solution)/shard_map/ppermute | solution.py:42
  38.7 1.9 %all-to-all-done = bf16[4,14,1536]{2,1,0:T(8,128)(2,1)S(1)} async-done(((bf16[4,14,1536]{2,1,0:T(8,128)(2,1)}), bf16[4,14,1536]{2,1,0:T(8,128)(2,1)S(1)}, u32[]{:S(2)}, u32[]{:S(2)}) %all-to-all-start) | async-done | bytes 172064 | tf_op jit(solution)/shard_map/all_to_all | solution.py:70
  40.6 0.9 collective-permute-done.4
  41.6 0.6 copy-done.19
  42.3 1.7 %broadcast_in_dim.81 = bf16[16,56,1536]{2,1,0:T(8,128)(2,1)} broadcast(bf16[56,1536]{1,0:T(8,128)(2,1)S(1)} %pad_maximum_fusion.1), dimensions={1,2} | broadcast | bytes 2924544 | tf_op jit(solution)/shard_map/broadcast_in_dim | solution.py:69
  43.9 6.5 %all-to-all-start.1 = ((bf16[16,56,1536]{2,1,0:T(8,128)(2,1)}), bf16[16,56,1536]{2,1,0:T(8,128)(2,1)S(1)}, u32[]{:S(2)}, u32[]{:S(2)}) async-start(bf16[16,56,1536]{2,1,0:T(8,128)(2,1)} %broadcast_in_dim.81), calls=%async_computation.1 | async-start | bytes 5505024 | tf_op jit(solution)/shard_map/all_to_all | solution.py:70
  50.5 0.1 select_reduce_fusion
  50.6 0.1 stack.35.flags
  50.8 0.2 fusion.3
  51.0 0.9 broadcast_select_fusion.1
  51.9 5.6 %collective-permute-start.8 = (bf16[384,384]{1,0:T(8,128)(2,1)S(1)}, bf16[384,384]{1,0:T(8,128)(2,1)S(1)}, u32[]{:S(2)}, u32[]{:S(2)}) collective-permute-start(bf16[384,384]{1,0:T(8,128)(2,1)S(1)} %pad_maximum_fusion.p0), channel_id=1, source_target_pairs={{0,3},{1,0},{2,1},{3,2},{4,7},{5,4},{6,5},{7,6},{8,11},{9,8},{10,9... | collective-permute-start | bytes 884744 | tf_op jit(solution)/shard_map/ppermute | solution.py:303
  57.6 4.6 %collective-permute-start.7 = (bf16[384,384]{1,0:T(8,128)(2,1)S(1)}, bf16[384,384]{1,0:T(8,128)(2,1)S(1)}, u32[]{:S(2)}, u32[]{:S(2)}) collective-permute-start(bf16[384,384]{1,0:T(8,128)(2,1)S(1)} %pad_maximum_fusion.p0), channel_id=1, source_target_pairs={{0,2},{1,3},{2,0},{3,1},{4,6},{5,7},{6,4},{7,5},{8,10},{9,11},{10,... | collective-permute-start | bytes 884744 | tf_op jit(solution)/shard_map/ppermute | solution.py:303
  62.2 2.6 %collective-permute-start.6 = (bf16[384,384]{1,0:T(8,128)(2,1)S(1)}, bf16[384,384]{1,0:T(8,128)(2,1)S(1)}, u32[]{:S(2)}, u32[]{:S(2)}) collective-permute-start(bf16[384,384]{1,0:T(8,128)(2,1)S(1)} %pad_maximum_fusion.p0), channel_id=1, source_target_pairs={{0,1},{1,2},{2,3},{3,0},{4,5},{5,6},{6,7},{7,4},{8,9},{9,10},{10,1... | collective-permute-start | bytes 884744 | tf_op jit(solution)/shard_map/ppermute | solution.py:303
  64.8 0.1 fusion.6.lines
  64.8 1.1 copy-done.16
  65.9 1.1 copy-done.17
  67.0 1.1 copy-done.18
  68.0 1.4 shard_map.122
  69.4 1.0 copy-done.8
  70.4 1.1 copy-done.10
  71.5 12.0 %collective-permute-done.7.p2 = bf16[384,384]{1,0:T(8,128)(2,1)S(1)} collective-permute-done((bf16[384,384]{1,0:T(8,128)(2,1)S(1)}, bf16[384,384]{1,0:T(8,128)(2,1)S(1)}, u32[]{:S(2)}, u32[]{:S(2)}) %collective-permute-start.7) | collective-permute-done | bytes 294944 | tf_op jit(solution)/shard_map/ppermute | solution.py:303
  83.5 0.0 collective-permute-done.6.p1
  83.5 1.0 shard_map.123
  84.5 0.9 copy-done.12
  85.4 0.9 copy-done.14
  86.3 0.0 all-to-all-done.1
  86.3 5.7 %collective-permute-start.9 = (bf16[896,1536]{1,0:T(8,128)(2,1)S(1)}, bf16[896,1536]{1,0:T(8,128)(2,1)S(1)}, u32[]{:S(2)}, u32[]{:S(2)}) collective-permute-start(bf16[896,1536]{1,0:T(8,128)(2,1)S(1)} %bitcast.19), channel_id=1, source_target_pairs={{0,4},{4,0},{8,12},{12,8},{16,20},{20,16},{24,28},{28,24},{32,36},... | collective-permute-start | bytes 8257544 | tf_op jit(solution)/shard_map/ppermute | solution.py:42
  92.1 1.3 copy-done.11
  93.3 1.1 copy-done.15
  94.5 3.3 %shard_map.124 = (f32[192,1152]{1,0:T(8,128)S(1)}, f32[192,384]{1,0:T(8,128)S(1)}, f32[192,768]{1,0:T(8,128)S(1)}, f32[384,768]{1,0:T(8,128)S(1)}, f32[128,768]{...) custom-call(s32[6]{0:T(128)S(1)} %stack.35.flags, bf16[4,576,224]{2,1,0:T(8,128)(2,1)S(1)} %copy-done.11, ...), custom_call_target="tpu_custom_call" | custom-call | flops 1000000000 | bytes 8000000 | tf_op jit(solution)/shard_map/pallas_call | solution.py:364
  97.7 0.0 collective-permute-done.9.wt
  97.8 8.8 %shard_map.125 = (bf16[192,384]{1,0:T(8,128)(2,1)S(1)}, bf16[768,768]{1,0:T(8,128)(2,1)S(1)}, bf16[384,768]{1,0:T(8,128)(2,1)}, bf16[384,768]{1,0:T(8,128)(2,1)}) custom-call(s32[6]{0:T(128)S(1)} %stack.35.flags, bf16[4,576,224]{2,1,0:T(8,128)(2,1)S(1)} %copy-done.9, bf16[4,384,224]{2,1,0:T(8,128)(2,1)S(1)} %copy-done.13, ...), custom_call_target="tpu_custom_call" | custom-call | flops 1000000000 | bytes 8000000 | tf_op jit(solution)/shard_map/pallas_call | solution.py:376
  106.6 1.0 copy-done.5
  107.6 2.2 %collective-permute-start.10 = (bf16[384,768]{1,0:T(8,128)(2,1)}, bf16[384,768]{1,0:T(8,128)(2,1)}, u32[]{:S(2)}, u32[]{:S(2)}) collective-permute-start(bf16[384,768]{1,0:T(8,128)(2,1)} %get-tuple-element.57), channel_id=1, source_target_pairs={{0,128},{4,132},{8,136},{12,140},{16,144},{20,148},{24,152},{28,15... | collective-permute-start | bytes 1769480 | tf_op jit(solution)/shard_map/ppermute | solution.py:42
  109.8 1.5 collective-permute-start.11
  111.3 1.5 shard_map.126
  112.8 0.8 copy-done.3
  113.6 4.2 %all-to-all-start.2 = ((bf16[4,192,384]{2,1,0:T(8,128)(2,1)}), bf16[4,192,384]{2,1,0:T(8,128)(2,1)}, u32[]{:S(2)}, u32[]{:S(2)}) async-start(bf16[4,192,384]{2,1,0:T(8,128)(2,1)} %copy-done.3), calls=%async_computation.2 | async-start | bytes 1179648 | tf_op jit(solution)/shard_map/all_to_all | solution.py:391
  117.8 6.9 %collective-permute-done.10.got_even = bf16[384,768]{1,0:T(8,128)(2,1)} collective-permute-done((bf16[384,768]{1,0:T(8,128)(2,1)}, bf16[384,768]{1,0:T(8,128)(2,1)}, u32[]{:S(2)}, u32[]{:S(2)}) %collective-permute-start.10) | collective-permute-done | bytes 589856 | tf_op jit(solution)/shard_map/ppermute | solution.py:42
  124.8 0.0 collective-permute-done.11.got_odd
  124.8 1.3 copy-done.6
  126.0 1.7 shard_map.127
  127.7 7.4 %collective-permute-start.12 = (bf16[192,768]{1,0:T(8,128)(2,1)S(1)}, bf16[192,768]{1,0:T(8,128)(2,1)S(1)}, u32[]{:S(2)}, u32[]{:S(2)}) collective-permute-start(bf16[192,768]{1,0:T(8,128)(2,1)S(1)} %get-tuple-element.60), channel_id=1, source_target_pairs={{4,8},{8,4},{12,16},{16,12},{20,24},{24,20},{28,32},{32,28},{36,40... | collective-permute-start | bytes 884744 | tf_op jit(solution)/shard_map/ppermute | solution.py:42
  135.1 1.9 %collective-permute-start.13 = (bf16[192,768]{1,0:T(8,128)(2,1)S(1)}, bf16[192,768]{1,0:T(8,128)(2,1)S(1)}, u32[]{:S(2)}, u32[]{:S(2)}) collective-permute-start(bf16[192,768]{1,0:T(8,128)(2,1)S(1)} %get-tuple-element.61), channel_id=1, source_target_pairs={{0,4},{4,0},{8,12},{12,8},{16,20},{20,16},{24,28},{28,24},{32,36},... | collective-permute-start | bytes 884744 | tf_op jit(solution)/shard_map/ppermute | solution.py:42
  137.1 14.2 %collective-permute-done.12.from_next = bf16[192,768]{1,0:T(8,128)(2,1)S(1)} collective-permute-done((bf16[192,768]{1,0:T(8,128)(2,1)S(1)}, bf16[192,768]{1,0:T(8,128)(2,1)S(1)}, u32[]{:S(2)}, u32[]{:S(2)}) %collective-permute-start.12) | collective-permute-done | bytes 294944 | tf_op jit(solution)/shard_map/ppermute | solution.py:42
  151.3 2.3 %shard_map.128 = bf16[4,192,384]{2,1,0:T(8,128)(2,1)S(1)} custom-call(f32[192,768]{1,0:T(8,128)S(1)} %get-tuple-element.59.own, bf16[192,768]{1,0:T(8,128)(2,1)S(1)} %collective-permute-done.12.from_next, bf16[192,768]{1,0:T(8,128)(2,1)S(1)} %collective-permute-done.13.from_mate, bf16[768,768]{1,0:T(8,128)(2,1)S(1)} %copy-done.7, ...), custom_call_target="tpu_custom_call" | custom-call | flops 1000000000 | bytes 8000000 | tf_op jit(solution)/shard_map/pallas_call | solution.py:401
  153.6 0.8 copy-done.4
  154.5 3.5 %all-to-all-start.3 = ((bf16[4,192,384]{2,1,0:T(8,128)(2,1)}), bf16[4,192,384]{2,1,0:T(8,128)(2,1)S(1)}, u32[]{:S(2)}, u32[]{:S(2)}) async-start(bf16[4,192,384]{2,1,0:T(8,128)(2,1)} %copy-done.4), calls=%async_computation.3 | async-start | bytes 1179648 | tf_op jit(solution)/shard_map/all_to_all | solution.py:404
  158.0 1.9 %fusion.4 = bf16[192,384]{1,0:T(8,128)(2,1)} fusion(bf16[4,192,384]{2,1,0:T(8,128)(2,1)} %all-to-all-done.2), kind=kLoop, calls=%fused_computation.13 | loop fusion | flops 589824 | bytes 737280 | tf_op jit(solution)/shard_map/add | solution.py:298
  159.8 7.9 %all-to-all-done.3 = bf16[4,192,384]{2,1,0:T(8,128)(2,1)S(1)} async-done(((bf16[4,192,384]{2,1,0:T(8,128)(2,1)}), bf16[4,192,384]{2,1,0:T(8,128)(2,1)S(1)}, u32[]{:S(2)}, u32[]{:S(2)}) %all-to-all-start.3) | async-done | bytes 589856 | tf_op jit(solution)/shard_map/all_to_all | solution.py:404
  167.8 0.7 fusion.5
  (53 shorter events, 0.3 us)
Async XLA Ops:
  0.6 27.3 %copy-start = (s32[128,2]{0,1:T(2,128)S(1)}, s32[128,2]{0,1:T(2,128)}, u32[]{:S(2)}) copy-start(s32[128,2]{0,1:T(2,128)} %param.20) | copy-start | bytes 3076
  1.6 28.2 %collective-permute-start.1 = (bf16[192,384]{1,0:T(8,128)(2,1)S(1)}, bf16[192,384]{1,0:T(8,128)(2,1)S(1)}, u32[]{:S(2)}, u32[]{:S(2)}) collective-permute-start(bf16[192,384]{1,0:T(8,128)(2,1)S(1)} %constant_dynamic-slice_fusion), channel_id=1, source_target_pairs={{4,8},{8,4},{12,16},{16,12},{20,24},{24,20},{28,32},{32,28},{36,40... | collective-permute-start | bytes 442376 | tf_op jit(solution)/shard_map/ppermute | solution.py:42
  10.6 19.2 %collective-permute-start = (bf16[192,384]{1,0:T(8,128)(2,1)S(1)}, bf16[192,384]{1,0:T(8,128)(2,1)S(1)}, u32[]{:S(2)}, u32[]{:S(2)}) collective-permute-start(bf16[192,384]{1,0:T(8,128)(2,1)S(1)} %constant_dynamic-slice_fusion), channel_id=1, source_target_pairs={{0,4},{4,0},{8,12},{12,8},{16,20},{20,16},{24,28},{28,24},{32,36},... | collective-permute-start | bytes 442376 | tf_op jit(solution)/shard_map/ppermute | solution.py:42
  12.6 17.3 %collective-permute-start.2 = (bf16[192,1536]{1,0:T(8,128)(2,1)}, bf16[192,1536]{1,0:T(8,128)(2,1)S(1)}, u32[]{:S(2)}, u32[]{:S(2)}) collective-permute-start(bf16[192,1536]{1,0:T(8,128)(2,1)} %x.3), channel_id=1, source_target_pairs={{0,128},{4,132},{8,136},{12,140},{16,144},{20,148},{24,152},{28,15... | collective-permute-start | bytes 1769480 | tf_op jit(solution)/shard_map/ppermute | solution.py:42
  15.7 14.2 %collective-permute-start.3 = (bf16[192,1536]{1,0:T(8,128)(2,1)}, bf16[192,1536]{1,0:T(8,128)(2,1)S(1)}, u32[]{:S(2)}, u32[]{:S(2)}) collective-permute-start(bf16[192,1536]{1,0:T(8,128)(2,1)} %x.3), channel_id=1, source_target_pairs={{128,256},{132,260},{136,264},{140,268},{144,272},{148,276},{152,2... | collective-permute-start | bytes 1769480 | tf_op jit(solution)/shard_map/ppermute | solution.py:42
  17.9 22.7 %all-to-all-start = ((bf16[4,14,1536]{2,1,0:T(8,128)(2,1)}), bf16[4,14,1536]{2,1,0:T(8,128)(2,1)S(1)}, u32[]{:S(2)}, u32[]{:S(2)}) async-start(bf16[4,14,1536]{2,1,0:T(8,128)(2,1)} %broadcast_in_dim.76), calls=%async_computation | async-start | bytes 393216 | tf_op jit(solution)/shard_map/all_to_all | solution.py:70
  30.8 9.8 %collective-permute-start.5 = (bf16[192,384]{1,0:T(8,128)(2,1)S(1)}, bf16[192,384]{1,0:T(8,128)(2,1)S(1)}, u32[]{:S(2)}, u32[]{:S(2)}) collective-permute-start(bf16[192,384]{1,0:T(8,128)(2,1)S(1)} %broadcast_select_fusion.2), channel_id=1, source_target_pairs={{128,256},{132,260},{136,264},{140,268},{144,272},{148,276},{152,2... | collective-permute-start | bytes 442376 | tf_op jit(solution)/shard_map/ppermute | solution.py:42
  31.4 10.1 %collective-permute-start.4 = (bf16[192,384]{1,0:T(8,128)(2,1)S(1)}, bf16[192,384]{1,0:T(8,128)(2,1)S(1)}, u32[]{:S(2)}, u32[]{:S(2)}) collective-permute-start(bf16[192,384]{1,0:T(8,128)(2,1)S(1)} %broadcast_select_fusion.2), channel_id=1, source_target_pairs={{0,128},{4,132},{8,136},{12,140},{16,144},{20,148},{24,152},{28,15... | collective-permute-start | bytes 442376 | tf_op jit(solution)/shard_map/ppermute | solution.py:42
  41.5 0.7 copy-start.19
  43.9 6.6 %copy-start.22 = (s32[256]{0:T(256)S(1)}, s32[256]{0:T(256)}, u32[]{:S(2)}) copy-start(s32[256]{0:T(256)} %param.19) | copy-start | bytes 3076
  43.9 42.4 %all-to-all-start.1 = ((bf16[16,56,1536]{2,1,0:T(8,128)(2,1)}), bf16[16,56,1536]{2,1,0:T(8,128)(2,1)S(1)}, u32[]{:S(2)}, u32[]{:S(2)}) async-start(bf16[16,56,1536]{2,1,0:T(8,128)(2,1)} %broadcast_in_dim.81), calls=%async_computation.1 | async-start | bytes 5505024 | tf_op jit(solution)/shard_map/all_to_all | solution.py:70
  51.9 19.6 %collective-permute-start.8 = (bf16[384,384]{1,0:T(8,128)(2,1)S(1)}, bf16[384,384]{1,0:T(8,128)(2,1)S(1)}, u32[]{:S(2)}, u32[]{:S(2)}) collective-permute-start(bf16[384,384]{1,0:T(8,128)(2,1)S(1)} %pad_maximum_fusion.p0), channel_id=1, source_target_pairs={{0,3},{1,0},{2,1},{3,2},{4,7},{5,4},{6,5},{7,6},{8,11},{9,8},{10,9... | collective-permute-start | bytes 884744 | tf_op jit(solution)/shard_map/ppermute | solution.py:303
  57.6 25.9 %collective-permute-start.7 = (bf16[384,384]{1,0:T(8,128)(2,1)S(1)}, bf16[384,384]{1,0:T(8,128)(2,1)S(1)}, u32[]{:S(2)}, u32[]{:S(2)}) collective-permute-start(bf16[384,384]{1,0:T(8,128)(2,1)S(1)} %pad_maximum_fusion.p0), channel_id=1, source_target_pairs={{0,2},{1,3},{2,0},{3,1},{4,6},{5,7},{6,4},{7,5},{8,10},{9,11},{10,... | collective-permute-start | bytes 884744 | tf_op jit(solution)/shard_map/ppermute | solution.py:303
  62.2 21.3 %collective-permute-start.6 = (bf16[384,384]{1,0:T(8,128)(2,1)S(1)}, bf16[384,384]{1,0:T(8,128)(2,1)S(1)}, u32[]{:S(2)}, u32[]{:S(2)}) collective-permute-start(bf16[384,384]{1,0:T(8,128)(2,1)S(1)} %pad_maximum_fusion.p0), channel_id=1, source_target_pairs={{0,1},{1,2},{2,3},{3,0},{4,5},{5,6},{6,7},{7,4},{8,9},{9,10},{10,1... | collective-permute-start | bytes 884744 | tf_op jit(solution)/shard_map/ppermute | solution.py:303
  64.8 1.1 copy-start.16
  65.9 1.1 copy-start.17
  67.0 1.1 copy-start.18
  69.4 1.0 copy-start.8
  70.4 1.1 copy-start.10
  71.5 20.5 %copy-start.20 = (f32[384]{0:T(512)S(1)}, f32[384]{0:T(512)}, u32[]{:S(2)}) copy-start(f32[384]{0:T(512)} %param.18) | copy-start | bytes 4612
  71.5 20.5 %copy-start.21 = (f32[384]{0:T(512)S(1)}, f32[384]{0:T(512)}, u32[]{:S(2)}) copy-start(f32[384]{0:T(512)} %param.17) | copy-start | bytes 4612
  84.5 0.9 copy-start.12
  85.4 0.9 copy-start.14
  86.3 11.4 %collective-permute-start.9 = (bf16[896,1536]{1,0:T(8,128)(2,1)S(1)}, bf16[896,1536]{1,0:T(8,128)(2,1)S(1)}, u32[]{:S(2)}, u32[]{:S(2)}) collective-permute-start(bf16[896,1536]{1,0:T(8,128)(2,1)S(1)} %bitcast.19), channel_id=1, source_target_pairs={{0,4},{4,0},{8,12},{12,8},{16,20},{20,16},{24,28},{28,24},{32,36},... | collective-permute-start | bytes 8257544 | tf_op jit(solution)/shard_map/ppermute | solution.py:42
  92.1 1.3 copy-start.11
  93.3 1.1 copy-start.15
  94.5 3.3 %copy-start.9 = (bf16[4,576,224]{2,1,0:T(8,128)(2,1)S(1)}, bf16[4,576,224]{2,1,0:T(8,128)(2,1)}, u32[]{:S(2)}) copy-start(bf16[4,576,224]{2,1,0:T(8,128)(2,1)} %copy-done.8) | copy-start | bytes 3096580
  94.5 3.3 %copy-start.13 = (bf16[4,384,224]{2,1,0:T(8,128)(2,1)S(1)}, bf16[4,384,224]{2,1,0:T(8,128)(2,1)}, u32[]{:S(2)}) copy-start(bf16[4,384,224]{2,1,0:T(8,128)(2,1)} %copy-done.12) | copy-start | bytes 2064388
  97.7 13.6 %copy-start.1 = (bf16[896,1536]{1,0:T(8,128)(2,1)}, bf16[896,1536]{1,0:T(8,128)(2,1)S(1)}, u32[]{:S(2)}) copy-start(bf16[896,1536]{1,0:T(8,128)(2,1)S(1)} %collective-permute-done.9.wt) | copy-start | bytes 8257540
  106.6 1.0 copy-start.5
  107.6 17.1 %collective-permute-start.10 = (bf16[384,768]{1,0:T(8,128)(2,1)}, bf16[384,768]{1,0:T(8,128)(2,1)}, u32[]{:S(2)}, u32[]{:S(2)}) collective-permute-start(bf16[384,768]{1,0:T(8,128)(2,1)} %get-tuple-element.57), channel_id=1, source_target_pairs={{0,128},{4,132},{8,136},{12,140},{16,144},{20,148},{24,152},{28,15... | collective-permute-start | bytes 1769480 | tf_op jit(solution)/shard_map/ppermute | solution.py:42
  109.8 15.0 %collective-permute-start.11 = (bf16[384,768]{1,0:T(8,128)(2,1)}, bf16[384,768]{1,0:T(8,128)(2,1)}, u32[]{:S(2)}, u32[]{:S(2)}) collective-permute-start(bf16[384,768]{1,0:T(8,128)(2,1)} %get-tuple-element.58), channel_id=1, source_target_pairs={{128,256},{132,260},{136,264},{140,268},{144,272},{148,276},{152,2... | collective-permute-start | bytes 1769480 | tf_op jit(solution)/shard_map/ppermute | solution.py:42
  112.8 0.9 copy-start.3
  113.6 40.8 %all-to-all-start.2 = ((bf16[4,192,384]{2,1,0:T(8,128)(2,1)}), bf16[4,192,384]{2,1,0:T(8,128)(2,1)}, u32[]{:S(2)}, u32[]{:S(2)}) async-start(bf16[4,192,384]{2,1,0:T(8,128)(2,1)} %copy-done.3), calls=%async_computation.2 | async-start | bytes 1179648 | tf_op jit(solution)/shard_map/all_to_all | solution.py:391
  124.8 1.3 copy-start.6
  126.0 25.3 %copy-start.2 = (bf16[896,1536]{1,0:T(8,128)(2,1)S(1)}, bf16[896,1536]{1,0:T(8,128)(2,1)}, u32[]{:S(2)}) copy-start(bf16[896,1536]{1,0:T(8,128)(2,1)} %copy-done.1) | copy-start | bytes 8257540
  126.0 25.3 %copy-start.7 = (bf16[768,768]{1,0:T(8,128)(2,1)S(1)}, bf16[768,768]{1,0:T(8,128)(2,1)}, u32[]{:S(2)}) copy-start(bf16[768,768]{1,0:T(8,128)(2,1)} %copy-done.5) | copy-start | bytes 3538948
  127.7 23.6 %collective-permute-start.12 = (bf16[192,768]{1,0:T(8,128)(2,1)S(1)}, bf16[192,768]{1,0:T(8,128)(2,1)S(1)}, u32[]{:S(2)}, u32[]{:S(2)}) collective-permute-start(bf16[192,768]{1,0:T(8,128)(2,1)S(1)} %get-tuple-element.60), channel_id=1, source_target_pairs={{4,8},{8,4},{12,16},{16,12},{20,24},{24,20},{28,32},{32,28},{36,40... | collective-permute-start | bytes 884744 | tf_op jit(solution)/shard_map/ppermute | solution.py:42
  135.1 16.2 %collective-permute-start.13 = (bf16[192,768]{1,0:T(8,128)(2,1)S(1)}, bf16[192,768]{1,0:T(8,128)(2,1)S(1)}, u32[]{:S(2)}, u32[]{:S(2)}) collective-permute-start(bf16[192,768]{1,0:T(8,128)(2,1)S(1)} %get-tuple-element.61), channel_id=1, source_target_pairs={{0,4},{4,0},{8,12},{12,8},{16,20},{20,16},{24,28},{28,24},{32,36},... | collective-permute-start | bytes 884744 | tf_op jit(solution)/shard_map/ppermute | solution.py:42
  153.6 0.8 copy-start.4
  154.5 13.3 %all-to-all-start.3 = ((bf16[4,192,384]{2,1,0:T(8,128)(2,1)}), bf16[4,192,384]{2,1,0:T(8,128)(2,1)S(1)}, u32[]{:S(2)}, u32[]{:S(2)}) async-start(bf16[4,192,384]{2,1,0:T(8,128)(2,1)} %copy-done.4), calls=%async_computation.3 | async-start | bytes 1179648 | tf_op jit(solution)/shard_map/all_to_all | solution.py:404
